TPU v7x, 128 devices: a whole 4x4x4 slice. The times are simulated.
128 devices in a mesh: node: 32 (over z, y, x_hi), local: 4 (over x_lo, core).
Axes of the slice: x: 4 (x_hi: 2, x_lo: 2; x = x_hi * 2 + x_lo), y: 4, z: 4, core: 2. Of those that a mesh axis runs over, the one named last changes fastest.
Arguments:
- tokens: bfloat16 [8192, 7168], P('node', 'local'), may hold values from -6 to 6
- expert_ids: int32 [8192, 8], P('node'), may hold values from 0 to 255, as said below
- keep_flags: int32 [8192, 8], P('node'), may hold values 0 or 1
- affinity: float32 [8192, 8], P('node'), may hold values from 0.05 to 1
- w_gate: bfloat16 [32, 7168, 1024], P('node', 'local'), may hold values from -0.0625 to 0.0625
- w_up: bfloat16 [32, 7168, 1024], P('node', 'local'), may hold values from -0.0625 to 0.0625
- w_down: bfloat16 [32, 1024, 7168], P('node', None, 'local'), may hold values from -0.1875 to 0.1875
- cotangent: bfloat16 [8192, 7168], P('node', 'local'), may hold values from -6 to 6
Outputs:
- mixed: bfloat16 [8192, 7168], P('node', 'local')
- token_grad: bfloat16 [8192, 7168], P('node', 'local')
- affinity_grad: float32 [8192, 8], P('node')
Inputs may be any that keep to these rules, and one draw needn't show every extreme that they name: `expert_ids`: each row names 8 different experts, all within at most 4 of the 8 groups of consecutive experts.
All inputs are finite; a program needn't handle non-finite values. No bound on the sum of `keep_flags` on one device may be relied on, other than what follows from the above.
Results may differ from a plain program's by a relative error of at most 0.04.
Values may be sent and summed in bfloat16 or wider, within the bound.
No kernel may reach another device: no remote copies, remote signals or barrier semaphores. Data moves between devices by JAX's collectives and lax.ppermute only.
A program may use at most 128 MiB of HBM per device.

v0:
```python
import jax
import jax.numpy as jnp
from jax import lax
from jax.sharding import PartitionSpec as P

EXPERTS = 256
TOP = 8
CAP = 10


route_scale = 2.5


def route_plan(expert_ids, keep_flags, flight):
    stride = EXPERTS // flight
    live = (keep_flags == 1) & (expert_ids % stride == 0)
    target = expert_ids // stride
    onehot = ((target[..., None] == jnp.arange(flight, dtype=jnp.int32)) & live[..., None]).astype(
        jnp.int32
    )
    counts = jnp.sum(onehot, axis=1)
    before = jnp.cumsum(counts, axis=0) - counts
    within = jnp.cumsum(onehot, axis=1) - onehot
    position = jnp.sum((before[:, None, :] + within) * onehot, axis=2)
    routed = live & (position < CAP)
    return jnp.where(routed, target * CAP + position, flight * CAP)


def share_total(rows, matrix, flipped):
    return lax.psum_scatter(
        lax.dot_general(
            rows,
            matrix,
            (((1,), (1 if flipped else 0,)), ((), ())),
            preferred_element_type=jnp.float32,
        ).astype(jnp.bfloat16),
        "local",
        scatter_dimension=0,
        tiled=True,
    ).astype(jnp.float32)


def share_spread(part, matrix, flipped):
    return lax.dot_general(
        lax.all_gather(part, "local", axis=0, tiled=True),
        matrix,
        (((1,), (1 if flipped else 0,)), ((), ())),
        preferred_element_type=jnp.float32,
    )


def per_device(tokens, expert_ids, keep_flags, affinity, w_gate, w_up, w_down, cotangent):
    flight = lax.axis_size("node")
    tok_count = tokens.shape[0]
    width_local = tokens.shape[1]
    rows_all = flight * CAP
    destination = route_plan(expert_ids, keep_flags, flight)
    route_rows = jnp.full((rows_all,), tok_count * TOP, jnp.int32)
    route_rows = route_rows.at[destination.reshape(-1)].set(
        jnp.arange(tok_count * TOP, dtype=jnp.int32), mode="drop"
    )
    token_rows = route_rows // TOP
    zero_row = jnp.zeros((1, width_local), jnp.bfloat16)
    total = jnp.sum(affinity, axis=1, keepdims=True)
    weight = route_scale * affinity / total
    weight_pad = jnp.concatenate([weight.reshape(-1), jnp.zeros((1,), jnp.float32)])
    tokens_pad = jnp.concatenate([tokens, zero_row], axis=0)
    cot_pad = jnp.concatenate([cotangent, zero_row], axis=0)
    token_send = jnp.take(tokens_pad, token_rows, axis=0)
    grad_send = (
        jnp.take(weight_pad, route_rows)[:, None] * jnp.take(cot_pad, token_rows, axis=0)
    ).astype(jnp.bfloat16)
    token_recv, grad_recv = (
        lax.all_to_all(
            token_send.reshape(flight, CAP, width_local),
            "node",
            split_axis=0,
            concat_axis=0,
            tiled=True,
        ),
        lax.all_to_all(
            grad_send.reshape(flight, CAP, width_local),
            "node",
            split_axis=0,
            concat_axis=0,
            tiled=True,
        ),
    )
    token_recv = token_recv.reshape(rows_all, width_local)
    grad_recv = grad_recv.reshape(rows_all, width_local)
    paired = jnp.concatenate([w_gate[0], w_up[0]], axis=1)
    down_local = w_down[0]
    hidden_units = down_local.shape[0]
    pre = share_total(token_recv, paired, False)
    gate_pre = pre[:, :hidden_units]
    up_pre = pre[:, hidden_units:]
    sigma = jax.nn.sigmoid(gate_pre)
    hidden = (gate_pre * sigma * up_pre).astype(jnp.bfloat16)
    rows_out = share_spread(hidden, down_local, False).astype(jnp.bfloat16)
    hidden_grad = share_total(grad_recv, down_local, True)
    gate_grad = (hidden_grad * up_pre * sigma * (1.0 + gate_pre * (1.0 - sigma))).astype(
        jnp.bfloat16
    )
    up_grad = (hidden_grad * gate_pre * sigma).astype(jnp.bfloat16)
    pair_grad = jnp.concatenate([gate_grad, up_grad], axis=1)
    rows_back = share_spread(pair_grad, paired, True).astype(jnp.bfloat16)
    out_back, grad_back = (
        lax.all_to_all(
            rows_out.reshape(flight, CAP, width_local),
            "node",
            split_axis=0,
            concat_axis=0,
            tiled=True,
        ),
        lax.all_to_all(
            rows_back.reshape(flight, CAP, width_local),
            "node",
            split_axis=0,
            concat_axis=0,
            tiled=True,
        ),
    )
    out_flat = jnp.concatenate([out_back.reshape(rows_all, width_local), zero_row], axis=0)
    grad_flat = jnp.concatenate([grad_back.reshape(rows_all, width_local), zero_row], axis=0)
    cot_wide = cotangent.astype(jnp.float32)
    mixed = jnp.zeros((tok_count, width_local), jnp.float32)
    grads = jnp.zeros((tok_count, width_local), jnp.float32)
    inner_list = []
    for column in range(TOP):
        picked = jnp.take(out_flat, destination[:, column], axis=0).astype(jnp.float32)
        mixed = mixed + weight[:, column : column + 1] * picked
        grads = grads + jnp.take(grad_flat, destination[:, column], axis=0).astype(jnp.float32)
        inner_list.append(jnp.sum(cot_wide * picked, axis=1))
    inner = lax.psum(jnp.stack(inner_list, axis=1), "local")
    shares = affinity / total
    affinity_grad = route_scale / total * (inner - jnp.sum(shares * inner, axis=1, keepdims=True))
    return (mixed.astype(jnp.bfloat16), grads.astype(jnp.bfloat16), affinity_grad)


def solution(mesh):
    placed = (
        P("node", "local"),
        P("node", None),
        P("node", None),
        P("node", None),
        P("node", "local", None),
        P("node", "local", None),
        P("node", None, "local"),
        P("node", "local"),
    )
    return jax.shard_map(
        per_device,
        mesh=mesh,
        in_specs=placed,
        out_specs=(P("node", "local"), P("node", "local"), P("node", None)),
        check_vma=False,
    )
```

profile of v0, /device:TPU:0, one launch (start us, length us, event | category | flops | bytes accessed | tf_op | source)
XLA Modules:
  0.0 283.9 jit_solution(13102410138106211191)
XLA Ops:
  7.2 0.7 add_select_fusion
  7.9 0.7 fusion.45
  8.7 0.6 reduce-window.6
  9.3 0.2 slice_reduce_fusion
  9.7 0.7 add_select_fusion.2
  10.4 0.1 copy.22
  10.5 0.1 reshape.102
  10.7 8.0 %scatter_custom_fusion = s32[320]{0:T(512)S(1)} fusion(s32[2048]{0:T(1024)S(1)} %bitcast.74, s32[2048]{0:T(1024)S(1)} %iota.7, s32[]{:T(128)} %constant.87.clone.1), kind=kCustom, calls=%fused_computation.151 | custom fusion | bytes 1284 | tf_op jit(solution)/shard_map/scatter | solution.py:59
  18.7 1.2 concatenate.21
  20.0 2.4 gather_fusion.1
  22.3 0.2 broadcast_select_fusion
  22.5 1.5 reshape.103
  24.0 11.0 %all-to-all-start = ((bf16[32,10,1792]{2,1,0:T(8,128)(2,1)}), bf16[32,10,1792]{2,1,0:T(8,128)(2,1)S(1)}, u32[]{:S(2)}, u32[]{:S(2)}) async-start(bf16[32,10,1792]{2,1,0:T(8,128)(2,1)} %reshape.103), calls=%async_computation | async-start | bytes 3670016 | tf_op jit(solution)/shard_map/all_to_all | solution.py:74
  35.1 0.1 copy.23
  35.3 1.2 concatenate.25
  36.6 2.9 %gather_fusion.10 = bf16[320,1792]{1,0:T(8,128)(2,1)} fusion(bf16[257,1792]{1,0:T(8,128)(2,1)S(1)} %concatenate.25, s32[1024]{0:T(1024)S(1)} %pad_clamp_fusion.9), kind=kCustom, calls=%fused_computation.2.clone | custom fusion | bytes 2295040 | tf_op jit(solution)/shard_map/jit(_take)/gather | solution.py:71
  39.5 2.2 gather_fusion
  41.8 21.0 %all-to-all-done = bf16[32,10,1792]{2,1,0:T(8,128)(2,1)S(1)} async-done(((bf16[32,10,1792]{2,1,0:T(8,128)(2,1)}), bf16[32,10,1792]{2,1,0:T(8,128)(2,1)S(1)}, u32[]{:S(2)}, u32[]{:S(2)}) %all-to-all-start) | async-done | bytes 1146912 | tf_op jit(solution)/shard_map/all_to_all | solution.py:74
  62.8 1.2 reshape.104
  64.0 7.1 %fusion.9 = bf16[320,2048]{1,0:T(8,128)(2,1)} fusion(bf16[320,1792]{1,0:T(8,128)(2,1)} %reshape.104, bf16[1792,1024]{1,0:T(8,128)(2,1)} %bitcast.91, bf16[1792,1024]{1,0:T(8,128)(2,1)} %bitcast.93), kind=kOutput, calls=%fused_computation.36 | convolution fusion | flops 2364145664 | bytes 9797632 | tf_op jit(solution)/shard_map/dot_general | solution.py:31
  71.1 1.2 copy-done.1
  72.4 0.3 multiply_convert_fusion
  72.7 1.5 reshape.108
  74.2 4.0 %all-to-all-start.2 = ((bf16[32,10,1792]{2,1,0:T(8,128)(2,1)}), bf16[32,10,1792]{2,1,0:T(8,128)(2,1)S(1)}, u32[]{:S(2)}, u32[]{:S(2)}) async-start(bf16[32,10,1792]{2,1,0:T(8,128)(2,1)} %reshape.108), calls=%async_computation.3 | async-start | bytes 3670016 | tf_op jit(solution)/shard_map/all_to_all | solution.py:81
  78.3 35.4 %all-to-all-done.2 = bf16[32,10,1792]{2,1,0:T(8,128)(2,1)S(1)} async-done(((bf16[32,10,1792]{2,1,0:T(8,128)(2,1)}), bf16[32,10,1792]{2,1,0:T(8,128)(2,1)S(1)}, u32[]{:S(2)}, u32[]{:S(2)}) %all-to-all-start.2) | async-done | bytes 1146912 | tf_op jit(solution)/shard_map/all_to_all | solution.py:81
  113.7 0.4 reshape.109
  114.1 4.3 %fusion.27 = bf16[320,1024]{1,0:T(8,128)(2,1)} fusion(bf16[320,1792]{1,0:T(8,128)(2,1)S(1)} %reshape.109, bf16[1,1024,1792]{2,1,0:T(8,128)(2,1)} %param.18), kind=kOutput, calls=%fused_computation.64 | convolution fusion | flops 1174732800 | bytes 5472256 | tf_op jit(solution)/shard_map/dot_general | solution.py:31
  118.6 1.0 convert_element_type.95
  119.6 12.6 %reduce-scatter.5.cloned.1.call-done = bf16[80,1024]{1,0:T(8,128)(2,1)} async-done(((bf16[320,1024]{1,0:T(8,128)(2,1)}), bf16[80,1024]{1,0:T(8,128)(2,1)}) %reduce-scatter.5.cloned.1.call-update) | async-done | bytes 163856 | tf_op jit(solution)/shard_map/reduce_scatter | solution.py:30
  132.2 1.1 fusion.35
  133.3 0.7 pad_maximum_fusion.7
  134.1 8.1 %all_gather.6 = bf16[320,1024]{1,0:T(8,128)(2,1)S(1)} all-gather(bf16[80,1024]{1,0:T(8,128)(2,1)S(1)} %get-tuple-element.17), channel_id=1, replica_groups=mesh['node'=32,'local'=4] {'local'}, dimensions={0}, use_global_device_ids=true | all-gather | bytes 819200 | tf_op jit(solution)/shard_map/all_gather | solution.py:45
  142.2 3.4 %fusion.6 = bf16[320,1792]{1,0:T(8,128)(2,1)S(1)} fusion(bf16[320,1024]{1,0:T(8,128)(2,1)S(1)} %all_gather.6, bf16[1,1024,1792]{2,1,0:T(8,128)(2,1)} %param.18), kind=kOutput, calls=%fused_computation.35 | convolution fusion | flops 1174978560 | bytes 5472256 | tf_op jit(solution)/shard_map/dot_general | solution.py:44
  145.6 1.5 reshape.105
  147.1 9.4 %all-to-all-start.1 = ((bf16[32,10,1792]{2,1,0:T(8,128)(2,1)}), bf16[32,10,1792]{2,1,0:T(8,128)(2,1)S(1)}, u32[]{:S(2)}, u32[]{:S(2)}) async-start(bf16[32,10,1792]{2,1,0:T(8,128)(2,1)} %reshape.105), calls=%async_computation.2 | async-start | bytes 3670016 | tf_op jit(solution)/shard_map/all_to_all | solution.py:108
  156.6 28.0 %all-to-all-done.1 = bf16[32,10,1792]{2,1,0:T(8,128)(2,1)S(1)} async-done(((bf16[32,10,1792]{2,1,0:T(8,128)(2,1)}), bf16[32,10,1792]{2,1,0:T(8,128)(2,1)S(1)}, u32[]{:S(2)}, u32[]{:S(2)}) %all-to-all-start.1) | async-done | bytes 1146912 | tf_op jit(solution)/shard_map/all_to_all | solution.py:108
  184.6 1.2 reshape.106
  185.9 1.3 concatenate.23
  187.2 1.3 gather_fusion.9
  188.5 1.3 gather_fusion.8
  189.9 2.3 gather_fusion.7
  192.2 2.3 gather_fusion.6
  194.5 2.3 gather_fusion.5
  196.7 2.3 gather_fusion.4
  199.0 2.3 gather_fusion.3
  201.3 2.3 gather_fusion.2
  203.5 4.2 %fusion.26 = (f32[256]{0:T(256)S(1)}, f32[256]{0:T(256)S(1)}, f32[256]{0:T(256)S(1)}, f32[256]{0:T(256)S(1)}, f32[256]{0:T(256)S(1)}, /*index=5*/f32[256]{0:T(256)S(1)}, f32[256]{0:T(256)S(1)}, f32[256]{0:T(256)S(1)}) fusion(bf16[256,1792]{1,0:T(8,128)(2,1)} %param.19, bf16[256,1792]{1,0:T(8,128)(2,1)S(1)} %gather_fusion.9, ...), kind=kLoop, calls=%fused_computation.62 | loop fusion | flops 15136768 | bytes 8267776 | tf_op jit(solution)/shard_map/reduce_sum | solution.py:133
  207.8 5.9 %psum.7 = f32[256,8]{0,1:T(8,128)S(1)} all-reduce(f32[256,8]{0,1:T(8,128)S(1)} %stack.35), channel_id=1, replica_groups=mesh['node'=32,'local'=4] {'local'}, use_global_device_ids=true, to_apply=%region_17.20 | all-reduce | flops 2048 | bytes 16384 | tf_op jit(solution)/shard_map/psum | solution.py:134
  213.7 6.1 %fusion.10 = bf16[320,1792]{1,0:T(8,128)(2,1)S(1)} fusion(bf16[320,2048]{1,0:T(8,128)(2,1)} %all-gather.2.cloned.1.call-done, bf16[1792,1024]{1,0:T(8,128)(2,1)} %bitcast.92, bf16[1792,1024]{1,0:T(8,128)(2,1)} %bitcast.94), kind=kOutput, calls=%fused_computation.37 | convolution fusion | flops 2364063744 | bytes 9797632 | tf_op jit(solution)/shard_map/dot_general | solution.py:44
  219.8 1.4 reshape.110
  221.2 5.7 %all-to-all-start.3 = ((bf16[32,10,1792]{2,1,0:T(8,128)(2,1)}), bf16[32,10,1792]{2,1,0:T(8,128)(2,1)}, u32[]{:S(2)}, u32[]{:S(2)}) async-start(bf16[32,10,1792]{2,1,0:T(8,128)(2,1)} %reshape.110), calls=%async_computation.5 | async-start | bytes 3670016 | tf_op jit(solution)/shard_map/all_to_all | solution.py:115
  227.0 0.6 subtract_multiply_fusion
  227.6 4.5 %fusion.18 = bf16[256,1792]{1,0:T(8,128)(2,1)} fusion(f32[256]{0:T(256)S(1)} %bitcast.76, f32[256]{0:T(256)S(1)} %bitcast.77, f32[256]{0:T(256)S(1)} %bitcast.78, f32[256]{0:T(256)S(1)} %bitcast.79, f32[256]{0:T(256)S(1)} %bitcast.80, f32[256]{0:T(256)S(1)} %bitcast.81, f32[256]{0:T(256)S(1)} %bitcast.82, f32[256]{0:T(256)S(1)} %bitcast.75, ...), kind=kLoop, calls=%fused_computation.54 | loop fusion | flops 14680064 | bytes 8267776 | tf_op jit(solution)/shard_map/convert_element_type | solution.py:137
  232.2 22.2 %all-to-all-done.3 = bf16[32,10,1792]{2,1,0:T(8,128)(2,1)} async-done(((bf16[32,10,1792]{2,1,0:T(8,128)(2,1)}), bf16[32,10,1792]{2,1,0:T(8,128)(2,1)}, u32[]{:S(2)}, u32[]{:S(2)}) %all-to-all-start.3) | async-done | bytes 1146912 | tf_op jit(solution)/shard_map/all_to_all | solution.py:115
  254.4 2.4 reshape.111
  256.9 1.3 gather_fusion.18
  258.2 1.3 gather_fusion.17
  259.6 2.3 gather_fusion.16
  261.8 2.3 gather_fusion.15
  264.1 2.3 gather_fusion.14
  266.4 2.3 gather_fusion.13
  268.7 2.3 gather_fusion.11
  270.9 2.3 gather_fusion.12
  273.2 4.2 %add_convert_fusion = bf16[256,1792]{1,0:T(8,128)(2,1)} fusion(bf16[256,1792]{1,0:T(8,128)(2,1)S(1)} %gather_fusion.18, bf16[256,1792]{1,0:T(8,128)(2,1)S(1)} %gather_fusion.17, bf16[256,1792]{1,0:T(8,128)(2,1)} %gather_fusion.16, bf16[256,1792]{1,0:T(8,128)(2,1)} %gather_fusion.15, bf16[256,1792]{1,0:T(8,128)(2,1)} %gather_fusion.14, ...), kind=kLoop, calls=%fused_computation.63 | loop fusion | flops 11010048 | bytes 8259584 | tf_op jit(solution)/shard_map/convert_element_type | solution.py:137
  (56 shorter events, 1.0 us)
Async XLA Ops:
  24.0 11.1 %copy-start.2 = (f32[256,8]{0,1:T(8,128)S(1)}, f32[256,8]{0,1:T(8,128)}, u32[]{:S(2)}) copy-start(f32[256,8]{0,1:T(8,128)} %param.15) | copy-start | bytes 24580
  24.0 38.8 %all-to-all-start = ((bf16[32,10,1792]{2,1,0:T(8,128)(2,1)}), bf16[32,10,1792]{2,1,0:T(8,128)(2,1)S(1)}, u32[]{:S(2)}, u32[]{:S(2)}) async-start(bf16[32,10,1792]{2,1,0:T(8,128)(2,1)} %reshape.103), calls=%async_computation | async-start | bytes 3670016 | tf_op jit(solution)/shard_map/all_to_all | solution.py:74
  35.0 83.6 %reduce-scatter.3.cloned.1.call-start = ((), (), s32[]{:S(2)}) async-start(), calls=%async_computation.6 | async-start | bytes 1638400 | tf_op jit(solution)/shard_map/reduce_scatter | solution.py:30
  71.1 1.3 copy-start.1
  74.2 39.6 %all-to-all-start.2 = ((bf16[32,10,1792]{2,1,0:T(8,128)(2,1)}), bf16[32,10,1792]{2,1,0:T(8,128)(2,1)S(1)}, u32[]{:S(2)}, u32[]{:S(2)}) async-start(bf16[32,10,1792]{2,1,0:T(8,128)(2,1)} %reshape.108), calls=%async_computation.3 | async-start | bytes 3670016 | tf_op jit(solution)/shard_map/all_to_all | solution.py:81
  78.2 54.1 %reduce-scatter.5.cloned.1.call-start = ((), (), s32[]{:S(2)}) async-start(), calls=%async_computation.7 | async-start | bytes 819200 | tf_op jit(solution)/shard_map/reduce_scatter | solution.py:30
  118.4 95.3 %all-gather.2.cloned.1.call-start = ((), (), s32[]{:S(2)}) async-start(), calls=%async_computation.8 | async-start | bytes 1638400 | tf_op jit(solution)/shard_map/all_gather | solution.py:45
  147.1 37.5 %all-to-all-start.1 = ((bf16[32,10,1792]{2,1,0:T(8,128)(2,1)}), bf16[32,10,1792]{2,1,0:T(8,128)(2,1)S(1)}, u32[]{:S(2)}, u32[]{:S(2)}) async-start(bf16[32,10,1792]{2,1,0:T(8,128)(2,1)} %reshape.105), calls=%async_computation.2 | async-start | bytes 3670016 | tf_op jit(solution)/shard_map/all_to_all | solution.py:108
  221.2 6.4 %copy-start = (bf16[256,1792]{1,0:T(8,128)(2,1)S(1)}, bf16[256,1792]{1,0:T(8,128)(2,1)}, u32[]{:S(2)}) copy-start(bf16[256,1792]{1,0:T(8,128)(2,1)} %gather_fusion.7) | copy-start | bytes 2752516
  221.2 33.1 %all-to-all-start.3 = ((bf16[32,10,1792]{2,1,0:T(8,128)(2,1)}), bf16[32,10,1792]{2,1,0:T(8,128)(2,1)}, u32[]{:S(2)}, u32[]{:S(2)}) async-start(bf16[32,10,1792]{2,1,0:T(8,128)(2,1)} %reshape.110), calls=%async_computation.5 | async-start | bytes 3670016 | tf_op jit(solution)/shard_map/all_to_all | solution.py:115
Sparse Core Ops, SparseCore 0:
  71.2 25.6 reduce-scatter.2
  118.5 13.6 reduce-scatter.4
  134.2 23.5 all-gather.1
where the time goes:
time: 285 us; the launch traced here: 284 us
  waiting for transfers between devices  119 us (42%)
  local copies, waits for them, and re-layouts  65.1 us (23%)
  starting transfers between devices  30.3 us (11%)
  matrix products  20.9 us (7%)
  other arithmetic  20.2 us (7%)
  between operations  14.2 us (5%)
  blocking collectives  14 us (5%)
    all_to_all x1, waiting for transfers between devices, per_device(): lax.all_to_all(grad_send.reshape(flight, CAP, width_local), 'node', split...  35.4 us
    all_to_all x1, waiting for transfers between devices, per_device(): lax.all_to_all(rows_out.reshape(flight, CAP, width_local), 'node', split_...  28 us
    all_to_all x1, waiting for transfers between devices, per_device(): lax.all_to_all(rows_back.reshape(flight, CAP, width_local), 'node', split...  22.2 us
    all_to_all x1, waiting for transfers between devices, per_device(): lax.all_to_all(token_send.reshape(flight, CAP, width_local), 'node', spli...  21 us
    gather x8, local copies, waits for them, and re-layouts, per_device(): jnp.take(grad_flat, destination[:, column], axis=0).astype(jnp.float32)  16.3 us
    gather x8, local copies, waits for them, and re-layouts, per_device(): jnp.take(out_flat, destination[:, column], axis=0).astype(jnp.float32)  16.3 us
    reduce_scatter x2, waiting for transfers between devices, share_total(): lax.psum_scatter(lax.dot_general(rows, matrix, (((1,), (1 if flipped else...  12.6 us
    dot_general x2, matrix products, share_total(): lax.dot_general(rows, matrix, (((1,), (1 if flipped else 0,)), ((), ())),...  11.4 us
  transfers between devices with their start and end apart: 7, of which 5 were waited for; matrix products, arithmetic and copies ran while one was open for 17% of the time, Pallas kernels for 0%

commit v1 on v0

v1 whole, which is shorter than its diff:
```python
import jax
import jax.numpy as jnp
from jax import lax
from jax.experimental import pallas as pl
from jax.experimental.pallas import tpu as pltpu
from jax.sharding import PartitionSpec as P

TOP = 8
CAP = 10
FLIGHT = 32
STRIDE = 8
TOK = 256
WIDTH = 1792
FF = 1024
MAIN = 8
TAIL = 512
PACKED = WIDTH + TAIL
ROWS = FLIGHT * MAIN
HALF_MAIN = ROWS // 2
HALF = FLIGHT * CAP // 2
TILE = 256
STEPS = WIDTH // TILE
ROUTE_SCALE = 2.5
F32 = jnp.float32
BF16 = jnp.bfloat16
NN = (((1,), (0,)), ((), ()))
NT = (((1,), (1,)), ((), ()))
TN = (((0,), (0,)), ((), ()))


def dot(a, b, dims=NN, exact=False):
    precision = lax.Precision.HIGHEST if exact else None
    return lax.dot_general(a, b, dims, precision=precision, preferred_element_type=F32)


def iota(shape, dim):
    return lax.broadcasted_iota(jnp.int32, shape, dim)


def expert_marks(ids_ref, keep_ref, values_ref=None):
    expert = iota((FLIGHT, TOK), 0) * STRIDE
    marks = jnp.zeros((FLIGHT, TOK), F32)
    values = jnp.zeros((FLIGHT, TOK), F32)
    for k in range(TOP):
        hit = (ids_ref[k : k + 1, :] == expert) & (keep_ref[k : k + 1, :] == 1)
        marks = jnp.where(hit, 1.0, marks)
        if values_ref is not None:
            values = jnp.where(hit, values_ref[k : k + 1, :], values)
    return marks, values


def spread_matrix():
    return (iota((ROWS, FLIGHT), 0) // MAIN == iota((ROWS, FLIGHT), 1)).astype(F32)


def slots_spread(marks):
    earlier = (iota((TOK, TOK), 0) < iota((TOK, TOK), 1)).astype(BF16)
    position = dot(marks.astype(BF16), earlier)
    slot = jnp.where((marks > 0.5) & (position < CAP), position, 31.0)
    return dot(spread_matrix().astype(BF16), slot.astype(BF16))


def picks(marks):
    spread = slots_spread(marks)
    sub = (iota((ROWS, TOK), 0) % MAIN).astype(F32)
    tail_sub = (iota((ROWS, TOK), 0) % 2 + MAIN).astype(F32)
    return spread == sub, spread == tail_sub


def gather_into(out_ref, source_ref, main, tail, main_scale, tail_scale):
    piece_of_row = iota((ROWS, TILE), 0) % MAIN // 2
    zero = jnp.zeros((ROWS, TILE), BF16)
    tails = [zero, zero]
    for n in range(STEPS):
        block = source_ref[:, n * TILE : (n + 1) * TILE]
        first = dot(main, block)
        second = dot(tail, block)
        if main_scale is not None:
            first = first * main_scale
            second = second * tail_scale
        out_ref[:, n * TILE : (n + 1) * TILE] = first.astype(BF16)
        tails[n % 2] = jnp.where(piece_of_row == n // 2, second.astype(BF16), tails[n % 2])
    out_ref[:, WIDTH : WIDTH + TILE] = tails[0]
    out_ref[:, WIDTH + TILE :] = tails[1]


def as_bf16(mask):
    return jnp.where(mask, 1.0, 0.0).astype(BF16)


def send_tokens_kernel(ids_ref, keep_ref, source_ref, out_ref):
    marks, unused = expert_marks(ids_ref, keep_ref)
    main, tail = picks(marks)
    gather_into(out_ref, source_ref, as_bf16(main), as_bf16(tail), None, None)


def weights_of(affinity_ref):
    affinity = affinity_ref[...]
    return ROUTE_SCALE * affinity / jnp.sum(affinity, axis=0, keepdims=True)


def send_grads_kernel(ids_ref, keep_ref, affinity_ref, source_ref, out_ref, weight_ref):
    weight_ref[...] = weights_of(affinity_ref)
    marks, weights = expert_marks(ids_ref, keep_ref, weight_ref)
    main, tail = picks(marks)
    wide = dot(spread_matrix(), weights, exact=True)
    main_scale = jnp.sum(jnp.where(main, wide, 0.0), axis=1, keepdims=True)
    tail_scale = jnp.sum(jnp.where(tail, wide, 0.0), axis=1, keepdims=True)
    gather_into(out_ref, source_ref, as_bf16(main), as_bf16(tail), main_scale, tail_scale)


def vmem(n):
    return [pl.BlockSpec(memory_space=pltpu.VMEM)] * n


def cost(flops, moved):
    return pl.CostEstimate(flops=int(flops), bytes_accessed=int(moved), transcendentals=0)


GATHER_COST = cost(4 * ROWS * TOK * WIDTH, 2 * TOK * WIDTH * 3)


def send_tokens(ids, keep, source):
    return pl.pallas_call(
        send_tokens_kernel,
        out_shape=jax.ShapeDtypeStruct((ROWS, PACKED), BF16),
        in_specs=vmem(3),
        out_specs=pl.BlockSpec(memory_space=pltpu.VMEM),
        cost_estimate=GATHER_COST,
        name="send_tokens",
    )(ids, keep, source)


def send_grads(ids, keep, affinity, source):
    return pl.pallas_call(
        send_grads_kernel,
        out_shape=jax.ShapeDtypeStruct((ROWS, PACKED), BF16),
        in_specs=vmem(4),
        out_specs=pl.BlockSpec(memory_space=pltpu.VMEM),
        scratch_shapes=[pltpu.VMEM((TOP, TOK), F32)],
        cost_estimate=GATHER_COST,
        name="send_grads",
    )(ids, keep, affinity, source)


def unpack_half(packed_ref, half, out_ref, base):
    rows = pl.ds(pl.multiple_of(half * HALF_MAIN, HALF_MAIN), HALF_MAIN)
    out_ref[base : base + HALF_MAIN, :] = packed_ref[rows, :WIDTH]
    tail = packed_ref[rows, WIDTH:]
    shape = (HALF - HALF_MAIN, HALF_MAIN)
    row, col = iota(shape, 0), iota(shape, 1)
    for g in range(4):
        same = (row // 2 == col // MAIN) & (col % MAIN == 2 * g + row % 2)
        piece = dot(as_bf16(same), tail).astype(BF16)
        width = min(TAIL, WIDTH - g * TAIL)
        out_ref[base + HALF_MAIN : base + HALF, g * TAIL : g * TAIL + width] = piece[:, :width]


def partial_kernel(flipped, count, core_ref, packed_ref, *rest):
    weight_refs, (send_ref, keep_ref, rows_ref) = rest[:count], rest[count:]

    @pl.when(pl.program_id(0) == 0)
    def _():
        core = core_ref[0]
        unpack_half(packed_ref, 1 - core, rows_ref, 0)
        unpack_half(packed_ref, core, rows_ref, HALF)

    for at, weight_ref in enumerate(weight_refs):
        product = dot(rows_ref[...], weight_ref[...], NT if flipped else NN)
        cols = slice(at * TILE, (at + 1) * TILE)
        send_ref[:, cols] = product[:HALF].astype(BF16)
        keep_ref[:, cols] = product[HALF:]


def partial_sums(name, core, packed, weights, flipped):
    count = len(weights)
    wide = count * TILE
    if flipped:
        weight_spec = pl.BlockSpec((TILE, WIDTH), lambda n: (n, 0))
    else:
        weight_spec = pl.BlockSpec((WIDTH, TILE), lambda n: (0, n))
    out_spec = pl.BlockSpec((HALF, wide), lambda n: (0, n))
    return pl.pallas_call(
        lambda *refs: partial_kernel(flipped, count, *refs),
        grid=(FF // TILE,),
        out_shape=(
            jax.ShapeDtypeStruct((HALF, count * FF), BF16),
            jax.ShapeDtypeStruct((HALF, count * FF), F32),
        ),
        in_specs=[
            pl.BlockSpec(memory_space=pltpu.SMEM),
            pl.BlockSpec((ROWS, PACKED), lambda n: (0, 0)),
        ]
        + [weight_spec] * count,
        out_specs=(out_spec, out_spec),
        scratch_shapes=[pltpu.VMEM((2 * HALF, WIDTH), BF16)],
        cost_estimate=cost(4 * HALF * WIDTH * count * FF, 2 * count * FF * WIDTH),
        name=name,
    )(core, packed, *weights)


def spread_kernel(flipped, count, core_ref, own_ref, peer_ref, *rest):
    weight_refs, (out_ref,) = rest[:count], rest[count:]
    n = pl.program_id(0)
    core = core_ref[0]

    @pl.when(n == 0)
    def _():
        out_ref[:, WIDTH:] = jnp.zeros((ROWS, TAIL), BF16)

    cols = pl.ds(pl.multiple_of(n * TILE, TILE), TILE)
    tail_cols = pl.ds(pl.multiple_of(WIDTH + n % 2 * TILE, TILE), TILE)
    shape = (HALF_MAIN, HALF - HALF_MAIN)
    row, col = iota(shape, 0), iota(shape, 1)
    place = as_bf16((row // MAIN == col // 2) & (row % MAIN == n // 2 * 2 + col % 2))
    for half_ref, half in ((own_ref, core), (peer_ref, 1 - core)):
        product = jnp.zeros((HALF, TILE), F32)
        for at, weight_ref in enumerate(weight_refs):
            if flipped:
                product += dot(half_ref[:, at * FF : (at + 1) * FF], weight_ref[...], NT)
            else:
                product += dot(half_ref[:, at * FF : (at + 1) * FF], weight_ref[...])
        product = product.astype(BF16)
        rows = pl.ds(pl.multiple_of(half * HALF_MAIN, HALF_MAIN), HALF_MAIN)
        out_ref[rows, cols] = product[:HALF_MAIN]
        out_ref[rows, tail_cols] += dot(place, product[HALF_MAIN:]).astype(BF16)


def spread_rows(name, core, own, peer, weights, flipped):
    count = len(weights)
    if flipped:
        weight_spec = pl.BlockSpec((TILE, FF), lambda n: (n, 0))
    else:
        weight_spec = pl.BlockSpec((FF, TILE), lambda n: (0, n))
    half_spec = pl.BlockSpec((HALF, count * FF), lambda n: (0, 0))
    return pl.pallas_call(
        lambda *refs: spread_kernel(flipped, count, *refs),
        grid=(STEPS,),
        out_shape=jax.ShapeDtypeStruct((ROWS, PACKED), BF16),
        in_specs=[pl.BlockSpec(memory_space=pltpu.SMEM), half_spec, half_spec]
        + [weight_spec] * count,
        out_specs=pl.BlockSpec((ROWS, PACKED), lambda n: (0, 0)),
        cost_estimate=cost(4 * HALF * WIDTH * count * FF, 2 * count * FF * WIDTH),
        name=name,
    )(core, own, peer, *weights)


def add_kernel(keep_ref, recv_ref, total_ref, send_ref):
    total = keep_ref[...] + recv_ref[...].astype(F32)
    total_ref[...] = total
    send_ref[...] = total.astype(BF16)


def add_halves(name, keep, recv):
    return pl.pallas_call(
        add_kernel,
        out_shape=(
            jax.ShapeDtypeStruct(keep.shape, F32),
            jax.ShapeDtypeStruct(keep.shape, BF16),
        ),
        in_specs=vmem(2),
        out_specs=tuple(vmem(2)),
        cost_estimate=cost(keep.size, keep.size * 12),
        name=name,
    )(keep, recv)


def hidden_kernel(total_ref, recv_ref, hidden_ref):
    pre = total_ref[...] + recv_ref[...].astype(F32)
    gate, up = pre[:, :TILE], pre[:, TILE:]
    hidden_ref[...] = (gate * jax.nn.sigmoid(gate) * up).astype(BF16)


def hidden_of(total, recv):
    wide = pl.BlockSpec((HALF, 2 * TILE), lambda n: (0, n))
    return pl.pallas_call(
        hidden_kernel,
        grid=(FF // TILE,),
        out_shape=jax.ShapeDtypeStruct((HALF, FF), BF16),
        in_specs=[wide, wide],
        out_specs=pl.BlockSpec((HALF, TILE), lambda n: (0, n)),
        cost_estimate=cost(HALF * FF * 20, HALF * FF * 14),
        name="hidden",
    )(total, recv)


def pair_grad_kernel(total_ref, recv_ref, grad_total_ref, grad_recv_ref, gate_ref, up_ref):
    pre = total_ref[...] + recv_ref[...].astype(F32)
    gate, up = pre[:, :TILE], pre[:, TILE:]
    grad = grad_total_ref[...] + grad_recv_ref[...].astype(F32)
    sigma = jax.nn.sigmoid(gate)
    gate_ref[...] = (grad * up * sigma * (1.0 + gate * (1.0 - sigma))).astype(BF16)
    up_ref[...] = (grad * gate * sigma).astype(BF16)


def pair_grad_whole_kernel(total_ref, recv_ref, grad_total_ref, grad_recv_ref, out_ref):
    for n in range(FF // TILE):
        wide = slice(2 * n * TILE, 2 * (n + 1) * TILE)
        cols = slice(n * TILE, (n + 1) * TILE)
        pair_grad_kernel(
            total_ref.at[:, wide],
            recv_ref.at[:, wide],
            grad_total_ref.at[:, cols],
            grad_recv_ref.at[:, cols],
            out_ref.at[:, cols],
            out_ref.at[:, slice(FF + n * TILE, FF + (n + 1) * TILE)],
        )


def pair_grads(total, recv, grad_total, grad_recv):
    return pl.pallas_call(
        pair_grad_whole_kernel,
        out_shape=jax.ShapeDtypeStruct((HALF, 2 * FF), BF16),
        in_specs=vmem(4),
        out_specs=pl.BlockSpec(memory_space=pltpu.VMEM),
        cost_estimate=cost(HALF * FF * 30, HALF * FF * 24),
        name="pair_grads",
    )(total, recv, grad_total, grad_recv)


def mixed_kernel(ids_ref, keep_ref, affinity_ref, cot_ref, packed_ref, mixed_ref, inner_ref, weight_ref):
    weight_ref[...] = weights_of(affinity_ref)
    marks, weights = expert_marks(ids_ref, keep_ref, weight_ref)
    main, tail = picks(marks)
    wide = dot(spread_matrix(), weights, exact=True)
    piece_of_row = iota((ROWS, TOK), 0) % MAIN // 2

    def split(values):
        high = values.astype(BF16)
        return high, (values - high.astype(F32)).astype(BF16)

    main_high, main_low = split(jnp.where(main, wide, 0.0))
    found = jnp.zeros((ROWS, TOK), F32)
    tails = []
    for g in range(4):
        tails.append(split(jnp.where(tail & (piece_of_row == g), wide, 0.0)))
    main_inner = jnp.zeros((ROWS, TOK), F32)
    for n in range(STEPS):
        cols = slice(n * TILE, (n + 1) * TILE)
        g = n // 2
        cot = cot_ref[:, cols]
        rows = packed_ref[:, cols]
        tail_rows = packed_ref[:, WIDTH + n % 2 * TILE : WIDTH + (n % 2 + 1) * TILE]
        total = dot(main_high, rows, TN) + dot(main_low, rows, TN)
        total += dot(tails[g][0], tail_rows, TN) + dot(tails[g][1], tail_rows, TN)
        mixed_ref[:, cols] = total.astype(BF16)
        main_inner += dot(rows, cot, NT)
        found += jnp.where(tail & (piece_of_row == g), dot(tail_rows, cot, NT), 0.0)
    found += jnp.where(main, main_inner, 0.0)
    by_expert = dot(spread_matrix(), found, TN, exact=True)
    expert = iota((FLIGHT, TOK), 0) * STRIDE
    for k in range(TOP):
        hit = (ids_ref[k : k + 1, :] == expert) & (keep_ref[k : k + 1, :] == 1)
        inner_ref[k : k + 1, :] = jnp.sum(jnp.where(hit, by_expert, 0.0), axis=0, keepdims=True)


def mix(ids, keep, affinity, cot, packed):
    return pl.pallas_call(
        mixed_kernel,
        out_shape=(
            jax.ShapeDtypeStruct((TOK, WIDTH), BF16),
            jax.ShapeDtypeStruct((TOP, TOK), F32),
        ),
        in_specs=vmem(5),
        out_specs=tuple(vmem(2)),
        scratch_shapes=[pltpu.VMEM((TOP, TOK), F32)],
        cost_estimate=cost(12 * ROWS * TOK * WIDTH, 2 * TOK * WIDTH * 3),
        name="mix",
    )(ids, keep, affinity, cot, packed)


def token_grad_kernel(ids_ref, keep_ref, packed_ref, out_ref):
    marks, unused = expert_marks(ids_ref, keep_ref)
    main, tail = picks(marks)
    piece_of_row = iota((ROWS, TOK), 0) % MAIN // 2
    main_place = as_bf16(main)
    for n in range(STEPS):
        cols = slice(n * TILE, (n + 1) * TILE)
        tail_rows = packed_ref[:, WIDTH + n % 2 * TILE : WIDTH + (n % 2 + 1) * TILE]
        tail_place = as_bf16(tail & (piece_of_row == n // 2))
        total = dot(main_place, packed_ref[:, cols], TN) + dot(tail_place, tail_rows, TN)
        out_ref[:, cols] = total.astype(BF16)


def token_grads(ids, keep, packed):
    return pl.pallas_call(
        token_grad_kernel,
        out_shape=jax.ShapeDtypeStruct((TOK, WIDTH), BF16),
        in_specs=vmem(3),
        out_specs=pl.BlockSpec(memory_space=pltpu.VMEM),
        cost_estimate=cost(4 * ROWS * TOK * WIDTH, 2 * TOK * WIDTH * 3),
        name="token_grads",
    )(ids, keep, packed)


def exchange(packed):
    return lax.all_to_all(packed, "node", split_axis=0, concat_axis=0, tiled=True)


def swap(values, distance):
    return lax.ppermute(values, "local", [(i, i ^ distance) for i in range(4)])


def per_device(tokens, expert_ids, keep_flags, affinity, w_gate, w_up, w_down, cotangent):
    core = (lax.axis_index("local") % 2).astype(jnp.int32).reshape(1)
    ids, keep, affinity_t = expert_ids.T, keep_flags.T, affinity.T
    w_gate, w_up, w_down = w_gate[0], w_up[0], w_down[0]

    token_rows = exchange(send_tokens(ids, keep, tokens))
    grad_rows = exchange(send_grads(ids, keep, affinity_t, cotangent))

    send, own = partial_sums("pre", core, token_rows, (w_gate, w_up), False)
    total, send = add_halves("pre_add", own, swap(send, 1))
    recv = swap(send, 2)
    hidden = hidden_of(total, recv)
    out = spread_rows("rows_out", core, hidden, swap(hidden, 1), (w_down,), False)
    out = exchange(out)

    send, own = partial_sums("hidden_grad", core, grad_rows, (w_down,), True)
    grad_total, send = add_halves("grad_add", own, swap(send, 1))
    grad_recv = swap(send, 2)
    pair = pair_grads(total, recv, grad_total, grad_recv)
    back = spread_rows("rows_back", core, pair, swap(pair, 1), (w_gate, w_up), True)
    back = exchange(back)

    mixed, inner = mix(ids, keep, affinity_t, cotangent, out)
    inner = inner + swap(inner, 1)
    inner = inner + swap(inner, 2)
    scale = jnp.sum(affinity_t, axis=0, keepdims=True)
    shares = affinity_t / scale
    affinity_grad = ROUTE_SCALE / scale * (inner - jnp.sum(shares * inner, axis=0, keepdims=True))
    token_grad = token_grads(ids, keep, back)
    return mixed, token_grad, affinity_grad.T


def solution(mesh):
    placed = (
        P("node", "local"),
        P("node", None),
        P("node", None),
        P("node", None),
        P("node", "local", None),
        P("node", "local", None),
        P("node", None, "local"),
        P("node", "local"),
    )
    return jax.shard_map(
        per_device,
        mesh=mesh,
        in_specs=placed,
        out_specs=(P("node", "local"), P("node", "local"), P("node", None)),
        check_vma=False,
    )
```

time: 285 us -> 165 us (0.58)
  waiting for transfers between devices: 119 us -> 55.2 us
  Pallas kernels: 0 us -> 61.6 us
  local copies, waits for them, and re-layouts: 65.1 us -> 8.83 us
  matrix products: 20.9 us -> 0 us
  other arithmetic: 20.2 us -> 1.35 us
  blocking collectives: 14 us -> 0 us
  between operations: 14.2 us -> 0.75 us
  starting transfers between devices: 30.3 us -> 36.6 us
    pallas_call x0 -> x12, Pallas kernels: none -> 61.6 us  [the longest x2 22.4 us: spread_rows(): pl.pallas_call(lambda *refs: spread_kernel(flipped, count, *refs), grid=(...]
    all_to_all x4, waiting for transfers between devices: 107 us -> 45.1 us  [exchange(): lax.all_to_all(packed, 'node', split_axis=0, concat_axis=0, tiled=True)]
    gather x19 -> x0, local copies, waits for them, and re-layouts: 40.1 us -> none  [the longest x8 16.3 us: per_device(): jnp.take(grad_flat, destination[:, column], axis=0).astype(jnp.float32)]
    dot_general x4 -> x0, matrix products: 20.9 us -> none  [the longest x2 11.4 us: share_total(): lax.dot_general(rows, matrix, (((1,), (1 if flipped else 0,)), ((), ())),...]
    reduce_scatter x2 -> x0, waiting for transfers between devices: 12.6 us -> none  [share_total(): lax.psum_scatter(lax.dot_general(rows, matrix, (((1,), (1 if flipped else...]
    reshape x11 -> x0, local copies, waits for them, and re-layouts: 11.3 us -> none  [the longest x1 2.41 us: per_device(): grad_back.reshape(rows_all, width_local)]
    convert_element_type x5 -> x0, other arithmetic: 11.2 us -> none  [the longest x1 4.54 us: per_device(): mixed.astype(jnp.bfloat16)]
    ppermute x0 -> x8, waiting for transfers between devices: none -> 10.1 us  [swap(): return lax.ppermute(values, 'local', [(i, i ^ distance) for i in range(4)])]
  transfers between devices with their start and end apart: 7 -> 12, of which waited for: 5 -> 7; matrix products, arithmetic and copies ran while one was open for 17% -> 1% of each run, Pallas kernels for 0% -> 29%
where the time goes in v1:
time: 165 us; the launch traced here: 164 us
  Pallas kernels  61.6 us (37%)
  waiting for transfers between devices  55.2 us (33%)
  starting transfers between devices  36.6 us (22%)
  local copies, waits for them, and re-layouts  8.83 us (5%)
    all_to_all x4, waiting for transfers between devices, exchange(): lax.all_to_all(packed, 'node', split_axis=0, concat_axis=0, tiled=True)  45.1 us
    all_to_all x4, starting transfers between devices, exchange(): lax.all_to_all(packed, 'node', split_axis=0, concat_axis=0, tiled=True)  32.8 us
    pallas_call x2, Pallas kernels, spread_rows(): pl.pallas_call(lambda *refs: spread_kernel(flipped, count, *refs), grid=(...  22.4 us
    pallas_call x2, Pallas kernels, partial_sums(): pl.pallas_call(lambda *refs: partial_kernel(flipped, count, *refs), grid=...  12.8 us
    ppermute x8, waiting for transfers between devices, swap(): return lax.ppermute(values, 'local', [(i, i ^ distance) for i in range(4)])  10.1 us
    unnamed x22, local copies, waits for them, and re-layouts  8.83 us
    pallas_call x2, Pallas kernels, add_halves(): pl.pallas_call(add_kernel, out_shape=(jax.ShapeDtypeStruct(keep.shape, F3...  5.09 us
    pallas_call x1, Pallas kernels, mix(): pl.pallas_call(mixed_kernel, out_shape=(jax.ShapeDtypeStruct((TOK, WIDTH)...  4.97 us
  transfers between devices with their start and end apart: 12, of which 7 were waited for; matrix products, arithmetic and copies ran while one was open for 1% of the time, Pallas kernels for 29%

profile of v1, /device:TPU:0, one launch (start us, length us, event | category | flops | bytes accessed | tf_op | source)
XLA Modules:
  0.0 164.3 jit_solution(7266339627982774228)
XLA Ops:
  0.6 3.2 %send_tokens.1 = bf16[256,2304]{1,0:T(8,128)(2,1)} custom-call(s32[8,256]{1,0:T(8,128)} %bitcast.32, s32[8,256]{1,0:T(8,128)} %bitcast.36, bf16[256,1792]{1,0:T(8,128)(2,1)} %source_ref.2), custom_call_target="tpu_custom_call" | custom-call | flops 469762048 | bytes 2752512 | tf_op jit(solution)/shard_map/send_tokens/pallas_call | solution.py:124
  3.8 10.9 %all-to-all-start = ((bf16[32,8,2304]{2,1,0:T(8,128)(2,1)}), bf16[32,8,2304]{2,1,0:T(8,128)(2,1)S(1)}, u32[]{:S(2)}, u32[]{:S(2)}) async-start(bf16[32,8,2304]{2,1,0:T(8,128)(2,1)} %bitcast.23), calls=%async_computation | async-start | bytes 2359296 | tf_op jit(solution)/shard_map/all_to_all | solution.py:397
  14.7 20.7 %all-to-all-done = bf16[32,8,2304]{2,1,0:T(8,128)(2,1)S(1)} async-done(((bf16[32,8,2304]{2,1,0:T(8,128)(2,1)}), bf16[32,8,2304]{2,1,0:T(8,128)(2,1)S(1)}, u32[]{:S(2)}, u32[]{:S(2)}) %all-to-all-start) | async-done | bytes 1179680 | tf_op jit(solution)/shard_map/all_to_all | solution.py:397
  35.4 0.0 copy-start.3
  35.4 1.0 copy-done.3
  36.5 7.3 %pre.1 = (bf16[160,2048]{1,0:T(8,128)(2,1)}, f32[160,2048]{1,0:T(8,128)}) custom-call(s32[1]{0:T(128)} %bitcast.3.refs_0_, bf16[256,2304]{1,0:T(8,128)(2,1)} %bitcast.30, bf16[1792,1024]{1,0:T(8,128)(2,1)} %bitcast.26, bf16[1792,1024]{1,0:T(8,128)(2,1)} %bitcast.28), custom_call_target="tpu_custom_call" | custom-call | flops 2348810240 | bytes 7340032 | tf_op jit(solution)/shard_map/pre/pallas_call | solution.py:183
  43.8 0.0 collective-permute-start
  43.8 3.4 %send_grads.1 = bf16[256,2304]{1,0:T(8,128)(2,1)} custom-call(s32[8,256]{1,0:T(8,128)} %bitcast.33, s32[8,256]{1,0:T(8,128)} %bitcast.37, f32[8,256]{1,0:T(8,128)} %bitcast.40, bf16[256,1792]{1,0:T(8,128)(2,1)} %source_ref.3), custom_call_target="tpu_custom_call" | custom-call | flops 469762048 | bytes 2752512 | tf_op jit(solution)/shard_map/send_grads/pallas_call | solution.py:135
  47.2 3.9 %all-to-all-start.2 = ((bf16[32,8,2304]{2,1,0:T(8,128)(2,1)}), bf16[32,8,2304]{2,1,0:T(8,128)(2,1)S(1)}, u32[]{:S(2)}, u32[]{:S(2)}) async-start(bf16[32,8,2304]{2,1,0:T(8,128)(2,1)} %bitcast.24), calls=%async_computation.2 | async-start | bytes 2359296 | tf_op jit(solution)/shard_map/all_to_all | solution.py:397
  51.2 0.0 collective-permute-done.recv_ref
  51.2 0.0 copy-start.6
  51.2 0.8 copy-done.6
  52.0 2.9 %pre_add.1 = (f32[160,2048]{1,0:T(8,128)}, bf16[160,2048]{1,0:T(8,128)(2,1)}) custom-call(f32[160,2048]{1,0:T(8,128)} %get-tuple-element.13.keep_ref, bf16[160,2048]{1,0:T(8,128)(2,1)} %copy-done.6), custom_call_target="tpu_custom_call" | custom-call | flops 327680 | bytes 3932160 | tf_op jit(solution)/shard_map/pre_add/pallas_call | solution.py:255
  54.9 0.6 collective-permute-start.1
  55.5 17.7 %all-to-all-done.2 = bf16[32,8,2304]{2,1,0:T(8,128)(2,1)S(1)} async-done(((bf16[32,8,2304]{2,1,0:T(8,128)(2,1)}), bf16[32,8,2304]{2,1,0:T(8,128)(2,1)S(1)}, u32[]{:S(2)}, u32[]{:S(2)}) %all-to-all-start.2) | async-done | bytes 1179680 | tf_op jit(solution)/shard_map/all_to_all | solution.py:397
  73.2 0.0 copy-start
  73.2 1.0 copy-done
  74.3 5.5 %hidden_grad.1 = (bf16[160,1024]{1,0:T(8,128)(2,1)}, f32[160,1024]{1,0:T(8,128)}) custom-call(s32[1]{0:T(128)} %bitcast.3.refs_0_, bf16[256,2304]{1,0:T(8,128)(2,1)} %bitcast.21, bf16[1024,1792]{1,0:T(8,128)(2,1)} %bitcast.18), custom_call_target="tpu_custom_call" | custom-call | flops 1174405120 | bytes 3670016 | tf_op jit(solution)/shard_map/hidden_grad/pallas_call | solution.py:183
  79.8 0.0 collective-permute-start.3
  79.8 0.0 collective-permute-done.1.recv_ref
  79.8 0.0 copy-start.2
  79.8 0.8 copy-done.2
  80.6 3.5 %hidden.1.refs_1_ = bf16[160,1024]{1,0:T(8,128)(2,1)} custom-call(f32[160,2048]{1,0:T(8,128)} %get-tuple-element.15.total_ref, bf16[160,2048]{1,0:T(8,128)(2,1)} %copy-done.2), custom_call_target="tpu_custom_call" | custom-call | flops 3276800 | bytes 2293760 | tf_op jit(solution)/shard_map/hidden/pallas_call | solution.py:276
  84.1 0.5 collective-permute-start.2
  84.6 0.0 collective-permute-done.3.recv_ref
  84.6 0.0 copy-start.9
  84.6 0.7 copy-done.9
  85.4 2.2 %grad_add.1 = (f32[160,1024]{1,0:T(8,128)}, bf16[160,1024]{1,0:T(8,128)(2,1)}) custom-call(f32[160,1024]{1,0:T(8,128)} %get-tuple-element.18.keep_ref, bf16[160,1024]{1,0:T(8,128)(2,1)} %copy-done.9), custom_call_target="tpu_custom_call" | custom-call | flops 163840 | bytes 1966080 | tf_op jit(solution)/shard_map/grad_add/pallas_call | solution.py:255
  87.6 1.9 %collective-permute-start.4 = (bf16[160,1024]{1,0:T(8,128)(2,1)}, bf16[160,1024]{1,0:T(8,128)(2,1)S(1)}, u32[]{:S(2)}, u32[]{:S(2)}) collective-permute-start(bf16[160,1024]{1,0:T(8,128)(2,1)} %get-tuple-element.21), channel_id=1, source_target_pairs={{0,2},{1,3},{2,0},{3,1},{4,6},{5,7},{6,4},{7,5},{8,10},{9,11},{10,... | collective-permute-start | bytes 983048 | tf_op jit(solution)/shard_map/ppermute | solution.py:401
  89.4 0.0 collective-permute-done.2.refs_2_
  89.4 0.0 copy-start.7
  89.4 0.7 copy-done.7
  90.2 8.6 %rows_out.1 = bf16[256,2304]{1,0:T(8,128)(2,1)} custom-call(s32[1]{0:T(128)} %bitcast.3.refs_0_, bf16[160,1024]{1,0:T(8,128)(2,1)} %hidden.1.refs_1_, bf16[160,1024]{1,0:T(8,128)(2,1)} %copy-done.7, bf16[1024,1792]{1,0:T(8,128)(2,1)} %bitcast.19), custom_call_target="tpu_custom_call" | custom-call | flops 1174405120 | bytes 3670016 | tf_op jit(solution)/shard_map/rows_out/pallas_call | solution.py:236
  98.7 8.7 %all-to-all-start.1 = ((bf16[32,8,2304]{2,1,0:T(8,128)(2,1)}), bf16[32,8,2304]{2,1,0:T(8,128)(2,1)S(1)}, u32[]{:S(2)}, u32[]{:S(2)}) async-start(bf16[32,8,2304]{2,1,0:T(8,128)(2,1)} %bitcast.25), calls=%async_computation.1 | async-start | bytes 2359296 | tf_op jit(solution)/shard_map/all_to_all | solution.py:397
  107.4 0.0 collective-permute-done.4.grad_recv_ref
  107.4 0.0 copy-start.8
  107.4 0.7 copy-done.8
  108.1 3.0 %pair_grads.1.refs_1_ = bf16[160,2048]{1,0:T(8,128)(2,1)} custom-call(f32[160,2048]{1,0:T(8,128)} %get-tuple-element.15.total_ref, bf16[160,2048]{1,0:T(8,128)(2,1)} %copy-done.2, f32[160,1024]{1,0:T(8,128)} %get-tuple-element.20.grad_total_ref, bf16[160,1024]{1,0:T(8,128)(2,1)} %copy-done.8), custom_call_target="tpu_custom_call" | custom-call | flops 4915200 | bytes 3932160 | tf_op jit(solution)/shard_map/pair_grads/pallas_call | solution.py:311
  111.1 0.0 collective-permute-start.5
  111.1 2.3 %collective-permute-done.5.refs_2_ = bf16[160,2048]{1,0:T(8,128)(2,1)S(1)} collective-permute-done((bf16[160,2048]{1,0:T(8,128)(2,1)}, bf16[160,2048]{1,0:T(8,128)(2,1)S(1)}, u32[]{:S(2)}, u32[]{:S(2)}) %collective-permute-start.5) | collective-permute-done | bytes 655392 | tf_op jit(solution)/shard_map/ppermute | solution.py:401
  113.4 0.0 copy-start.5
  113.4 0.8 copy-done.5
  114.3 13.8 %rows_back.1 = bf16[256,2304]{1,0:T(8,128)(2,1)} custom-call(s32[1]{0:T(128)} %bitcast.3.refs_0_, bf16[160,2048]{1,0:T(8,128)(2,1)} %pair_grads.1.refs_1_, bf16[160,2048]{1,0:T(8,128)(2,1)} %copy-done.5, bf16[1792,1024]{1,0:T(8,128)(2,1)} %bitcast.27, bf16[1792,1024]{1,0:T(8,128)(2,1)} %bitcast.29), custom_call_target="tpu_custom_call" | custom-call | flops 2348810240 | bytes 7340032 | tf_op jit(solution)/shard_map/rows_back/pallas_call | solution.py:236
  128.1 0.5 all-to-all-done.1
  128.5 0.0 copy-start.4
  128.5 1.0 copy-done.4
  129.6 9.3 %all-to-all-start.3 = ((bf16[32,8,2304]{2,1,0:T(8,128)(2,1)}), bf16[32,8,2304]{2,1,0:T(8,128)(2,1)S(1)}, u32[]{:S(2)}, u32[]{:S(2)}) async-start(bf16[32,8,2304]{2,1,0:T(8,128)(2,1)} %bitcast.20), calls=%async_computation.3 | async-start | bytes 2359296 | tf_op jit(solution)/shard_map/all_to_all | solution.py:397
  138.9 0.0 copy-start.10
  138.9 5.0 %mix.1 = (bf16[256,1792]{1,0:T(8,128)(2,1)}, f32[8,256]{1,0:T(8,128)}) custom-call(s32[8,256]{1,0:T(8,128)} %bitcast.34, s32[8,256]{1,0:T(8,128)} %bitcast.38, f32[8,256]{1,0:T(8,128)} %bitcast.41, bf16[256,1792]{1,0:T(8,128)(2,1)} %source_ref.3, bf16[256,2304]{1,0:T(8,128)(2,1)} %bitcast.31), custom_call_target="tpu_custom_call" | custom-call | flops 1409286144 | bytes 2752512 | tf_op jit(solution)/shard_map/mix/pallas_call | solution.py:358
  143.9 0.0 collective-permute-start.6
  143.9 0.0 copy-done.10
  143.9 1.4 collective-permute-done.6
  145.3 0.7 add.11
  146.0 0.8 collective-permute-start.7
  146.8 6.4 %collective-permute-done.7 = f32[8,256]{1,0:T(8,128)S(1)} collective-permute-done((f32[8,256]{1,0:T(8,128)S(1)}, f32[8,256]{1,0:T(8,128)S(1)}, u32[]{:S(2)}, u32[]{:S(2)}) %collective-permute-start.7) | collective-permute-done | bytes 8224 | tf_op jit(solution)/shard_map/ppermute | solution.py:401
  153.2 0.6 multiply_bitcast_fusion
  153.8 6.2 %all-to-all-done.3 = bf16[32,8,2304]{2,1,0:T(8,128)(2,1)S(1)} async-done(((bf16[32,8,2304]{2,1,0:T(8,128)(2,1)}), bf16[32,8,2304]{2,1,0:T(8,128)(2,1)S(1)}, u32[]{:S(2)}, u32[]{:S(2)}) %all-to-all-start.3) | async-done | bytes 1179680 | tf_op jit(solution)/shard_map/all_to_all | solution.py:397
  160.0 0.0 copy-start.1
  160.0 1.0 copy-done.1
  161.1 3.3 %token_grads.1 = bf16[256,1792]{1,0:T(8,128)(2,1)} custom-call(s32[8,256]{1,0:T(8,128)} %bitcast.35, s32[8,256]{1,0:T(8,128)} %bitcast.39, bf16[256,2304]{1,0:T(8,128)(2,1)} %bitcast.22), custom_call_target="tpu_custom_call" | custom-call | flops 469762048 | bytes 2752512 | tf_op jit(solution)/shard_map/token_grads/pallas_call | solution.py:386
  (3 shorter events, 0.0 us)
Async XLA Ops:
  3.8 31.6 %all-to-all-start = ((bf16[32,8,2304]{2,1,0:T(8,128)(2,1)}), bf16[32,8,2304]{2,1,0:T(8,128)(2,1)S(1)}, u32[]{:S(2)}, u32[]{:S(2)}) async-start(bf16[32,8,2304]{2,1,0:T(8,128)(2,1)} %bitcast.23), calls=%async_computation | async-start | bytes 2359296 | tf_op jit(solution)/shard_map/all_to_all | solution.py:397
  35.4 1.0 copy-start.3
  43.8 7.4 %collective-permute-start = (bf16[160,2048]{1,0:T(8,128)(2,1)}, bf16[160,2048]{1,0:T(8,128)(2,1)S(1)}, u32[]{:S(2)}, u32[]{:S(2)}) collective-permute-start(bf16[160,2048]{1,0:T(8,128)(2,1)} %get-tuple-element.14), channel_id=1, source_target_pairs={{0,1},{1,0},{2,3},{3,2},{4,5},{5,4},{6,7},{7,6},{8,9},{9,8},{10,11... | collective-permute-start | bytes 1966088 | tf_op jit(solution)/shard_map/ppermute | solution.py:401
  47.2 26.0 %all-to-all-start.2 = ((bf16[32,8,2304]{2,1,0:T(8,128)(2,1)}), bf16[32,8,2304]{2,1,0:T(8,128)(2,1)S(1)}, u32[]{:S(2)}, u32[]{:S(2)}) async-start(bf16[32,8,2304]{2,1,0:T(8,128)(2,1)} %bitcast.24), calls=%async_computation.2 | async-start | bytes 2359296 | tf_op jit(solution)/shard_map/all_to_all | solution.py:397
  51.2 0.8 copy-start.6
  54.9 24.9 %collective-permute-start.1 = (bf16[160,2048]{1,0:T(8,128)(2,1)}, bf16[160,2048]{1,0:T(8,128)(2,1)S(1)}, u32[]{:S(2)}, u32[]{:S(2)}) collective-permute-start(bf16[160,2048]{1,0:T(8,128)(2,1)} %get-tuple-element.16), channel_id=1, source_target_pairs={{0,2},{1,3},{2,0},{3,1},{4,6},{5,7},{6,4},{7,5},{8,10},{9,11},{10,... | collective-permute-start | bytes 1966088 | tf_op jit(solution)/shard_map/ppermute | solution.py:401
  73.2 1.0 copy-start
  79.8 4.8 %collective-permute-start.3 = (bf16[160,1024]{1,0:T(8,128)(2,1)}, bf16[160,1024]{1,0:T(8,128)(2,1)S(1)}, u32[]{:S(2)}, u32[]{:S(2)}) collective-permute-start(bf16[160,1024]{1,0:T(8,128)(2,1)} %get-tuple-element.19), channel_id=1, source_target_pairs={{0,1},{1,0},{2,3},{3,2},{4,5},{5,4},{6,7},{7,6},{8,9},{9,8},{10,11... | collective-permute-start | bytes 983048 | tf_op jit(solution)/shard_map/ppermute | solution.py:401
  79.8 0.8 copy-start.2
  84.1 5.3 %collective-permute-start.2 = (bf16[160,1024]{1,0:T(8,128)(2,1)}, bf16[160,1024]{1,0:T(8,128)(2,1)S(1)}, u32[]{:S(2)}, u32[]{:S(2)}) collective-permute-start(bf16[160,1024]{1,0:T(8,128)(2,1)} %hidden.1.refs_1_), channel_id=1, source_target_pairs={{0,1},{1,0},{2,3},{3,2},{4,5},{5,4},{6,7},{7,6},{8,9},{9,8},{10,11... | collective-permute-start | bytes 983048 | tf_op jit(solution)/shard_map/ppermute | solution.py:401
  84.6 0.7 copy-start.9
  87.6 19.9 %collective-permute-start.4 = (bf16[160,1024]{1,0:T(8,128)(2,1)}, bf16[160,1024]{1,0:T(8,128)(2,1)S(1)}, u32[]{:S(2)}, u32[]{:S(2)}) collective-permute-start(bf16[160,1024]{1,0:T(8,128)(2,1)} %get-tuple-element.21), channel_id=1, source_target_pairs={{0,2},{1,3},{2,0},{3,1},{4,6},{5,7},{6,4},{7,5},{8,10},{9,11},{10,... | collective-permute-start | bytes 983048 | tf_op jit(solution)/shard_map/ppermute | solution.py:401
  89.4 0.7 copy-start.7
  98.7 29.8 %all-to-all-start.1 = ((bf16[32,8,2304]{2,1,0:T(8,128)(2,1)}), bf16[32,8,2304]{2,1,0:T(8,128)(2,1)S(1)}, u32[]{:S(2)}, u32[]{:S(2)}) async-start(bf16[32,8,2304]{2,1,0:T(8,128)(2,1)} %bitcast.25), calls=%async_computation.1 | async-start | bytes 2359296 | tf_op jit(solution)/shard_map/all_to_all | solution.py:397
  107.4 0.7 copy-start.8
  111.1 2.3 %collective-permute-start.5 = (bf16[160,2048]{1,0:T(8,128)(2,1)}, bf16[160,2048]{1,0:T(8,128)(2,1)S(1)}, u32[]{:S(2)}, u32[]{:S(2)}) collective-permute-start(bf16[160,2048]{1,0:T(8,128)(2,1)} %pair_grads.1.refs_1_), channel_id=1, source_target_pairs={{0,1},{1,0},{2,3},{3,2},{4,5},{5,4},{6,7},{7,6},{8,9},{9,8},{10,11... | collective-permute-start | bytes 1966088 | tf_op jit(solution)/shard_map/ppermute | solution.py:401
  113.4 0.8 copy-start.5
  128.5 1.0 copy-start.4
  129.6 30.5 %all-to-all-start.3 = ((bf16[32,8,2304]{2,1,0:T(8,128)(2,1)}), bf16[32,8,2304]{2,1,0:T(8,128)(2,1)S(1)}, u32[]{:S(2)}, u32[]{:S(2)}) async-start(bf16[32,8,2304]{2,1,0:T(8,128)(2,1)} %bitcast.20), calls=%async_computation.3 | async-start | bytes 2359296 | tf_op jit(solution)/shard_map/all_to_all | solution.py:397
  138.9 5.0 %copy-start.10 = (f32[256,8]{0,1:T(8,128)S(1)}, f32[256,8]{0,1:T(8,128)}, u32[]{:S(2)}) copy-start(f32[256,8]{0,1:T(8,128)} %param.11) | copy-start | bytes 24580
  143.9 1.4 collective-permute-start.6
  146.0 7.2 %collective-permute-start.7 = (f32[8,256]{1,0:T(8,128)S(1)}, f32[8,256]{1,0:T(8,128)S(1)}, u32[]{:S(2)}, u32[]{:S(2)}) collective-permute-start(f32[8,256]{1,0:T(8,128)S(1)} %add.11), channel_id=1, source_target_pairs={{0,2},{1,3},{2,0},{3,1},{4,6},{5,7},{6,4},{7,5},{8,10},{9,11},{10,... | collective-permute-start | bytes 24584 | tf_op jit(solution)/shard_map/ppermute | solution.py:401
  160.0 1.0 copy-start.1

commit v2 on v1

v2 whole, which is shorter than its diff:
```python
import jax
import jax.numpy as jnp
from jax import lax
from jax.experimental import pallas as pl
from jax.experimental.pallas import tpu as pltpu
from jax.sharding import PartitionSpec as P

TOP = 8
CAP = 10
FLIGHT = 32
STRIDE = 8
TOK = 256
WIDTH = 1792
FF = 1024
MAIN = 8
TAIL = 512
PACKED = WIDTH + TAIL
PAYLOAD = 2 * PACKED
HALF_WIDTH = WIDTH // 2
SPARE = WIDTH + 256
BLOCK = 3 * 512
ROWS = FLIGHT * MAIN
HALF_MAIN = ROWS // 2
HALF = FLIGHT * CAP // 2
TILE = 256
SPAN = 512
STEPS = WIDTH // TILE
ROUTE_SCALE = 2.5
F32 = jnp.float32
BF16 = jnp.bfloat16
NN = (((1,), (0,)), ((), ()))
NT = (((1,), (1,)), ((), ()))
TN = (((0,), (0,)), ((), ()))


def dot(a, b, dims=NN, exact=False):
    precision = lax.Precision.HIGHEST if exact else None
    return lax.dot_general(a, b, dims, precision=precision, preferred_element_type=F32)


def iota(shape, dim):
    return lax.broadcasted_iota(jnp.int32, shape, dim)


def expert_marks(ids_ref, keep_ref, values_ref=None):
    expert = iota((FLIGHT, TOK), 0) * STRIDE
    marks = jnp.zeros((FLIGHT, TOK), F32)
    values = jnp.zeros((FLIGHT, TOK), F32)
    for k in range(TOP):
        hit = (ids_ref[k : k + 1, :] == expert) & (keep_ref[k : k + 1, :] == 1)
        marks = jnp.where(hit, 1.0, marks)
        if values_ref is not None:
            values = jnp.where(hit, values_ref[k : k + 1, :], values)
    return marks, values


def spread_matrix():
    return as_bf16(iota((ROWS, FLIGHT), 0) // MAIN == iota((ROWS, FLIGHT), 1))


def slots_of(marks):
    earlier = as_bf16(iota((TOK, TOK), 0) < iota((TOK, TOK), 1))
    position = dot(marks.astype(BF16), earlier)
    return jnp.where((marks > 0.5) & (position < CAP), position, 31.0)


def picks(slot):
    spread = dot(spread_matrix(), slot.astype(BF16))
    sub = (iota((ROWS, TOK), 0) % MAIN).astype(F32)
    tail_sub = (iota((ROWS, TOK), 0) % 2 + MAIN).astype(F32)
    return spread == sub, spread == tail_sub


def as_bf16(mask):
    return jnp.where(mask, 1.0, 0.0).astype(BF16)


def halves_of(values):
    high = values.astype(BF16)
    return high, (values - high.astype(F32)).astype(BF16)


def weights_of(affinity_ref):
    affinity = affinity_ref[...]
    return ROUTE_SCALE * affinity / jnp.sum(affinity, axis=0, keepdims=True)


def send_kernel(ids_ref, keep_ref, affinity_ref, token_ref, cot_ref, out_ref, weight_ref, in_ref, packed_ref, in_sem, out_sem):
    def load(i):
        source = (token_ref, cot_ref)[i // 2]
        cols = slice(i % 2 * HALF_WIDTH, (i % 2 + 1) * HALF_WIDTH)
        return pltpu.make_async_copy(source.at[:, cols], in_ref.at[i], in_sem.at[i])

    def store(i):
        first = i // 3 * PACKED + i % 3 * HALF_WIDTH
        last = first + (TAIL if i % 3 == 2 else HALF_WIDTH)
        cols = slice(first, last)
        return pltpu.make_async_copy(packed_ref.at[:, cols], out_ref.at[:, cols], out_sem.at[i])

    for i in range(4):
        load(i).start()
    weight_ref[...] = weights_of(affinity_ref)
    marks, weights = expert_marks(ids_ref, keep_ref, weight_ref)
    main, tail = picks(slots_of(marks))
    main_place, tail_place = as_bf16(main), as_bf16(tail)
    piece_of_row = iota((ROWS, 128), 0) % MAIN // 2
    scales = None
    for array in range(2):
        if array == 1:
            high, low = halves_of(weights)
            wide = dot(spread_matrix(), high) + dot(spread_matrix(), low)
            scales = [
                jnp.sum(jnp.where(mask, wide, 0.0), axis=1, keepdims=True) for mask in (main, tail)
            ]
        tails = [jnp.zeros((ROWS, 128), BF16)] * 4
        for half in range(2):
            load(2 * array + half).wait()
            block = in_ref[2 * array + half]
            first, second = dot(main_place, block), dot(tail_place, block)
            if scales is not None:
                first, second = first * scales[0], second * scales[1]
            at = array * PACKED + half * HALF_WIDTH
            packed_ref[:, at : at + HALF_WIDTH] = first.astype(BF16)
            store(3 * array + half).start()
            second = second.astype(BF16)
            for m in range(7):
                feature = 7 * half + m
                tails[feature % 4] = jnp.where(
                    piece_of_row == feature // 4, second[:, 128 * m : 128 * (m + 1)], tails[feature % 4]
                )
        at = array * PACKED + WIDTH
        for m in range(4):
            packed_ref[:, at + 128 * m : at + 128 * (m + 1)] = tails[m]
        store(3 * array + 2).start()
    for i in range(6):
        store(i).wait()


ROOMY = pltpu.CompilerParams(vmem_limit_bytes=60 * 2**20)
LIMITED = pltpu.CompilerParams(vmem_limit_bytes=24 * 2**20)


def vmem(n):
    return [pl.BlockSpec(memory_space=pltpu.VMEM)] * n


def cost(flops, moved):
    return pl.CostEstimate(flops=int(flops), bytes_accessed=int(moved), transcendentals=0)


def send_rows(ids, keep, affinity, tokens, cotangent):
    return pl.pallas_call(
        send_kernel,
        out_shape=jax.ShapeDtypeStruct((ROWS, PAYLOAD), BF16),
        in_specs=vmem(3) + [pl.BlockSpec(memory_space=pl.ANY)] * 2,
        out_specs=pl.BlockSpec(memory_space=pl.ANY),
        scratch_shapes=[
            pltpu.VMEM((TOP, TOK), F32),
            pltpu.VMEM((4, TOK, HALF_WIDTH), BF16),
            pltpu.VMEM((ROWS, PAYLOAD), BF16),
            pltpu.SemaphoreType.DMA((4,)),
            pltpu.SemaphoreType.DMA((6,)),
        ],
        compiler_params=ROOMY,
        cost_estimate=cost(8 * ROWS * TOK * WIDTH, 2 * TOK * WIDTH * 6),
        name="send_rows",
    )(ids, keep, affinity, tokens, cotangent)


def unpack_half(packed_ref, at, half, out_ref, base):
    rows = pl.ds(pl.multiple_of(half * HALF_MAIN, HALF_MAIN), HALF_MAIN)
    out_ref[base : base + HALF_MAIN, :] = packed_ref[rows, at : at + WIDTH]
    tail = packed_ref[rows, at + WIDTH : at + PACKED]
    shape = (HALF - HALF_MAIN, HALF_MAIN)
    row, col = iota(shape, 0), iota(shape, 1)
    for g in range(4):
        same = (row // 2 == col // MAIN) & (col % MAIN == 2 * g + row % 2)
        piece = dot(as_bf16(same), tail).astype(BF16)
        width = min(TAIL, WIDTH - g * TAIL)
        out_ref[base + HALF_MAIN : base + HALF, g * TAIL : g * TAIL + width] = piece[:, :width]


def partial_kernel(flipped, spans, at, core_ref, packed_ref, *rest):
    count = len(spans)
    weight_refs, (send_ref, keep_ref, rows_ref) = rest[:count], rest[count:]
    if at is None:
        rows_ref = packed_ref
    else:
        core = core_ref[0]
        unpack_half(packed_ref, at, 1 - core, rows_ref, 0)
        unpack_half(packed_ref, at, core, rows_ref, HALF)
    for i, (weight_ref, first) in enumerate(zip(weight_refs, spans)):
        span = slice(first, first + SPAN)
        weight = weight_ref[span, :] if flipped else weight_ref[:, span]
        product = dot(rows_ref[...], weight, NT if flipped else NN)
        cols = slice(i * SPAN, (i + 1) * SPAN)
        send_ref[:, cols] = product[:HALF].astype(BF16)
        keep_ref[:, cols] = product[HALF:]


def partial_sums(name, core, packed, at, weights, spans, flipped):
    count = len(weights)
    return pl.pallas_call(
        lambda *refs: partial_kernel(flipped, spans, at, *refs),
        out_shape=(
            jax.ShapeDtypeStruct((HALF, count * SPAN), BF16),
            jax.ShapeDtypeStruct((HALF, count * SPAN), F32),
            jax.ShapeDtypeStruct((2 * HALF, WIDTH) if at is not None else (8, 128), BF16),
        ),
        in_specs=[pl.BlockSpec(memory_space=pltpu.SMEM)] + vmem(1 + count),
        out_specs=tuple(vmem(3)),
        compiler_params=LIMITED,
        cost_estimate=cost(1e6, 1e4),
        name=name,
    )(core, packed, *weights)


def grad_kernel(core_ref, packed_ref, weight_ref, send_ref, keep_ref, rows_ref):
    core = core_ref[0]
    unpack_half(packed_ref, PACKED, 1 - core, rows_ref, 0)
    unpack_half(packed_ref, PACKED, core, rows_ref, HALF)
    product = dot(rows_ref[...], weight_ref[...], NT)
    send_ref[...] = product[:HALF].astype(BF16)
    keep_ref[...] = product[HALF:]


def grad_sums(core, packed, weight):
    return pl.pallas_call(
        grad_kernel,
        out_shape=(
            jax.ShapeDtypeStruct((HALF, FF), BF16),
            jax.ShapeDtypeStruct((HALF, FF), F32),
        ),
        in_specs=[pl.BlockSpec(memory_space=pltpu.SMEM)] + vmem(2),
        out_specs=tuple(vmem(2)),
        scratch_shapes=[pltpu.VMEM((2 * HALF, WIDTH), BF16)],
        compiler_params=LIMITED,
        cost_estimate=cost(1e6, 1e4),
        name="grad",
    )(core, packed, weight)


def block_products(rows_ref, first, gate_ref, up_ref, down_ref, cols):
    span = slice(first, first + SPAN)
    out = dot(rows_ref[:, :SPAN], down_ref[span, cols])
    back = dot(rows_ref[:, SPAN : 2 * SPAN], gate_ref[cols, span], NT)
    back += dot(rows_ref[:, 2 * SPAN : BLOCK], up_ref[cols, span], NT)
    return out, back


def spread_first_kernel(own_ref, peer_ref, gate_ref, up_ref, down_ref, out_ref, back_ref, rows_ref):
    rows_ref[:HALF] = own_ref[...]
    rows_ref[HALF:] = peer_ref[...]
    for g in range(2):
        cols = slice(g * HALF_WIDTH, (g + 1) * HALF_WIDTH)
        out_ref[:, cols], back_ref[:, cols] = block_products(
            rows_ref, 0, gate_ref, up_ref, down_ref, cols
        )


def spread_first(own, peer, gate, up, down):
    return pl.pallas_call(
        spread_first_kernel,
        out_shape=(
            jax.ShapeDtypeStruct((2 * HALF, WIDTH), F32),
            jax.ShapeDtypeStruct((2 * HALF, WIDTH), F32),
        ),
        in_specs=vmem(5),
        out_specs=tuple(vmem(2)),
        scratch_shapes=[pltpu.VMEM((2 * HALF, BLOCK), BF16)],
        compiler_params=LIMITED,
        cost_estimate=cost(1e6, 1e4),
        name="spread_a",
    )(own, peer, gate, up, down)


def spread_last_kernel(core_ref, own_ref, peer_ref, gate_ref, up_ref, down_ref, out_sum, back_sum, packed_ref, rows_ref):
    core = core_ref[0]
    rows_ref[:HALF] = own_ref[:, :BLOCK]
    rows_ref[HALF:] = peer_ref[:, :BLOCK]
    for at in (WIDTH, PACKED + WIDTH):
        packed_ref[:, at : at + TAIL] = jnp.zeros((ROWS, TAIL), BF16)
    shape = (HALF_MAIN, HALF - HALF_MAIN)
    row, col = iota(shape, 0), iota(shape, 1)
    for g in range(4):
        width = min(TAIL, WIDTH - g * TAIL)
        cols = slice(g * TAIL, g * TAIL + width)
        products = block_products(rows_ref, SPAN, gate_ref, up_ref, down_ref, cols)
        place = as_bf16((row // MAIN == col // 2) & (row % MAIN == 2 * g + col % 2))
        for product, sum_ref, at in zip(products, (out_sum, back_sum), (0, PACKED)):
            product = (product + sum_ref[:, cols]).astype(BF16)
            for base, half in ((0, core), (HALF, 1 - core)):
                rows = pl.ds(pl.multiple_of(half * HALF_MAIN, HALF_MAIN), HALF_MAIN)
                packed_ref[rows, at + g * TAIL : at + g * TAIL + width] = product[
                    base : base + HALF_MAIN
                ]
                tail = dot(place, product[base + HALF_MAIN : base + HALF]).astype(BF16)
                packed_ref[rows, at + WIDTH : at + WIDTH + width] += tail
    for half_ref, half in ((own_ref, core), (peer_ref, 1 - core)):
        carried = half_ref[:, BLOCK:]
        total = jnp.zeros((HALF_MAIN, 128), F32)
        for first, count, each, base in ((0, HALF_MAIN, MAIN, 0), (HALF_MAIN, HALF - HALF_MAIN, 2, MAIN)):
            row, col = iota((HALF_MAIN, count), 0), iota((HALF_MAIN, count), 1)
            lane = iota((count, 128), 1) == base + iota((count, 128), 0) % each
            for part in range(2):
                place = as_bf16((row // MAIN == col // each) & (row % MAIN == 6 + part))
                column = carried[first : first + count, part : part + 1].astype(F32)
                total += dot(place, jnp.where(lane, column, 0.0).astype(BF16))
        rows = pl.ds(pl.multiple_of(half * HALF_MAIN, HALF_MAIN), HALF_MAIN)
        spare = slice(PACKED + SPARE, PACKED + SPARE + 128)
        packed_ref[rows, spare] = (packed_ref[rows, spare].astype(F32) + total).astype(BF16)


def spread_last(core, own, peer, gate, up, down, out_sum, back_sum):
    return pl.pallas_call(
        spread_last_kernel,
        out_shape=jax.ShapeDtypeStruct((ROWS, PAYLOAD), BF16),
        in_specs=[pl.BlockSpec(memory_space=pltpu.SMEM)] + vmem(7),
        out_specs=pl.BlockSpec(memory_space=pltpu.VMEM),
        scratch_shapes=[pltpu.VMEM((2 * HALF, BLOCK), BF16)],
        compiler_params=LIMITED,
        cost_estimate=cost(1e6, 1e4),
        name="spread_b",
    )(core, own, peer, gate, up, down, out_sum, back_sum)


def add_kernel(keep_ref, recv_ref, total_ref, send_ref):
    total = keep_ref[...] + recv_ref[...].astype(F32)
    total_ref[...] = total
    send_ref[...] = total.astype(BF16)


def add_halves(name, keep, recv):
    return pl.pallas_call(
        add_kernel,
        out_shape=(
            jax.ShapeDtypeStruct(keep.shape, F32),
            jax.ShapeDtypeStruct(keep.shape, BF16),
        ),
        in_specs=vmem(2),
        out_specs=tuple(vmem(2)),
        compiler_params=LIMITED,
        cost_estimate=cost(1e6, 1e4),
        name=name,
    )(keep, recv)


def block_kernel(first, total_ref, recv_ref, grad_total_ref, grad_recv_ref, *rest):
    pre = total_ref[...] + recv_ref[...].astype(F32)
    gate, up = pre[:, :SPAN], pre[:, SPAN:]
    cols = slice(first, first + SPAN)
    grad = grad_total_ref[:, cols] + grad_recv_ref[:, cols].astype(F32)
    sigma = jax.nn.sigmoid(gate)
    hidden = gate * sigma * up
    inner = jnp.sum(hidden * grad, axis=1, keepdims=True)
    if first == 0:
        out_ref, inner_ref = rest
        inner_ref[...] = jnp.broadcast_to(inner, (HALF, 128))
    else:
        inner_ref, out_ref = rest
        high, low = halves_of(inner + inner_ref[:, :1])
        lane = iota((HALF, 128), 1)
        both = jnp.where(lane == 0, high.astype(F32), jnp.where(lane == 1, low.astype(F32), 0.0))
        out_ref[:, BLOCK:] = both.astype(BF16)
    out_ref[:, :SPAN] = hidden.astype(BF16)
    out_ref[:, SPAN : 2 * SPAN] = (grad * up * sigma * (1.0 + gate * (1.0 - sigma))).astype(BF16)
    out_ref[:, 2 * SPAN : BLOCK] = (grad * gate * sigma).astype(BF16)


def block_of(name, first, total, recv, grad_total, grad_recv, *inner):
    block = jax.ShapeDtypeStruct((HALF, BLOCK + (128 if inner else 0)), BF16)
    return pl.pallas_call(
        lambda *refs: block_kernel(first, *refs),
        out_shape=block if inner else (block, jax.ShapeDtypeStruct((HALF, 128), F32)),
        in_specs=vmem(4 + len(inner)),
        out_specs=vmem(1)[0] if inner else tuple(vmem(2)),
        compiler_params=LIMITED,
        cost_estimate=cost(1e6, 1e4),
        name=name,
    )(total, recv, grad_total, grad_recv, *inner)


def combine_kernel(ids_ref, keep_ref, affinity_ref, packed_ref, mixed_ref, grad_ref, share_ref, weight_ref):
    weight_ref[...] = weights_of(affinity_ref)
    marks, weights = expert_marks(ids_ref, keep_ref, weight_ref)
    slot = slots_of(marks)
    main, tail = picks(slot)
    wide = dot(spread_matrix(), weights.astype(BF16))
    piece_of_row = iota((ROWS, TOK), 0) % MAIN // 2
    main_place = as_bf16(main)
    main_weight = jnp.where(main, wide, 0.0).astype(BF16)
    for n in range(STEPS):
        cols = slice(n * TILE, (n + 1) * TILE)
        chosen = tail & (piece_of_row == n // 2)
        first = WIDTH + n % 2 * TILE
        total = dot(main_weight, packed_ref[:, cols], TN)
        total += dot(
            jnp.where(chosen, wide, 0.0).astype(BF16), packed_ref[:, first : first + TILE], TN
        )
        mixed_ref[:, cols] = total.astype(BF16)
        total = dot(main_place, packed_ref[:, PACKED + n * TILE : PACKED + (n + 1) * TILE], TN)
        first += PACKED
        total += dot(as_bf16(chosen), packed_ref[:, first : first + TILE], TN)
        grad_ref[:, cols] = total.astype(BF16)

    row, col = iota((FLIGHT, ROWS), 0), iota((FLIGHT, ROWS), 1)
    both = as_bf16((col // MAIN == row) & (col % MAIN >= 6))
    carried = dot(both, packed_ref[:, PACKED + SPARE : PACKED + SPARE + 128])
    by_expert = jnp.zeros((FLIGHT, TOK), F32)
    for s in range(CAP):
        by_expert += jnp.where(slot == float(s), carried[:, s : s + 1], 0.0)
    expert = iota((FLIGHT, TOK), 0) * STRIDE
    for k in range(TOP):
        hit = (ids_ref[k : k + 1, :] == expert) & (keep_ref[k : k + 1, :] == 1)
        share_ref[k : k + 1, :] = jnp.sum(jnp.where(hit, by_expert, 0.0), axis=0, keepdims=True)
    affinity = affinity_ref[...]
    total = jnp.sum(affinity, axis=0, keepdims=True)
    inner = share_ref[...] / weight_ref[...]
    shares = affinity / total
    share_ref[...] = (
        ROUTE_SCALE / total * (inner - jnp.sum(shares * inner, axis=0, keepdims=True))
    )


def combine(ids, keep, affinity, packed):
    return pl.pallas_call(
        combine_kernel,
        out_shape=(
            jax.ShapeDtypeStruct((TOK, WIDTH), BF16),
            jax.ShapeDtypeStruct((TOK, WIDTH), BF16),
            jax.ShapeDtypeStruct((TOP, TOK), F32),
        ),
        in_specs=vmem(4),
        out_specs=tuple(vmem(3)),
        scratch_shapes=[pltpu.VMEM((TOP, TOK), F32)],
        compiler_params=LIMITED,
        cost_estimate=cost(8 * ROWS * TOK * WIDTH, 2 * TOK * WIDTH * 4),
        name="combine",
    )(ids, keep, affinity, packed)


def exchange(packed):
    return lax.all_to_all(packed, "node", split_axis=0, concat_axis=0, tiled=True)


def swap(values, distance):
    return lax.ppermute(values, "local", [(i, i ^ distance) for i in range(4)])


def per_device(tokens, expert_ids, keep_flags, affinity, w_gate, w_up, w_down, cotangent):
    core = (lax.axis_index("local") % 2).astype(jnp.int32).reshape(1)
    ids, keep, affinity_t = expert_ids.T, keep_flags.T, affinity.T
    w_gate, w_up, w_down = w_gate[0], w_up[0], w_down[0]

    rows = exchange(send_rows(ids, keep, affinity_t, tokens, cotangent))

    send_g, own_g = grad_sums(core, rows, w_down)
    total_g, send_g = add_halves("add_g", own_g, swap(send_g, 1))
    recv_g = swap(send_g, 2)
    gate_up = (w_gate, w_up)
    send_a, own_a, unpacked = partial_sums("pre_a", core, rows, 0, gate_up, (0, 0), False)
    total_a, send_a = add_halves("add_a", own_a, swap(send_a, 1))
    recv_a = swap(send_a, 2)
    unpacked, send_g = lax.optimization_barrier((unpacked, send_g))
    send_b, own_b, unused = partial_sums("pre_b", core, unpacked, None, gate_up, (SPAN, SPAN), False)
    total_b, send_b = add_halves("add_b", own_b, swap(send_b, 1))
    recv_b = swap(send_b, 2)

    block_a, inner = block_of("block_a", 0, total_a, recv_a, total_g, recv_g)
    peer_a = swap(block_a, 1)
    block_b = block_of("block_b", SPAN, total_b, recv_b, total_g, recv_g, inner)
    peer_b = swap(block_b, 1)
    block_a, block_b = lax.optimization_barrier((block_a, block_b))
    out_sum, back_sum = spread_first(block_a, peer_a, w_gate, w_up, w_down)
    payload = spread_last(core, block_b, peer_b, w_gate, w_up, w_down, out_sum, back_sum)
    rows = exchange(payload)
    mixed, token_grad, affinity_grad = combine(ids, keep, affinity_t, rows)
    return mixed, token_grad, affinity_grad.T


def solution(mesh):
    placed = (
        P("node", "local"),
        P("node", None),
        P("node", None),
        P("node", None),
        P("node", "local", None),
        P("node", "local", None),
        P("node", None, "local"),
        P("node", "local"),
    )
    return jax.shard_map(
        per_device,
        mesh=mesh,
        in_specs=placed,
        out_specs=(P("node", "local"), P("node", "local"), P("node", None)),
        check_vma=False,
    )
```

time: 165 us -> 134 us (0.81)
  Pallas kernels: 61.6 us -> 18.5 us
  blocking collectives: 0 us -> 38.9 us
  starting transfers between devices: 36.6 us -> 15.2 us
  local copies, waits for them, and re-layouts: 8.83 us -> 4.53 us
    all_to_all x0 -> x1, blocking collectives: none -> 38.9 us  [exchange(): lax.all_to_all(packed, 'node', split_axis=0, concat_axis=0, tiled=True)]
    pallas_call x10 -> x9, Pallas kernels: 56.5 us -> 18.2 us  [the longest x1 4.67 us: send_rows(): pl.pallas_call(send_kernel, out_shape=jax.ShapeDtypeStruct((ROWS, PAYLOAD...]
    all_to_all x4 -> x1, starting transfers between devices: 32.8 us -> 10.9 us  [exchange(): lax.all_to_all(packed, 'node', split_axis=0, concat_axis=0, tiled=True)]
    ppermute x8, waiting for transfers between devices: 10.1 us -> 22.4 us  [swap(): return lax.ppermute(values, 'local', [(i, i ^ distance) for i in range(4)])]
    all_to_all x4 -> x1, waiting for transfers between devices: 45.1 us -> 33.4 us  [exchange(): lax.all_to_all(packed, 'node', split_axis=0, concat_axis=0, tiled=True)]
    pallas_call x2 -> x3, Pallas kernels: 5.09 us -> 0.3 us  [add_halves(): pl.pallas_call(add_kernel, out_shape=(jax.ShapeDtypeStruct(keep.shape, F3...]
    unnamed x22 -> x16, local copies, waits for them, and re-layouts: 8.83 us -> 4.53 us
  transfers between devices with their start and end apart: 12 -> 9, of which waited for: 7 -> 5; matrix products, arithmetic and copies ran while one was open for 1% -> 0% of each run, Pallas kernels for 29% -> 4%
where the time goes in v2:
time: 134 us
  waiting for transfers between devices  55.7 us (42%)
  blocking collectives  38.9 us (29%)
  Pallas kernels  18.5 us (14%)
  starting transfers between devices  15.2 us (11%)
  local copies, waits for them, and re-layouts  4.53 us (3%)
    all_to_all x1, blocking collectives, exchange(): lax.all_to_all(packed, 'node', split_axis=0, concat_axis=0, tiled=True)  38.9 us
    all_to_all x1, waiting for transfers between devices, exchange(): lax.all_to_all(packed, 'node', split_axis=0, concat_axis=0, tiled=True)  33.4 us
    ppermute x8, waiting for transfers between devices, swap(): return lax.ppermute(values, 'local', [(i, i ^ distance) for i in range(4)])  22.4 us
    all_to_all x1, starting transfers between devices, exchange(): lax.all_to_all(packed, 'node', split_axis=0, concat_axis=0, tiled=True)  10.9 us
    pallas_call x1, Pallas kernels, send_rows(): pl.pallas_call(send_kernel, out_shape=jax.ShapeDtypeStruct((ROWS, PAYLOAD...  4.67 us
    unnamed x16, local copies, waits for them, and re-layouts  4.53 us
    ppermute x8, starting transfers between devices, swap(): return lax.ppermute(values, 'local', [(i, i ^ distance) for i in range(4)])  4.27 us
    pallas_call x1, Pallas kernels, spread_last(): pl.pallas_call(spread_last_kernel, out_shape=jax.ShapeDtypeStruct((ROWS,...  3.37 us
  transfers between devices with their start and end apart: 9, of which 5 were waited for; matrix products, arithmetic and copies ran while one was open for 0% of the time, Pallas kernels for 4%

profile of v2, /device:TPU:0, one launch (start us, length us, event | category | flops | bytes accessed | tf_op | source)
XLA Modules:
  0.0 133.5 jit_solution(17555568543803850569)
XLA Ops:
  0.6 4.7 %send_rows.1 = bf16[256,4608]{1,0:T(8,128)(2,1)} custom-call(s32[8,256]{1,0:T(8,128)} %bitcast.27, s32[8,256]{1,0:T(8,128)} %bitcast.29, f32[8,256]{1,0:T(8,128)} %bitcast.31, bf16[256,1792]{1,0:T(8,128)(2,1)} %token_ref.1, bf16[256,1792]{1,0:T(8,128)(2,1)} %cot_ref.1), custom_call_target="tpu_custom_call" | custom-call | flops 939524096 | bytes 5505024 | tf_op jit(solution)/shard_map/send_rows/pallas_call | solution.py:152
  5.3 10.9 %all-to-all-start = ((bf16[32,8,4608]{2,1,0:T(8,128)(2,1)}), bf16[32,8,4608]{2,1,0:T(8,128)(2,1)S(1)}, u32[]{:S(2)}, u32[]{:S(2)}) async-start(bf16[32,8,4608]{2,1,0:T(8,128)(2,1)} %bitcast.33), calls=%async_computation | async-start | bytes 4718592 | tf_op jit(solution)/shard_map/all_to_all | solution.py:443
  16.2 33.4 %all-to-all-done = bf16[32,8,4608]{2,1,0:T(8,128)(2,1)S(1)} async-done(((bf16[32,8,4608]{2,1,0:T(8,128)(2,1)}), bf16[32,8,4608]{2,1,0:T(8,128)(2,1)S(1)}, u32[]{:S(2)}, u32[]{:S(2)}) %all-to-all-start) | async-done | bytes 2359328 | tf_op jit(solution)/shard_map/all_to_all | solution.py:443
  49.6 0.0 copy-start.3
  49.6 2.0 %copy-done.3 = bf16[1,1024,1792]{2,1,0:T(8,128)(2,1)S(1)} copy-done((bf16[1,1024,1792]{2,1,0:T(8,128)(2,1)S(1)}, bf16[1,1024,1792]{2,1,0:T(8,128)(2,1)}, u32[]{:S(2)}) %copy-start.3) | copy-done | bytes 3670040
  51.6 0.0 copy-start
  51.6 1.5 %grad.1 = (bf16[160,1024]{1,0:T(8,128)(2,1)S(1)}, f32[160,1024]{1,0:T(8,128)S(1)}) custom-call(s32[1]{0:T(128)} %bitcast.3.refs_0_.core_ref, bf16[256,4608]{1,0:T(8,128)(2,1)S(1)} %bitcast.23, bf16[1024,1792]{1,0:T(8,128)(2,1)S(1)} %bitcast.20), custom_call_target="tpu_custom_call" | custom-call | flops 1000000 | bytes 10000 | tf_op jit(solution)/shard_map/grad/pallas_call | solution.py:228
  53.2 0.1 collective-permute-start.2
  53.2 0.4 copy-done
  53.7 0.0 copy-start.1
  53.7 2.0 %copy-done.1 = bf16[1,1792,1024]{2,1,0:T(8,128)(2,1)S(1)} copy-done((bf16[1,1792,1024]{2,1,0:T(8,128)(2,1)S(1)}, bf16[1,1792,1024]{2,1,0:T(8,128)(2,1)}, u32[]{:S(2)}) %copy-start.1) | copy-done | bytes 3670040
  55.7 1.5 %pre_a.1 = (bf16[160,1024]{1,0:T(8,128)(2,1)S(1)}, f32[160,1024]{1,0:T(8,128)S(1)}, bf16[320,1792]{1,0:T(8,128)(2,1)S(1)}) custom-call(s32[1]{0:T(128)} %bitcast.3.refs_0_.core_ref, bf16[256,4608]{1,0:T(8,128)(2,1)S(1)} %bitcast.24, bf16[1792,1024]{1,0:T(8,128)(2,1)S(1)} %bitcast.12, bf16[1792,1024]{1,0:T(8,128)(2,1)S(1)} %bitcast.16), custom_call_target="tpu_custom_call" | custom-call | flops 1000000 | bytes 10000 | tf_op jit(solution)/shard_map/pre_a/pallas_call | solution.py:203
  57.2 0.2 collective-permute-start
  57.4 0.0 collective-permute-done.2.recv_ref
  57.4 0.1 add_g.1
  57.5 0.0 copy-start.4
  57.5 1.3 %pre_b.1 = (bf16[160,1024]{1,0:T(8,128)(2,1)S(1)}, f32[160,1024]{1,0:T(8,128)S(1)}, bf16[8,128]{1,0:T(8,128)(2,1)}) custom-call(s32[1]{0:T(128)} %bitcast.3.refs_0_.core_ref, bf16[320,1792]{1,0:T(8,128)(2,1)S(1)} %get-tuple-element.36.refs_1_, bf16[1792,1024]{1,0:T(8,128)(2,1)S(1)} %bitcast.13, bf16[1792,1024]{1,0:T(8,128)(2,1)S(1)} %bitcast.17), custom_call_target="tpu_custom_call" | custom-call | flops 1000000 | bytes 10000 | tf_op jit(solution)/shard_map/pre_b/pallas_call | solution.py:203
  58.8 0.5 collective-permute-start.4
  59.3 0.8 collective-permute-start.3
  60.1 0.0 collective-permute-done.recv_ref
  60.1 0.1 add_a.1
  60.2 1.3 collective-permute-start.1
  61.5 0.0 collective-permute-done.4.recv_ref
  61.6 0.1 add_b.1
  61.7 0.0 copy-start.2
  61.7 0.9 collective-permute-start.5
  62.5 7.4 %collective-permute-done.3.refs_3_ = bf16[160,1024]{1,0:T(8,128)(2,1)S(1)} collective-permute-done((bf16[160,1024]{1,0:T(8,128)(2,1)S(1)}, bf16[160,1024]{1,0:T(8,128)(2,1)S(1)}, u32[]{:S(2)}, u32[]{:S(2)}) %collective-permute-start.3) | collective-permute-done | bytes 327712 | tf_op jit(solution)/shard_map/ppermute | solution.py:447
  69.9 7.0 %collective-permute-done.1.refs_1_ = bf16[160,1024]{1,0:T(8,128)(2,1)S(1)} collective-permute-done((bf16[160,1024]{1,0:T(8,128)(2,1)S(1)}, bf16[160,1024]{1,0:T(8,128)(2,1)S(1)}, u32[]{:S(2)}, u32[]{:S(2)}) %collective-permute-start.1) | collective-permute-done | bytes 327712 | tf_op jit(solution)/shard_map/ppermute | solution.py:447
  76.9 0.3 block_a.1
  77.2 5.8 %collective-permute-done.5.refs_1_ = bf16[160,1024]{1,0:T(8,128)(2,1)S(1)} collective-permute-done((bf16[160,1024]{1,0:T(8,128)(2,1)S(1)}, bf16[160,1024]{1,0:T(8,128)(2,1)S(1)}, u32[]{:S(2)}, u32[]{:S(2)}) %collective-permute-start.5) | collective-permute-done | bytes 327712 | tf_op jit(solution)/shard_map/ppermute | solution.py:447
  83.1 0.4 block_b.1.own_ref
  83.5 0.1 collective-permute-start.6
  83.6 0.5 collective-permute-start.7
  84.1 2.1 %collective-permute-done.7.peer_ref = bf16[160,1536]{1,0:T(8,128)(2,1)S(1)} collective-permute-done((bf16[160,1536]{1,0:T(8,128)(2,1)S(1)}, bf16[160,1536]{1,0:T(8,128)(2,1)S(1)}, u32[]{:S(2)}, u32[]{:S(2)}) %collective-permute-start.7) | collective-permute-done | bytes 491552 | tf_op jit(solution)/shard_map/ppermute | solution.py:447
  86.2 0.0 copy-done.4
  86.2 0.0 copy-done.2
  86.2 2.2 %spread_a.1 = (f32[320,1792]{1,0:T(8,128)S(1)}, f32[320,1792]{1,0:T(8,128)S(1)}) custom-call(bf16[160,1536]{1,0:T(8,128)(2,1)S(1)} %get-tuple-element.43.own_ref, bf16[160,1536]{1,0:T(8,128)(2,1)S(1)} %collective-permute-done.7.peer_ref, bf16[1792,1024]{1,0:T(8,128)(2,1)S(1)} %bitcast.14, bf16[1792,1024]{1,0:T(8,128)(2,1)S(1)} %bitcast.18, ...), custom_call_target="tpu_custom_call" | custom-call | flops 1000000 | bytes 10000 | tf_op jit(solution)/shard_map/spread_a/pallas_call | solution.py:262
  88.4 0.0 collective-permute-done.6.peer_ref
  88.4 3.4 %spread_b.1 = bf16[256,4608]{1,0:T(8,128)(2,1)S(1)} custom-call(s32[1]{0:T(128)} %bitcast.3.refs_0_.core_ref, bf16[160,1664]{1,0:T(8,128)(2,1)S(1)} %block_b.1.own_ref, bf16[160,1664]{1,0:T(8,128)(2,1)S(1)} %collective-permute-done.6.peer_ref, bf16[1792,1024]{1,0:T(8,128)(2,1)S(1)} %bitcast.15, bf16[1792,1024]{1,0:T(8,128)(2,1)S(1)} %bitcast.19, ...), custom_call_target="tpu_custom_call" | custom-call | flops 1000000 | bytes 10000 | tf_op jit(solution)/shard_map/spread_b/pallas_call | solution.py:315
  91.8 0.0 copy-start.5
  91.8 0.0 copy-start.6
  91.8 0.0 copy-start.7
  91.8 38.9 %all_to_all.22 = bf16[32,8,4608]{2,1,0:T(8,128)(2,1)S(1)} all-to-all(bf16[32,8,4608]{2,1,0:T(8,128)(2,1)S(1)} %bitcast.25), channel_id=1, replica_groups=mesh['node'=32,'local'=4] {'node'}, dimensions={0} | all-to-all | bytes 4718592 | tf_op jit(solution)/shard_map/all_to_all | solution.py:443
  130.7 0.0 copy-done.5
  130.7 0.0 copy-done.6
  130.7 0.0 copy-done.7
  130.7 2.8 %combine.1 = (bf16[256,1792]{1,0:T(8,128)(2,1)}, bf16[256,1792]{1,0:T(8,128)(2,1)}, f32[8,256]{1,0:T(8,128)}) custom-call(s32[8,256]{1,0:T(8,128)S(1)} %bitcast.28, s32[8,256]{1,0:T(8,128)S(1)} %bitcast.30, f32[8,256]{1,0:T(8,128)S(1)} %bitcast.32, bf16[256,4608]{1,0:T(8,128)(2,1)S(1)} %bitcast.26), custom_call_target="tpu_custom_call" | custom-call | flops 939524096 | bytes 3670016 | tf_op jit(solution)/shard_map/combine/pallas_call | solution.py:426
Async XLA Ops:
  5.3 44.3 %all-to-all-start = ((bf16[32,8,4608]{2,1,0:T(8,128)(2,1)}), bf16[32,8,4608]{2,1,0:T(8,128)(2,1)S(1)}, u32[]{:S(2)}, u32[]{:S(2)}) async-start(bf16[32,8,4608]{2,1,0:T(8,128)(2,1)} %bitcast.33), calls=%async_computation | async-start | bytes 4718592 | tf_op jit(solution)/shard_map/all_to_all | solution.py:443
  49.6 2.0 %copy-start.3 = (bf16[1,1024,1792]{2,1,0:T(8,128)(2,1)S(1)}, bf16[1,1024,1792]{2,1,0:T(8,128)(2,1)}, u32[]{:S(2)}) copy-start(bf16[1,1024,1792]{2,1,0:T(8,128)(2,1)} %param.14) | copy-start | bytes 11010052
  51.6 2.0 %copy-start = (bf16[1,1792,1024]{2,1,0:T(8,128)(2,1)S(1)}, bf16[1,1792,1024]{2,1,0:T(8,128)(2,1)}, u32[]{:S(2)}) copy-start(bf16[1,1792,1024]{2,1,0:T(8,128)(2,1)} %param.12) | copy-start | bytes 11010052
  53.2 4.2 %collective-permute-start.2 = (bf16[160,1024]{1,0:T(8,128)(2,1)S(1)}, bf16[160,1024]{1,0:T(8,128)(2,1)S(1)}, u32[]{:S(2)}, u32[]{:S(2)}) collective-permute-start(bf16[160,1024]{1,0:T(8,128)(2,1)S(1)} %get-tuple-element.31), channel_id=1, source_target_pairs={{0,1},{1,0},{2,3},{3,2},{4,5},{5,4},{6,7},{7,6},{8,9},{9,8},{10,11... | collective-permute-start | bytes 983048 | tf_op jit(solution)/shard_map/ppermute | solution.py:447
  53.7 2.0 %copy-start.1 = (bf16[1,1792,1024]{2,1,0:T(8,128)(2,1)S(1)}, bf16[1,1792,1024]{2,1,0:T(8,128)(2,1)}, u32[]{:S(2)}) copy-start(bf16[1,1792,1024]{2,1,0:T(8,128)(2,1)} %param.13) | copy-start | bytes 11010052
  57.2 2.9 %collective-permute-start = (bf16[160,1024]{1,0:T(8,128)(2,1)S(1)}, bf16[160,1024]{1,0:T(8,128)(2,1)S(1)}, u32[]{:S(2)}, u32[]{:S(2)}) collective-permute-start(bf16[160,1024]{1,0:T(8,128)(2,1)S(1)} %get-tuple-element.27), channel_id=1, source_target_pairs={{0,1},{1,0},{2,3},{3,2},{4,5},{5,4},{6,7},{7,6},{8,9},{9,8},{10,11... | collective-permute-start | bytes 983048 | tf_op jit(solution)/shard_map/ppermute | solution.py:447
  57.5 28.7 %copy-start.4 = (bf16[1,1024,1792]{2,1,0:T(8,128)(2,1)S(1)}, bf16[1,1024,1792]{2,1,0:T(8,128)(2,1)}, u32[]{:S(2)}) copy-start(bf16[1,1024,1792]{2,1,0:T(8,128)(2,1)} %param.14) | copy-start | bytes 11010052
  58.8 2.7 %collective-permute-start.4 = (bf16[160,1024]{1,0:T(8,128)(2,1)S(1)}, bf16[160,1024]{1,0:T(8,128)(2,1)S(1)}, u32[]{:S(2)}, u32[]{:S(2)}) collective-permute-start(bf16[160,1024]{1,0:T(8,128)(2,1)S(1)} %get-tuple-element.38), channel_id=1, source_target_pairs={{0,1},{1,0},{2,3},{3,2},{4,5},{5,4},{6,7},{7,6},{8,9},{9,8},{10,11... | collective-permute-start | bytes 983048 | tf_op jit(solution)/shard_map/ppermute | solution.py:447
  59.3 10.6 %collective-permute-start.3 = (bf16[160,1024]{1,0:T(8,128)(2,1)S(1)}, bf16[160,1024]{1,0:T(8,128)(2,1)S(1)}, u32[]{:S(2)}, u32[]{:S(2)}) collective-permute-start(bf16[160,1024]{1,0:T(8,128)(2,1)S(1)} %get-tuple-element.33), channel_id=1, source_target_pairs={{0,2},{1,3},{2,0},{3,1},{4,6},{5,7},{6,4},{7,5},{8,10},{9,11},{10,... | collective-permute-start | bytes 983048 | tf_op jit(solution)/shard_map/ppermute | solution.py:447
  60.2 16.7 %collective-permute-start.1 = (bf16[160,1024]{1,0:T(8,128)(2,1)S(1)}, bf16[160,1024]{1,0:T(8,128)(2,1)S(1)}, u32[]{:S(2)}, u32[]{:S(2)}) collective-permute-start(bf16[160,1024]{1,0:T(8,128)(2,1)S(1)} %get-tuple-element.29), channel_id=1, source_target_pairs={{0,2},{1,3},{2,0},{3,1},{4,6},{5,7},{6,4},{7,5},{8,10},{9,11},{10,... | collective-permute-start | bytes 983048 | tf_op jit(solution)/shard_map/ppermute | solution.py:447
  61.7 24.5 %copy-start.2 = (bf16[1,1792,1024]{2,1,0:T(8,128)(2,1)S(1)}, bf16[1,1792,1024]{2,1,0:T(8,128)(2,1)}, u32[]{:S(2)}) copy-start(bf16[1,1792,1024]{2,1,0:T(8,128)(2,1)} %param.13) | copy-start | bytes 11010052
  61.7 21.4 %collective-permute-start.5 = (bf16[160,1024]{1,0:T(8,128)(2,1)S(1)}, bf16[160,1024]{1,0:T(8,128)(2,1)S(1)}, u32[]{:S(2)}, u32[]{:S(2)}) collective-permute-start(bf16[160,1024]{1,0:T(8,128)(2,1)S(1)} %get-tuple-element.40), channel_id=1, source_target_pairs={{0,2},{1,3},{2,0},{3,1},{4,6},{5,7},{6,4},{7,5},{8,10},{9,11},{10,... | collective-permute-start | bytes 983048 | tf_op jit(solution)/shard_map/ppermute | solution.py:447
  83.5 4.9 %collective-permute-start.6 = (bf16[160,1664]{1,0:T(8,128)(2,1)S(1)}, bf16[160,1664]{1,0:T(8,128)(2,1)S(1)}, u32[]{:S(2)}, u32[]{:S(2)}) collective-permute-start(bf16[160,1664]{1,0:T(8,128)(2,1)S(1)} %block_b.1.own_ref), channel_id=1, source_target_pairs={{0,1},{1,0},{2,3},{3,2},{4,5},{5,4},{6,7},{7,6},{8,9},{9,8},{10,11... | collective-permute-start | bytes 1597448 | tf_op jit(solution)/shard_map/ppermute | solution.py:447
  83.6 2.6 %collective-permute-start.7 = (bf16[160,1536]{1,0:T(8,128)(2,1)S(1)}, bf16[160,1536]{1,0:T(8,128)(2,1)S(1)}, u32[]{:S(2)}, u32[]{:S(2)}) collective-permute-start(bf16[160,1536]{1,0:T(8,128)(2,1)S(1)} %get-tuple-element.43.own_ref), channel_id=1, source_target_pairs={{0,1},{1,0},{2,3},{3,2},{4,5},{5,4},{6,7},{7,6},{8,9},{9,8},{10,11... | collective-permute-start | bytes 1474568 | tf_op jit(solution)/shard_map/ppermute | solution.py:447
  91.8 38.9 %copy-start.5 = (s32[256,8]{0,1:T(8,128)S(1)}, s32[256,8]{0,1:T(8,128)}, u32[]{:S(2)}) copy-start(s32[256,8]{0,1:T(8,128)} %param.9) | copy-start | bytes 24580
  91.8 38.9 %copy-start.6 = (s32[256,8]{0,1:T(8,128)S(1)}, s32[256,8]{0,1:T(8,128)}, u32[]{:S(2)}) copy-start(s32[256,8]{0,1:T(8,128)} %param.10) | copy-start | bytes 24580
  91.8 38.9 %copy-start.7 = (f32[256,8]{0,1:T(8,128)S(1)}, f32[256,8]{0,1:T(8,128)}, u32[]{:S(2)}) copy-start(f32[256,8]{0,1:T(8,128)} %param.11) | copy-start | bytes 24580

commit v3 on v2

--- a/solution.py
+++ b/solution.py
@@ -180,39 +180,38 @@
         out_ref[base + HALF_MAIN : base + HALF, g * TAIL : g * TAIL + width] = piece[:, :width]
 
 
-def partial_kernel(flipped, spans, at, core_ref, packed_ref, *rest):
-    count = len(spans)
-    weight_refs, (send_ref, keep_ref, rows_ref) = rest[:count], rest[count:]
-    if at is None:
-        rows_ref = packed_ref
-    else:
+def partial_kernel(first, at, core_ref, packed_ref, gate_ref, up_ref, keep_ref, *rest):
+    if at is not None:
+        *send_refs, rows_ref = rest
         core = core_ref[0]
         unpack_half(packed_ref, at, 1 - core, rows_ref, 0)
         unpack_half(packed_ref, at, core, rows_ref, HALF)
-    for i, (weight_ref, first) in enumerate(zip(weight_refs, spans)):
-        span = slice(first, first + SPAN)
-        weight = weight_ref[span, :] if flipped else weight_ref[:, span]
-        product = dot(rows_ref[...], weight, NT if flipped else NN)
-        cols = slice(i * SPAN, (i + 1) * SPAN)
-        send_ref[:, cols] = product[:HALF].astype(BF16)
-        keep_ref[:, cols] = product[HALF:]
-
-
-def partial_sums(name, core, packed, at, weights, spans, flipped):
-    count = len(weights)
-    return pl.pallas_call(
-        lambda *refs: partial_kernel(flipped, spans, at, *refs),
-        out_shape=(
-            jax.ShapeDtypeStruct((HALF, count * SPAN), BF16),
-            jax.ShapeDtypeStruct((HALF, count * SPAN), F32),
-            jax.ShapeDtypeStruct((2 * HALF, WIDTH) if at is not None else (8, 128), BF16),
-        ),
-        in_specs=[pl.BlockSpec(memory_space=pltpu.SMEM)] + vmem(1 + count),
-        out_specs=tuple(vmem(3)),
+    else:
+        send_refs, rows_ref = rest, packed_ref
+    span = slice(first, first + SPAN)
+    width = 2 * SPAN // len(send_refs)
+    for i, weight_ref in enumerate((gate_ref, up_ref)):
+        product = dot(rows_ref[...], weight_ref[:, span])
+        sent = product[:HALF].astype(BF16)
+        for j in range(SPAN // width):
+            send_refs[i * SPAN // width + j][...] = sent[:, j * width : (j + 1) * width]
+        keep_ref[:, i * SPAN : (i + 1) * SPAN] = product[HALF:]
+
+
+def partial_sums(name, core, packed, at, gate, up, first, pieces):
+    shapes = (jax.ShapeDtypeStruct((HALF, 2 * SPAN), F32),)
+    shapes += (jax.ShapeDtypeStruct((HALF, 2 * SPAN // pieces), BF16),) * pieces
+    if at is not None:
+        shapes += (jax.ShapeDtypeStruct((2 * HALF, WIDTH), BF16),)
+    return pl.pallas_call(
+        lambda *refs: partial_kernel(first, at, *refs),
+        out_shape=shapes,
+        in_specs=[pl.BlockSpec(memory_space=pltpu.SMEM)] + vmem(3),
+        out_specs=tuple(vmem(len(shapes))),
         compiler_params=LIMITED,
         cost_estimate=cost(1e6, 1e4),
         name=name,
-    )(core, packed, *weights)
+    )(core, packed, gate, up)
 
 
 def grad_kernel(core_ref, packed_ref, weight_ref, send_ref, keep_ref, rows_ref):
@@ -248,9 +247,12 @@
     return out, back
 
 
-def spread_first_kernel(own_ref, peer_ref, gate_ref, up_ref, down_ref, out_ref, back_ref, rows_ref):
-    rows_ref[:HALF] = own_ref[...]
-    rows_ref[HALF:] = peer_ref[...]
+def spread_first_kernel(*refs):
+    own_refs, peer_refs = refs[:3], refs[3:6]
+    gate_ref, up_ref, down_ref, out_ref, back_ref, rows_ref = refs[6:]
+    for i in range(3):
+        rows_ref[:HALF, i * SPAN : (i + 1) * SPAN] = own_refs[i][...]
+        rows_ref[HALF:, i * SPAN : (i + 1) * SPAN] = peer_refs[i][...]
     for g in range(2):
         cols = slice(g * HALF_WIDTH, (g + 1) * HALF_WIDTH)
         out_ref[:, cols], back_ref[:, cols] = block_products(
@@ -265,13 +267,13 @@
             jax.ShapeDtypeStruct((2 * HALF, WIDTH), F32),
             jax.ShapeDtypeStruct((2 * HALF, WIDTH), F32),
         ),
-        in_specs=vmem(5),
+        in_specs=vmem(9),
         out_specs=tuple(vmem(2)),
         scratch_shapes=[pltpu.VMEM((2 * HALF, BLOCK), BF16)],
         compiler_params=LIMITED,
         cost_estimate=cost(1e6, 1e4),
         name="spread_a",
-    )(own, peer, gate, up, down)
+    )(*own, *peer, gate, up, down)
 
 
 def spread_last_kernel(core_ref, own_ref, peer_ref, gate_ref, up_ref, down_ref, out_sum, back_sum, packed_ref, rows_ref):
@@ -324,25 +326,30 @@
     )(core, own, peer, gate, up, down, out_sum, back_sum)
 
 
-def add_kernel(keep_ref, recv_ref, total_ref, send_ref):
-    total = keep_ref[...] + recv_ref[...].astype(F32)
-    total_ref[...] = total
-    send_ref[...] = total.astype(BF16)
-
-
-def add_halves(name, keep, recv):
+def add_kernel(keep_ref, *refs):
+    recv_refs, (total_ref, send_ref) = refs[:-2], refs[-2:]
+    at = 0
+    for recv_ref in recv_refs:
+        cols = slice(at, at + recv_ref.shape[1])
+        total = keep_ref[:, cols] + recv_ref[...].astype(F32)
+        total_ref[:, cols] = total
+        send_ref[:, cols] = total.astype(BF16)
+        at += recv_ref.shape[1]
+
+
+def add_halves(name, keep, *recv):
     return pl.pallas_call(
         add_kernel,
         out_shape=(
             jax.ShapeDtypeStruct(keep.shape, F32),
             jax.ShapeDtypeStruct(keep.shape, BF16),
         ),
-        in_specs=vmem(2),
+        in_specs=vmem(1 + len(recv)),
         out_specs=tuple(vmem(2)),
         compiler_params=LIMITED,
         cost_estimate=cost(1e6, 1e4),
         name=name,
-    )(keep, recv)
+    )(keep, *recv)
 
 
 def block_kernel(first, total_ref, recv_ref, grad_total_ref, grad_recv_ref, *rest):
@@ -354,26 +361,31 @@
     hidden = gate * sigma * up
     inner = jnp.sum(hidden * grad, axis=1, keepdims=True)
     if first == 0:
-        out_ref, inner_ref = rest
+        *parts, inner_ref = rest
         inner_ref[...] = jnp.broadcast_to(inner, (HALF, 128))
     else:
         inner_ref, out_ref = rest
+        parts = [out_ref.at[:, i * SPAN : (i + 1) * SPAN] for i in range(3)]
         high, low = halves_of(inner + inner_ref[:, :1])
         lane = iota((HALF, 128), 1)
         both = jnp.where(lane == 0, high.astype(F32), jnp.where(lane == 1, low.astype(F32), 0.0))
         out_ref[:, BLOCK:] = both.astype(BF16)
-    out_ref[:, :SPAN] = hidden.astype(BF16)
-    out_ref[:, SPAN : 2 * SPAN] = (grad * up * sigma * (1.0 + gate * (1.0 - sigma))).astype(BF16)
-    out_ref[:, 2 * SPAN : BLOCK] = (grad * gate * sigma).astype(BF16)
+    parts[0][...] = hidden.astype(BF16)
+    parts[1][...] = (grad * up * sigma * (1.0 + gate * (1.0 - sigma))).astype(BF16)
+    parts[2][...] = (grad * gate * sigma).astype(BF16)
 
 
 def block_of(name, first, total, recv, grad_total, grad_recv, *inner):
-    block = jax.ShapeDtypeStruct((HALF, BLOCK + (128 if inner else 0)), BF16)
+    if inner:
+        shapes = jax.ShapeDtypeStruct((HALF, BLOCK + 128), BF16)
+    else:
+        shapes = (jax.ShapeDtypeStruct((HALF, SPAN), BF16),) * 3
+        shapes += (jax.ShapeDtypeStruct((HALF, 128), F32),)
     return pl.pallas_call(
         lambda *refs: block_kernel(first, *refs),
-        out_shape=block if inner else (block, jax.ShapeDtypeStruct((HALF, 128), F32)),
+        out_shape=shapes,
         in_specs=vmem(4 + len(inner)),
-        out_specs=vmem(1)[0] if inner else tuple(vmem(2)),
+        out_specs=vmem(1)[0] if inner else tuple(vmem(4)),
         compiler_params=LIMITED,
         cost_estimate=cost(1e6, 1e4),
         name=name,
@@ -452,27 +464,28 @@
     ids, keep, affinity_t = expert_ids.T, keep_flags.T, affinity.T
     w_gate, w_up, w_down = w_gate[0], w_up[0], w_down[0]
 
-    rows = exchange(send_rows(ids, keep, affinity_t, tokens, cotangent))
+    payload = send_rows(ids, keep, affinity_t, tokens, cotangent)
+    payload, core = lax.optimization_barrier((payload, core))
+    rows = exchange(payload)
 
     send_g, own_g = grad_sums(core, rows, w_down)
     total_g, send_g = add_halves("add_g", own_g, swap(send_g, 1))
+    rows, send_g = lax.optimization_barrier((rows, send_g))
     recv_g = swap(send_g, 2)
-    gate_up = (w_gate, w_up)
-    send_a, own_a, unpacked = partial_sums("pre_a", core, rows, 0, gate_up, (0, 0), False)
-    total_a, send_a = add_halves("add_a", own_a, swap(send_a, 1))
+    own_a, *sends, unpacked = partial_sums("pre_a", core, rows, 0, w_gate, w_up, 0, 4)
+    total_a, send_a = add_halves("add_a", own_a, *[swap(part, 1) for part in sends])
+    own_b, *sends = partial_sums("pre_b", core, unpacked, None, w_gate, w_up, SPAN, 2)
+    total_b, send_b = add_halves("add_b", own_b, *[swap(part, 1) for part in sends])
+    send_b, recv_g = lax.optimization_barrier((send_b, recv_g))
     recv_a = swap(send_a, 2)
-    unpacked, send_g = lax.optimization_barrier((unpacked, send_g))
-    send_b, own_b, unused = partial_sums("pre_b", core, unpacked, None, gate_up, (SPAN, SPAN), False)
-    total_b, send_b = add_halves("add_b", own_b, swap(send_b, 1))
     recv_b = swap(send_b, 2)
 
-    block_a, inner = block_of("block_a", 0, total_a, recv_a, total_g, recv_g)
-    peer_a = swap(block_a, 1)
+    *block_a, inner = block_of("block_a", 0, total_a, recv_a, total_g, recv_g)
+    peer_a = [swap(part, 1) for part in block_a]
+    out_sum, back_sum = spread_first(block_a, peer_a, w_gate, w_up, w_down)
+    recv_b, out_sum, back_sum = lax.optimization_barrier((recv_b, out_sum, back_sum))
     block_b = block_of("block_b", SPAN, total_b, recv_b, total_g, recv_g, inner)
-    peer_b = swap(block_b, 1)
-    block_a, block_b = lax.optimization_barrier((block_a, block_b))
-    out_sum, back_sum = spread_first(block_a, peer_a, w_gate, w_up, w_down)
-    payload = spread_last(core, block_b, peer_b, w_gate, w_up, w_down, out_sum, back_sum)
+    payload = spread_last(core, block_b, swap(block_b, 1), w_gate, w_up, w_down, out_sum, back_sum)
     rows = exchange(payload)
     mixed, token_grad, affinity_grad = combine(ids, keep, affinity_t, rows)
     return mixed, token_grad, affinity_grad.T

time: 134 us -> 123 us (0.918)
  blocking collectives: 38.9 us -> 81.8 us
  waiting for transfers between devices: 55.7 us -> 16.7 us
  starting transfers between devices: 15.2 us -> 5.44 us
  local copies, waits for them, and re-layouts: 4.53 us -> 0.04 us
    all_to_all x1 -> x2, blocking collectives: 38.9 us -> 81.8 us  [exchange(): lax.all_to_all(packed, 'node', split_axis=0, concat_axis=0, tiled=True)]
    all_to_all x1 -> x0, waiting for transfers between devices: 33.4 us -> none  [exchange(): lax.all_to_all(packed, 'node', split_axis=0, concat_axis=0, tiled=True)]
    all_to_all x1 -> x0, starting transfers between devices: 10.9 us -> none  [exchange(): lax.all_to_all(packed, 'node', split_axis=0, concat_axis=0, tiled=True)]
    ppermute x8 -> x14, waiting for transfers between devices: 22.4 us -> 16.7 us  [swap(): return lax.ppermute(values, 'local', [(i, i ^ distance) for i in range(4)])]
    unnamed x16 -> x12, local copies, waits for them, and re-layouts: 4.53 us -> 0.04 us
    ppermute x8 -> x14, starting transfers between devices: 4.27 us -> 5.44 us  [swap(): return lax.ppermute(values, 'local', [(i, i ^ distance) for i in range(4)])]
  transfers between devices with their start and end apart: 9 -> 14, of which waited for: 5 -> 14; matrix products, arithmetic and copies ran while one was open for 0% -> 0% of each run, Pallas kernels for 4% -> 5%
where the time goes in v3:
time: 123 us
  blocking collectives  81.8 us (67%)
  Pallas kernels  18.4 us (15%)
  waiting for transfers between devices  16.7 us (14%)
  starting transfers between devices  5.44 us (4%)
    all_to_all x2, blocking collectives, exchange(): lax.all_to_all(packed, 'node', split_axis=0, concat_axis=0, tiled=True)  81.8 us
    ppermute x14, waiting for transfers between devices, swap(): return lax.ppermute(values, 'local', [(i, i ^ distance) for i in range(4)])  16.7 us
    ppermute x14, starting transfers between devices, swap(): return lax.ppermute(values, 'local', [(i, i ^ distance) for i in range(4)])  5.44 us
    pallas_call x1, Pallas kernels, send_rows(): pl.pallas_call(send_kernel, out_shape=jax.ShapeDtypeStruct((ROWS, PAYLOAD...  4.64 us
    pallas_call x1, Pallas kernels, spread_last(): pl.pallas_call(spread_last_kernel, out_shape=jax.ShapeDtypeStruct((ROWS,...  3.34 us
    pallas_call x2, Pallas kernels, partial_sums(): pl.pallas_call(lambda *refs: partial_kernel(first, at, *refs), out_shape=...  2.86 us
    pallas_call x1, Pallas kernels, combine(): pl.pallas_call(combine_kernel, out_shape=(jax.ShapeDtypeStruct((TOK, WIDT...  2.83 us
  transfers between devices with their start and end apart: 14, of which 14 were waited for; matrix products, arithmetic and copies ran while one was open for 0% of the time, Pallas kernels for 5%

profile of v3, /device:TPU:0, one launch (start us, length us, event | category | flops | bytes accessed | tf_op | source)
XLA Modules:
  0.0 123.1 jit_solution(937288961029355022)
XLA Ops:
  0.6 4.6 %send_rows.1 = bf16[256,4608]{1,0:T(8,128)(2,1)} custom-call(s32[8,256]{1,0:T(8,128)} %bitcast.27, s32[8,256]{1,0:T(8,128)} %bitcast.29, f32[8,256]{1,0:T(8,128)} %bitcast.31, bf16[256,1792]{1,0:T(8,128)(2,1)} %token_ref.1, bf16[256,1792]{1,0:T(8,128)(2,1)} %cot_ref.1), custom_call_target="tpu_custom_call" | custom-call | flops 939524096 | bytes 5505024 | tf_op jit(solution)/shard_map/send_rows/pallas_call | solution.py:152
  5.3 0.0 copy-start.2
  5.3 0.0 copy-start.1
  5.3 44.5 %all_to_all.22 = bf16[32,8,4608]{2,1,0:T(8,128)(2,1)S(1)} all-to-all(bf16[32,8,4608]{2,1,0:T(8,128)(2,1)} %bitcast.33), channel_id=1, replica_groups=mesh['node'=32,'local'=4] {'node'}, dimensions={0} | all-to-all | bytes 4718592 | tf_op jit(solution)/shard_map/all_to_all | solution.py:455
  49.9 0.0 copy-done.2
  49.9 0.0 copy-start
  49.9 1.5 %grad.1 = (bf16[160,1024]{1,0:T(8,128)(2,1)S(1)}, f32[160,1024]{1,0:T(8,128)S(1)}) custom-call(s32[1]{0:T(128)} %bitcast.3.core_ref.refs_0_, bf16[256,4608]{1,0:T(8,128)(2,1)S(1)} %bitcast.23, bf16[1024,1792]{1,0:T(8,128)(2,1)S(1)} %bitcast.20), custom_call_target="tpu_custom_call" | custom-call | flops 1000000 | bytes 10000 | tf_op jit(solution)/shard_map/grad/pallas_call | solution.py:227
  51.4 0.1 collective-permute-start
  51.5 1.6 %collective-permute-done.refs_0_ = bf16[160,1024]{1,0:T(8,128)(2,1)S(1)} collective-permute-done((bf16[160,1024]{1,0:T(8,128)(2,1)S(1)}, bf16[160,1024]{1,0:T(8,128)(2,1)S(1)}, u32[]{:S(2)}, u32[]{:S(2)}) %collective-permute-start) | collective-permute-done | bytes 327712 | tf_op jit(solution)/shard_map/ppermute | solution.py:459
  53.1 0.1 add_g.1
  53.2 0.7 collective-permute-start.3
  53.9 0.0 copy-done.1
  53.9 0.0 copy-done
  53.9 1.5 %pre_a.1 = (f32[160,1024]{1,0:T(8,128)S(1)}, bf16[160,256]{1,0:T(8,128)(2,1)S(1)}, bf16[160,256]{1,0:T(8,128)(2,1)S(1)}, bf16[160,256]{1,0:T(8,128)(2,1)S(1)}, b...) custom-call(s32[1]{0:T(128)} %bitcast.3.core_ref.refs_0_, bf16[256,4608]{1,0:T(8,128)(2,1)S(1)} %bitcast.24, ...), custom_call_target="tpu_custom_call" | custom-call | flops 1000000 | bytes 10000 | tf_op jit(solution)/shard_map/pre_a/pallas_call | solution.py:206
  55.4 0.1 collective-permute-start.5
  55.5 0.5 collective-permute-start.6
  56.0 0.1 collective-permute-start.7
  56.1 0.4 collective-permute-start.8
  56.5 0.3 collective-permute-done.5.refs_0_
  56.8 0.2 collective-permute-done.6.refs_1_
  56.9 0.4 collective-permute-done.7.refs_2_
  57.3 0.2 collective-permute-done.8.refs_3_
  57.4 0.1 add_a.1
  57.5 1.5 %collective-permute-start.9 = (bf16[160,1024]{1,0:T(8,128)(2,1)S(1)}, bf16[160,1024]{1,0:T(8,128)(2,1)S(1)}, u32[]{:S(2)}, u32[]{:S(2)}) collective-permute-start(bf16[160,1024]{1,0:T(8,128)(2,1)S(1)} %get-tuple-element.58), channel_id=1, source_target_pairs={{0,2},{1,3},{2,0},{3,1},{4,6},{5,7},{6,4},{7,5},{8,10},{9,11},{10,... | collective-permute-start | bytes 983048 | tf_op jit(solution)/shard_map/ppermute | solution.py:459
  59.0 1.4 %pre_b.1 = (f32[160,1024]{1,0:T(8,128)S(1)}, bf16[160,512]{1,0:T(8,128)(2,1)S(1)}, bf16[160,512]{1,0:T(8,128)(2,1)S(1)}) custom-call(s32[1]{0:T(128)} %bitcast.3.core_ref.refs_0_, bf16[320,1792]{1,0:T(8,128)(2,1)S(1)} %get-tuple-element.44.refs_1_, bf16[1792,1024]{1,0:T(8,128)(2,1)S(1)} %bitcast.13, bf16[1792,1024]{1,0:T(8,128)(2,1)S(1)} %bitcast.17), custom_call_target="tpu_custom_call" | custom-call | flops 1000000 | bytes 10000 | tf_op jit(solution)/shard_map/pre_b/pallas_call | solution.py:206
  60.4 0.2 collective-permute-start.1
  60.5 0.4 collective-permute-start.2
  61.0 0.9 collective-permute-done.1.refs_0_
  61.8 0.2 collective-permute-done.2.refs_1_
  62.1 0.1 add_b.1
  62.2 1.6 %collective-permute-done.3.refs_3_ = bf16[160,1024]{1,0:T(8,128)(2,1)S(1)} collective-permute-done((bf16[160,1024]{1,0:T(8,128)(2,1)S(1)}, bf16[160,1024]{1,0:T(8,128)(2,1)S(1)}, u32[]{:S(2)}, u32[]{:S(2)}) %collective-permute-start.3) | collective-permute-done | bytes 327712 | tf_op jit(solution)/shard_map/ppermute | solution.py:459
  63.8 0.6 collective-permute-start.4
  64.4 6.4 %collective-permute-done.9.refs_1_ = bf16[160,1024]{1,0:T(8,128)(2,1)S(1)} collective-permute-done((bf16[160,1024]{1,0:T(8,128)(2,1)S(1)}, bf16[160,1024]{1,0:T(8,128)(2,1)S(1)}, u32[]{:S(2)}, u32[]{:S(2)}) %collective-permute-start.9) | collective-permute-done | bytes 327712 | tf_op jit(solution)/shard_map/ppermute | solution.py:459
  70.8 0.3 block_a.1
  71.1 0.0 collective-permute-start.10
  71.2 0.5 collective-permute-start.11
  71.7 0.1 collective-permute-start.12
  71.8 0.8 collective-permute-done.10.refs_3_
  72.6 0.2 collective-permute-done.11.refs_4_
  72.8 0.3 collective-permute-done.12.refs_5_
  73.1 2.2 %spread_a.1 = (f32[320,1792]{1,0:T(8,128)S(1)}, f32[320,1792]{1,0:T(8,128)S(1)}) custom-call(bf16[160,512]{1,0:T(8,128)(2,1)S(1)} %get-tuple-element.61.refs_0_, bf16[160,512]{1,0:T(8,128)(2,1)S(1)} %get-tuple-element.62.refs_1_, bf16[160,512]{1,0:T(8,128)(2,1)S(1)} %get-tuple-element.63.refs_2_, bf16[160,512]{1,0:T(8,128)(2,1)S(1)} %collective-permute-done.10.refs_3_, ...), custom_call_target="tpu_custom_call" | custom-call | flops 1000000 | bytes 10000 | tf_op jit(solution)/shard_map/spread_a/pallas_call | solution.py:264
  75.3 1.8 %collective-permute-done.4.refs_1_ = bf16[160,1024]{1,0:T(8,128)(2,1)S(1)} collective-permute-done((bf16[160,1024]{1,0:T(8,128)(2,1)S(1)}, bf16[160,1024]{1,0:T(8,128)(2,1)S(1)}, u32[]{:S(2)}, u32[]{:S(2)}) %collective-permute-start.4) | collective-permute-done | bytes 327712 | tf_op jit(solution)/shard_map/ppermute | solution.py:459
  77.1 0.4 block_b.1.own_ref
  77.4 0.2 collective-permute-start.13
  77.7 1.9 %collective-permute-done.13.peer_ref = bf16[160,1664]{1,0:T(8,128)(2,1)S(1)} collective-permute-done((bf16[160,1664]{1,0:T(8,128)(2,1)S(1)}, bf16[160,1664]{1,0:T(8,128)(2,1)S(1)}, u32[]{:S(2)}, u32[]{:S(2)}) %collective-permute-start.13) | collective-permute-done | bytes 532512 | tf_op jit(solution)/shard_map/ppermute | solution.py:459
  79.6 3.3 %spread_b.1 = bf16[256,4608]{1,0:T(8,128)(2,1)S(1)} custom-call(s32[1]{0:T(128)} %bitcast.3.core_ref.refs_0_, bf16[160,1664]{1,0:T(8,128)(2,1)S(1)} %block_b.1.own_ref, bf16[160,1664]{1,0:T(8,128)(2,1)S(1)} %collective-permute-done.13.peer_ref, bf16[1792,1024]{1,0:T(8,128)(2,1)S(1)} %bitcast.15, bf16[1792,1024]{1,0:T(8,128)(2,1)S(1)} %bitcast.19, ...), custom_call_target="tpu_custom_call" | custom-call | flops 1000000 | bytes 10000 | tf_op jit(solution)/shard_map/spread_b/pallas_call | solution.py:317
  82.9 0.0 copy-start.3
  83.0 0.0 copy-start.4
  83.0 0.0 copy-start.5
  83.0 37.3 %all_to_all.23 = bf16[32,8,4608]{2,1,0:T(8,128)(2,1)S(1)} all-to-all(bf16[32,8,4608]{2,1,0:T(8,128)(2,1)S(1)} %bitcast.25), channel_id=1, replica_groups=mesh['node'=32,'local'=4] {'node'}, dimensions={0} | all-to-all | bytes 4718592 | tf_op jit(solution)/shard_map/all_to_all | solution.py:455
  120.3 0.0 copy-done.3
  120.3 0.0 copy-done.4
  120.3 0.0 copy-done.5
  120.3 2.8 %combine.1 = (bf16[256,1792]{1,0:T(8,128)(2,1)}, bf16[256,1792]{1,0:T(8,128)(2,1)}, f32[8,256]{1,0:T(8,128)}) custom-call(s32[8,256]{1,0:T(8,128)S(1)} %bitcast.28, s32[8,256]{1,0:T(8,128)S(1)} %bitcast.30, f32[8,256]{1,0:T(8,128)S(1)} %bitcast.32, bf16[256,4608]{1,0:T(8,128)(2,1)S(1)} %bitcast.26), custom_call_target="tpu_custom_call" | custom-call | flops 939524096 | bytes 3670016 | tf_op jit(solution)/shard_map/combine/pallas_call | solution.py:438
Async XLA Ops:
  5.3 44.6 %copy-start.2 = (bf16[1,1024,1792]{2,1,0:T(8,128)(2,1)S(1)}, bf16[1,1024,1792]{2,1,0:T(8,128)(2,1)}, u32[]{:S(2)}) copy-start(bf16[1,1024,1792]{2,1,0:T(8,128)(2,1)} %param.14) | copy-start | bytes 11010052
  5.3 48.6 %copy-start.1 = (bf16[1,1792,1024]{2,1,0:T(8,128)(2,1)S(1)}, bf16[1,1792,1024]{2,1,0:T(8,128)(2,1)}, u32[]{:S(2)}) copy-start(bf16[1,1792,1024]{2,1,0:T(8,128)(2,1)} %param.13) | copy-start | bytes 11010052
  49.9 4.0 %copy-start = (bf16[1,1792,1024]{2,1,0:T(8,128)(2,1)S(1)}, bf16[1,1792,1024]{2,1,0:T(8,128)(2,1)}, u32[]{:S(2)}) copy-start(bf16[1,1792,1024]{2,1,0:T(8,128)(2,1)} %param.12) | copy-start | bytes 11010052
  51.4 1.7 %collective-permute-start = (bf16[160,1024]{1,0:T(8,128)(2,1)S(1)}, bf16[160,1024]{1,0:T(8,128)(2,1)S(1)}, u32[]{:S(2)}, u32[]{:S(2)}) collective-permute-start(bf16[160,1024]{1,0:T(8,128)(2,1)S(1)} %get-tuple-element.41), channel_id=1, source_target_pairs={{0,1},{1,0},{2,3},{3,2},{4,5},{5,4},{6,7},{7,6},{8,9},{9,8},{10,11... | collective-permute-start | bytes 983048 | tf_op jit(solution)/shard_map/ppermute | solution.py:459
  53.2 10.6 %collective-permute-start.3 = (bf16[160,1024]{1,0:T(8,128)(2,1)S(1)}, bf16[160,1024]{1,0:T(8,128)(2,1)S(1)}, u32[]{:S(2)}, u32[]{:S(2)}) collective-permute-start(bf16[160,1024]{1,0:T(8,128)(2,1)S(1)} %get-tuple-element.50), channel_id=1, source_target_pairs={{0,2},{1,3},{2,0},{3,1},{4,6},{5,7},{6,4},{7,5},{8,10},{9,11},{10,... | collective-permute-start | bytes 983048 | tf_op jit(solution)/shard_map/ppermute | solution.py:459
  55.4 1.4 %collective-permute-start.5 = (bf16[160,256]{1,0:T(8,128)(2,1)S(1)}, bf16[160,256]{1,0:T(8,128)(2,1)S(1)}, u32[]{:S(2)}, u32[]{:S(2)}) collective-permute-start(bf16[160,256]{1,0:T(8,128)(2,1)S(1)} %get-tuple-element.53), channel_id=1, source_target_pairs={{0,1},{1,0},{2,3},{3,2},{4,5},{5,4},{6,7},{7,6},{8,9},{9,8},{10,11... | collective-permute-start | bytes 245768 | tf_op jit(solution)/shard_map/ppermute | solution.py:459
  55.5 1.4 %collective-permute-start.6 = (bf16[160,256]{1,0:T(8,128)(2,1)S(1)}, bf16[160,256]{1,0:T(8,128)(2,1)S(1)}, u32[]{:S(2)}, u32[]{:S(2)}) collective-permute-start(bf16[160,256]{1,0:T(8,128)(2,1)S(1)} %get-tuple-element.54), channel_id=1, source_target_pairs={{0,1},{1,0},{2,3},{3,2},{4,5},{5,4},{6,7},{7,6},{8,9},{9,8},{10,11... | collective-permute-start | bytes 245768 | tf_op jit(solution)/shard_map/ppermute | solution.py:459
  56.0 1.3 %collective-permute-start.7 = (bf16[160,256]{1,0:T(8,128)(2,1)S(1)}, bf16[160,256]{1,0:T(8,128)(2,1)S(1)}, u32[]{:S(2)}, u32[]{:S(2)}) collective-permute-start(bf16[160,256]{1,0:T(8,128)(2,1)S(1)} %get-tuple-element.55), channel_id=1, source_target_pairs={{0,1},{1,0},{2,3},{3,2},{4,5},{5,4},{6,7},{7,6},{8,9},{9,8},{10,11... | collective-permute-start | bytes 245768 | tf_op jit(solution)/shard_map/ppermute | solution.py:459
  56.1 1.3 %collective-permute-start.8 = (bf16[160,256]{1,0:T(8,128)(2,1)S(1)}, bf16[160,256]{1,0:T(8,128)(2,1)S(1)}, u32[]{:S(2)}, u32[]{:S(2)}) collective-permute-start(bf16[160,256]{1,0:T(8,128)(2,1)S(1)} %get-tuple-element.56), channel_id=1, source_target_pairs={{0,1},{1,0},{2,3},{3,2},{4,5},{5,4},{6,7},{7,6},{8,9},{9,8},{10,11... | collective-permute-start | bytes 245768 | tf_op jit(solution)/shard_map/ppermute | solution.py:459
  57.5 13.3 %collective-permute-start.9 = (bf16[160,1024]{1,0:T(8,128)(2,1)S(1)}, bf16[160,1024]{1,0:T(8,128)(2,1)S(1)}, u32[]{:S(2)}, u32[]{:S(2)}) collective-permute-start(bf16[160,1024]{1,0:T(8,128)(2,1)S(1)} %get-tuple-element.58), channel_id=1, source_target_pairs={{0,2},{1,3},{2,0},{3,1},{4,6},{5,7},{6,4},{7,5},{8,10},{9,11},{10,... | collective-permute-start | bytes 983048 | tf_op jit(solution)/shard_map/ppermute | solution.py:459
  60.4 1.5 %collective-permute-start.1 = (bf16[160,512]{1,0:T(8,128)(2,1)S(1)}, bf16[160,512]{1,0:T(8,128)(2,1)S(1)}, u32[]{:S(2)}, u32[]{:S(2)}) collective-permute-start(bf16[160,512]{1,0:T(8,128)(2,1)S(1)} %get-tuple-element.46), channel_id=1, source_target_pairs={{0,1},{1,0},{2,3},{3,2},{4,5},{5,4},{6,7},{7,6},{8,9},{9,8},{10,11... | collective-permute-start | bytes 491528 | tf_op jit(solution)/shard_map/ppermute | solution.py:459
  60.5 1.6 %collective-permute-start.2 = (bf16[160,512]{1,0:T(8,128)(2,1)S(1)}, bf16[160,512]{1,0:T(8,128)(2,1)S(1)}, u32[]{:S(2)}, u32[]{:S(2)}) collective-permute-start(bf16[160,512]{1,0:T(8,128)(2,1)S(1)} %get-tuple-element.47), channel_id=1, source_target_pairs={{0,1},{1,0},{2,3},{3,2},{4,5},{5,4},{6,7},{7,6},{8,9},{9,8},{10,11... | collective-permute-start | bytes 491528 | tf_op jit(solution)/shard_map/ppermute | solution.py:459
  63.8 13.2 %collective-permute-start.4 = (bf16[160,1024]{1,0:T(8,128)(2,1)S(1)}, bf16[160,1024]{1,0:T(8,128)(2,1)S(1)}, u32[]{:S(2)}, u32[]{:S(2)}) collective-permute-start(bf16[160,1024]{1,0:T(8,128)(2,1)S(1)} %get-tuple-element.51), channel_id=1, source_target_pairs={{0,2},{1,3},{2,0},{3,1},{4,6},{5,7},{6,4},{7,5},{8,10},{9,11},{10,... | collective-permute-start | bytes 983048 | tf_op jit(solution)/shard_map/ppermute | solution.py:459
  71.1 1.4 %collective-permute-start.10 = (bf16[160,512]{1,0:T(8,128)(2,1)S(1)}, bf16[160,512]{1,0:T(8,128)(2,1)S(1)}, u32[]{:S(2)}, u32[]{:S(2)}) collective-permute-start(bf16[160,512]{1,0:T(8,128)(2,1)S(1)} %get-tuple-element.61.refs_0_), channel_id=1, source_target_pairs={{0,1},{1,0},{2,3},{3,2},{4,5},{5,4},{6,7},{7,6},{8,9},{9,8},{10,11... | collective-permute-start | bytes 491528 | tf_op jit(solution)/shard_map/ppermute | solution.py:459
  71.2 1.6 %collective-permute-start.11 = (bf16[160,512]{1,0:T(8,128)(2,1)S(1)}, bf16[160,512]{1,0:T(8,128)(2,1)S(1)}, u32[]{:S(2)}, u32[]{:S(2)}) collective-permute-start(bf16[160,512]{1,0:T(8,128)(2,1)S(1)} %get-tuple-element.62.refs_1_), channel_id=1, source_target_pairs={{0,1},{1,0},{2,3},{3,2},{4,5},{5,4},{6,7},{7,6},{8,9},{9,8},{10,11... | collective-permute-start | bytes 491528 | tf_op jit(solution)/shard_map/ppermute | solution.py:459
  71.7 1.4 %collective-permute-start.12 = (bf16[160,512]{1,0:T(8,128)(2,1)S(1)}, bf16[160,512]{1,0:T(8,128)(2,1)S(1)}, u32[]{:S(2)}, u32[]{:S(2)}) collective-permute-start(bf16[160,512]{1,0:T(8,128)(2,1)S(1)} %get-tuple-element.63.refs_2_), channel_id=1, source_target_pairs={{0,1},{1,0},{2,3},{3,2},{4,5},{5,4},{6,7},{7,6},{8,9},{9,8},{10,11... | collective-permute-start | bytes 491528 | tf_op jit(solution)/shard_map/ppermute | solution.py:459
  77.4 2.2 %collective-permute-start.13 = (bf16[160,1664]{1,0:T(8,128)(2,1)S(1)}, bf16[160,1664]{1,0:T(8,128)(2,1)S(1)}, u32[]{:S(2)}, u32[]{:S(2)}) collective-permute-start(bf16[160,1664]{1,0:T(8,128)(2,1)S(1)} %block_b.1.own_ref), channel_id=1, source_target_pairs={{0,1},{1,0},{2,3},{3,2},{4,5},{5,4},{6,7},{7,6},{8,9},{9,8},{10,11... | collective-permute-start | bytes 1597448 | tf_op jit(solution)/shard_map/ppermute | solution.py:459
  82.9 37.3 %copy-start.3 = (s32[256,8]{0,1:T(8,128)S(1)}, s32[256,8]{0,1:T(8,128)}, u32[]{:S(2)}) copy-start(s32[256,8]{0,1:T(8,128)} %param.9) | copy-start | bytes 24580
  83.0 37.3 %copy-start.4 = (s32[256,8]{0,1:T(8,128)S(1)}, s32[256,8]{0,1:T(8,128)}, u32[]{:S(2)}) copy-start(s32[256,8]{0,1:T(8,128)} %param.10) | copy-start | bytes 24580
  83.0 37.3 %copy-start.5 = (f32[256,8]{0,1:T(8,128)S(1)}, f32[256,8]{0,1:T(8,128)}, u32[]{:S(2)}) copy-start(f32[256,8]{0,1:T(8,128)} %param.11) | copy-start | bytes 24580

commit v4 on v3

--- a/solution.py
+++ b/solution.py
@@ -17,6 +17,7 @@
 PACKED = WIDTH + TAIL
 PAYLOAD = 2 * PACKED
 HALF_WIDTH = WIDTH // 2
+SENT = 2 * WIDTH + HALF_WIDTH
 SPARE = WIDTH + 256
 BLOCK = 3 * 512
 ROWS = FLIGHT * MAIN
@@ -85,54 +86,53 @@
     return ROUTE_SCALE * affinity / jnp.sum(affinity, axis=0, keepdims=True)
 
 
-def send_kernel(ids_ref, keep_ref, affinity_ref, token_ref, cot_ref, out_ref, weight_ref, in_ref, packed_ref, in_sem, out_sem):
+def send_kernel(*refs):
+    route_refs, (token_ref, cot_ref, out_ref) = refs[:3], refs[3:6]
+    ids_ref, keep_ref, affinity_ref, weight_ref, in_ref, packed_ref, route_sem, in_sem, out_sem = refs[6:]
+    held = (ids_ref, keep_ref, affinity_ref)
+    route = [pltpu.make_async_copy(route_refs[i], held[i], route_sem.at[i]) for i in range(3)]
+    for copy in route:
+        copy.start()
+
     def load(i):
         source = (token_ref, cot_ref)[i // 2]
         cols = slice(i % 2 * HALF_WIDTH, (i % 2 + 1) * HALF_WIDTH)
         return pltpu.make_async_copy(source.at[:, cols], in_ref.at[i], in_sem.at[i])
 
     def store(i):
-        first = i // 3 * PACKED + i % 3 * HALF_WIDTH
-        last = first + (TAIL if i % 3 == 2 else HALF_WIDTH)
-        cols = slice(first, last)
+        cols = slice(i * HALF_WIDTH, (i + 1) * HALF_WIDTH)
         return pltpu.make_async_copy(packed_ref.at[:, cols], out_ref.at[:, cols], out_sem.at[i])
 
     for i in range(4):
         load(i).start()
+    for copy in route:
+        copy.wait()
     weight_ref[...] = weights_of(affinity_ref)
     marks, weights = expert_marks(ids_ref, keep_ref, weight_ref)
     main, tail = picks(slots_of(marks))
-    main_place, tail_place = as_bf16(main), as_bf16(tail)
-    piece_of_row = iota((ROWS, 128), 0) % MAIN // 2
-    scales = None
-    for array in range(2):
-        if array == 1:
-            high, low = halves_of(weights)
-            wide = dot(spread_matrix(), high) + dot(spread_matrix(), low)
-            scales = [
-                jnp.sum(jnp.where(mask, wide, 0.0), axis=1, keepdims=True) for mask in (main, tail)
-            ]
-        tails = [jnp.zeros((ROWS, 128), BF16)] * 4
-        for half in range(2):
-            load(2 * array + half).wait()
-            block = in_ref[2 * array + half]
-            first, second = dot(main_place, block), dot(tail_place, block)
-            if scales is not None:
-                first, second = first * scales[0], second * scales[1]
-            at = array * PACKED + half * HALF_WIDTH
-            packed_ref[:, at : at + HALF_WIDTH] = first.astype(BF16)
-            store(3 * array + half).start()
-            second = second.astype(BF16)
-            for m in range(7):
-                feature = 7 * half + m
-                tails[feature % 4] = jnp.where(
-                    piece_of_row == feature // 4, second[:, 128 * m : 128 * (m + 1)], tails[feature % 4]
-                )
-        at = array * PACKED + WIDTH
-        for m in range(4):
-            packed_ref[:, at + 128 * m : at + 128 * (m + 1)] = tails[m]
-        store(3 * array + 2).start()
-    for i in range(6):
+    place = jnp.concatenate([as_bf16(main), as_bf16(tail)], axis=0)
+    high, low = halves_of(weights)
+    wide = dot(spread_matrix(), high) + dot(spread_matrix(), low)
+    main_scale, tail_scale = [
+        jnp.sum(jnp.where(mask, wide, 0.0), axis=1, keepdims=True) for mask in (main, tail)
+    ]
+    sub = iota((ROWS, HALF_WIDTH), 0) % MAIN
+    tails = jnp.zeros((ROWS, HALF_WIDTH), BF16)
+    for i in range(4):
+        load(i).wait()
+    for i in range(4):
+        block = in_ref[i]
+        both = dot(place, block)
+        first, second = both[:ROWS], both[ROWS:]
+        if i >= 2:
+            first, second = first * main_scale, second * tail_scale
+        packed_ref[:, i * HALF_WIDTH : (i + 1) * HALF_WIDTH] = first.astype(BF16)
+        store(i).start()
+        here = sub // 2 == 2 * (i % 2) + i // 2
+        tails = jnp.where(here, second.astype(BF16), tails)
+    packed_ref[:, 2 * WIDTH :] = tails
+    store(4).start()
+    for i in range(5):
         store(i).wait()
 
 
@@ -151,15 +151,19 @@
 def send_rows(ids, keep, affinity, tokens, cotangent):
     return pl.pallas_call(
         send_kernel,
-        out_shape=jax.ShapeDtypeStruct((ROWS, PAYLOAD), BF16),
-        in_specs=vmem(3) + [pl.BlockSpec(memory_space=pl.ANY)] * 2,
+        out_shape=jax.ShapeDtypeStruct((ROWS, SENT), BF16),
+        in_specs=[pl.BlockSpec(memory_space=pl.ANY)] * 5,
         out_specs=pl.BlockSpec(memory_space=pl.ANY),
         scratch_shapes=[
+            pltpu.VMEM((TOP, TOK), jnp.int32),
+            pltpu.VMEM((TOP, TOK), jnp.int32),
+            pltpu.VMEM((TOP, TOK), F32),
             pltpu.VMEM((TOP, TOK), F32),
             pltpu.VMEM((4, TOK, HALF_WIDTH), BF16),
-            pltpu.VMEM((ROWS, PAYLOAD), BF16),
+            pltpu.VMEM((ROWS, SENT), BF16),
+            pltpu.SemaphoreType.DMA((3,)),
             pltpu.SemaphoreType.DMA((4,)),
-            pltpu.SemaphoreType.DMA((6,)),
+            pltpu.SemaphoreType.DMA((5,)),
         ],
         compiler_params=ROOMY,
         cost_estimate=cost(8 * ROWS * TOK * WIDTH, 2 * TOK * WIDTH * 6),
@@ -167,17 +171,16 @@
     )(ids, keep, affinity, tokens, cotangent)
 
 
-def unpack_half(packed_ref, at, half, out_ref, base):
+def unpack_half(packed_ref, array, half, out_ref, base):
     rows = pl.ds(pl.multiple_of(half * HALF_MAIN, HALF_MAIN), HALF_MAIN)
-    out_ref[base : base + HALF_MAIN, :] = packed_ref[rows, at : at + WIDTH]
-    tail = packed_ref[rows, at + WIDTH : at + PACKED]
+    out_ref[base : base + HALF_MAIN, :] = packed_ref[rows, array * WIDTH : (array + 1) * WIDTH]
+    tail = packed_ref[rows, 2 * WIDTH :]
     shape = (HALF - HALF_MAIN, HALF_MAIN)
     row, col = iota(shape, 0), iota(shape, 1)
-    for g in range(4):
-        same = (row // 2 == col // MAIN) & (col % MAIN == 2 * g + row % 2)
-        piece = dot(as_bf16(same), tail).astype(BF16)
-        width = min(TAIL, WIDTH - g * TAIL)
-        out_ref[base + HALF_MAIN : base + HALF, g * TAIL : g * TAIL + width] = piece[:, :width]
+    for h in range(2):
+        same = (row // 2 == col // MAIN) & (col % MAIN == 4 * h + 2 * array + row % 2)
+        cols = slice(h * HALF_WIDTH, (h + 1) * HALF_WIDTH)
+        out_ref[base + HALF_MAIN : base + HALF, cols] = dot(as_bf16(same), tail).astype(BF16)
 
 
 def partial_kernel(first, at, core_ref, packed_ref, gate_ref, up_ref, keep_ref, *rest):
@@ -216,8 +219,8 @@
 
 def grad_kernel(core_ref, packed_ref, weight_ref, send_ref, keep_ref, rows_ref):
     core = core_ref[0]
-    unpack_half(packed_ref, PACKED, 1 - core, rows_ref, 0)
-    unpack_half(packed_ref, PACKED, core, rows_ref, HALF)
+    unpack_half(packed_ref, 1, 1 - core, rows_ref, 0)
+    unpack_half(packed_ref, 1, core, rows_ref, HALF)
     product = dot(rows_ref[...], weight_ref[...], NT)
     send_ref[...] = product[:HALF].astype(BF16)
     keep_ref[...] = product[HALF:]
@@ -280,24 +283,32 @@
     core = core_ref[0]
     rows_ref[:HALF] = own_ref[:, :BLOCK]
     rows_ref[HALF:] = peer_ref[:, :BLOCK]
-    for at in (WIDTH, PACKED + WIDTH):
-        packed_ref[:, at : at + TAIL] = jnp.zeros((ROWS, TAIL), BF16)
-    shape = (HALF_MAIN, HALF - HALF_MAIN)
-    row, col = iota(shape, 0), iota(shape, 1)
+    halves = [
+        (base, pl.ds(pl.multiple_of(half * HALF_MAIN, HALF_MAIN), HALF_MAIN))
+        for base, half in ((0, core), (HALF, 1 - core))
+    ]
+    tails = {}
     for g in range(4):
         width = min(TAIL, WIDTH - g * TAIL)
         cols = slice(g * TAIL, g * TAIL + width)
         products = block_products(rows_ref, SPAN, gate_ref, up_ref, down_ref, cols)
-        place = as_bf16((row // MAIN == col // 2) & (row % MAIN == 2 * g + col % 2))
         for product, sum_ref, at in zip(products, (out_sum, back_sum), (0, PACKED)):
             product = (product + sum_ref[:, cols]).astype(BF16)
-            for base, half in ((0, core), (HALF, 1 - core)):
-                rows = pl.ds(pl.multiple_of(half * HALF_MAIN, HALF_MAIN), HALF_MAIN)
+            for base, rows in halves:
                 packed_ref[rows, at + g * TAIL : at + g * TAIL + width] = product[
                     base : base + HALF_MAIN
                 ]
-                tail = dot(place, product[base + HALF_MAIN : base + HALF]).astype(BF16)
-                packed_ref[rows, at + WIDTH : at + WIDTH + width] += tail
+                tail = product[base + HALF_MAIN : base + HALF]
+                if width < TAIL:
+                    tail = jnp.concatenate([tail, jnp.zeros((HALF - HALF_MAIN, TAIL - width), BF16)], axis=1)
+                tails[at, base, g] = tail
+    row, col = iota((HALF_MAIN, HALF_MAIN), 0), iota((HALF_MAIN, HALF_MAIN), 1)
+    piece, pair = col // (HALF - HALF_MAIN), col % (HALF - HALF_MAIN)
+    place = as_bf16((row // MAIN == pair // 2) & (row % MAIN == 2 * piece + pair % 2))
+    for at in (0, PACKED):
+        for base, rows in halves:
+            stacked = jnp.concatenate([tails[at, base, g] for g in range(4)], axis=0)
+            packed_ref[rows, at + WIDTH : at + PACKED] = dot(place, stacked).astype(BF16)
     for half_ref, half in ((own_ref, core), (peer_ref, 1 - core)):
         carried = half_ref[:, BLOCK:]
         total = jnp.zeros((HALF_MAIN, 128), F32)
@@ -392,29 +403,53 @@
     )(total, recv, grad_total, grad_recv, *inner)
 
 
-def combine_kernel(ids_ref, keep_ref, affinity_ref, packed_ref, mixed_ref, grad_ref, share_ref, weight_ref):
+def plan_kernel(ids_ref, keep_ref, affinity_ref, places_ref, slot_ref, weight_ref):
     weight_ref[...] = weights_of(affinity_ref)
     marks, weights = expert_marks(ids_ref, keep_ref, weight_ref)
     slot = slots_of(marks)
-    main, tail = picks(slot)
+    slot_ref[...] = slot
     wide = dot(spread_matrix(), weights.astype(BF16))
-    piece_of_row = iota((ROWS, TOK), 0) % MAIN // 2
-    main_place = as_bf16(main)
-    main_weight = jnp.where(main, wide, 0.0).astype(BF16)
-    for n in range(STEPS):
-        cols = slice(n * TILE, (n + 1) * TILE)
-        chosen = tail & (piece_of_row == n // 2)
-        first = WIDTH + n % 2 * TILE
-        total = dot(main_weight, packed_ref[:, cols], TN)
-        total += dot(
-            jnp.where(chosen, wide, 0.0).astype(BF16), packed_ref[:, first : first + TILE], TN
-        )
-        mixed_ref[:, cols] = total.astype(BF16)
-        total = dot(main_place, packed_ref[:, PACKED + n * TILE : PACKED + (n + 1) * TILE], TN)
-        first += PACKED
-        total += dot(as_bf16(chosen), packed_ref[:, first : first + TILE], TN)
-        grad_ref[:, cols] = total.astype(BF16)
-
+    for i, mask in enumerate(picks(slot)):
+        places_ref[i] = jnp.where(mask, wide, 0.0).T.astype(BF16)
+        places_ref[2 + i] = jnp.where(mask, 1.0, 0.0).T.astype(BF16)
+
+
+def plan(ids, keep, affinity):
+    return pl.pallas_call(
+        plan_kernel,
+        out_shape=(
+            jax.ShapeDtypeStruct((4, TOK, ROWS), BF16),
+            jax.ShapeDtypeStruct((FLIGHT, TOK), F32),
+            jax.ShapeDtypeStruct((TOP, TOK), F32),
+        ),
+        in_specs=vmem(3),
+        out_specs=tuple(vmem(3)),
+        compiler_params=LIMITED,
+        cost_estimate=cost(1e6, 1e4),
+        name="plan",
+    )(ids, keep, affinity)
+
+
+def combine_kernel(ids_ref, keep_ref, affinity_ref, places_ref, slot_ref, weight_ref, packed_ref, mixed_ref, grad_ref, share_ref, held_ref, sem):
+    def store(array, g):
+        cols = slice(g * TAIL, min((g + 1) * TAIL, WIDTH))
+        target = (mixed_ref, grad_ref)[array]
+        return pltpu.make_async_copy(held_ref.at[array, :, cols], target.at[:, cols], sem.at[array, g])
+
+    piece = iota((TOK, ROWS), 1) % MAIN // 2
+    for g in range(4):
+        cols = slice(g * TAIL, min((g + 1) * TAIL, WIDTH))
+        width = cols.stop - cols.start
+        for array in range(2):
+            at = array * PACKED
+            total = dot(places_ref[2 * array], packed_ref[:, at + cols.start : at + cols.stop])
+            tail = places_ref[2 * array + 1]
+            chosen = jnp.where(piece == g, tail, jnp.zeros_like(tail))
+            total += dot(chosen, packed_ref[:, at + WIDTH : at + WIDTH + width])
+            held_ref[array, :, cols] = total.astype(BF16)
+            store(array, g).start()
+
+    slot = slot_ref[...]
     row, col = iota((FLIGHT, ROWS), 0), iota((FLIGHT, ROWS), 1)
     both = as_bf16((col // MAIN == row) & (col % MAIN >= 6))
     carried = dot(both, packed_ref[:, PACKED + SPARE : PACKED + SPARE + 128])
@@ -432,9 +467,12 @@
     share_ref[...] = (
         ROUTE_SCALE / total * (inner - jnp.sum(shares * inner, axis=0, keepdims=True))
     )
-
-
-def combine(ids, keep, affinity, packed):
+    for array in range(2):
+        for g in range(4):
+            store(array, g).wait()
+
+
+def combine(ids, keep, affinity, planned, packed):
     return pl.pallas_call(
         combine_kernel,
         out_shape=(
@@ -442,13 +480,16 @@
             jax.ShapeDtypeStruct((TOK, WIDTH), BF16),
             jax.ShapeDtypeStruct((TOP, TOK), F32),
         ),
-        in_specs=vmem(4),
-        out_specs=tuple(vmem(3)),
-        scratch_shapes=[pltpu.VMEM((TOP, TOK), F32)],
+        in_specs=vmem(7),
+        out_specs=(pl.BlockSpec(memory_space=pl.ANY),) * 2 + tuple(vmem(1)),
+        scratch_shapes=[
+            pltpu.VMEM((2, TOK, WIDTH), BF16),
+            pltpu.SemaphoreType.DMA((2, 4)),
+        ],
         compiler_params=LIMITED,
         cost_estimate=cost(8 * ROWS * TOK * WIDTH, 2 * TOK * WIDTH * 4),
         name="combine",
-    )(ids, keep, affinity, packed)
+    )(ids, keep, affinity, *planned, packed)
 
 
 def exchange(packed):
@@ -478,16 +519,18 @@
     total_b, send_b = add_halves("add_b", own_b, *[swap(part, 1) for part in sends])
     send_b, recv_g = lax.optimization_barrier((send_b, recv_g))
     recv_a = swap(send_a, 2)
+    route, send_b = lax.optimization_barrier(((ids, keep, affinity_t), send_b))
     recv_b = swap(send_b, 2)
+    planned = plan(*route)
 
     *block_a, inner = block_of("block_a", 0, total_a, recv_a, total_g, recv_g)
     peer_a = [swap(part, 1) for part in block_a]
     out_sum, back_sum = spread_first(block_a, peer_a, w_gate, w_up, w_down)
-    recv_b, out_sum, back_sum = lax.optimization_barrier((recv_b, out_sum, back_sum))
+    recv_b, out_sum, back_sum, planned = lax.optimization_barrier((recv_b, out_sum, back_sum, planned))
     block_b = block_of("block_b", SPAN, total_b, recv_b, total_g, recv_g, inner)
     payload = spread_last(core, block_b, swap(block_b, 1), w_gate, w_up, w_down, out_sum, back_sum)
     rows = exchange(payload)
-    mixed, token_grad, affinity_grad = combine(ids, keep, affinity_t, rows)
+    mixed, token_grad, affinity_grad = combine(ids, keep, affinity_t, planned, rows)
     return mixed, token_grad, affinity_grad.T
 
 

time: 123 us -> 121 us (0.984)
    pallas_call x1 -> x2, Pallas kernels: 4.64 us -> 4.61 us  [the longest x1 4.04 us: send_rows(): pl.pallas_call(send_kernel, out_shape=jax.ShapeDtypeStruct((ROWS, SENT),...]
  transfers between devices with their start and end apart: 14 -> 14, of which waited for: 14 -> 9; matrix products, arithmetic and copies ran while one was open for 0% -> 0% of each run, Pallas kernels for 5% -> 5%
where the time goes in v4:
time: 121 us
  blocking collectives  81 us (67%)
  Pallas kernels  17.3 us (14%)
  waiting for transfers between devices  16.3 us (13%)
  starting transfers between devices  5.14 us (4%)
    all_to_all x2, blocking collectives, exchange(): lax.all_to_all(packed, 'node', split_axis=0, concat_axis=0, tiled=True)  81 us
    ppermute x14, waiting for transfers between devices, swap(): return lax.ppermute(values, 'local', [(i, i ^ distance) for i in range(4)])  16.3 us
    ppermute x14, starting transfers between devices, swap(): return lax.ppermute(values, 'local', [(i, i ^ distance) for i in range(4)])  5.14 us
    pallas_call x1, Pallas kernels, send_rows(): pl.pallas_call(send_kernel, out_shape=jax.ShapeDtypeStruct((ROWS, SENT),...  4.04 us
    pallas_call x2, Pallas kernels, partial_sums(): pl.pallas_call(lambda *refs: partial_kernel(first, at, *refs), out_shape=...  2.89 us
    pallas_call x1, Pallas kernels, spread_last(): pl.pallas_call(spread_last_kernel, out_shape=jax.ShapeDtypeStruct((ROWS,...  2.52 us
    pallas_call x1, Pallas kernels, combine(): pl.pallas_call(combine_kernel, out_shape=(jax.ShapeDtypeStruct((TOK, WIDT...  2.5 us
  transfers between devices with their start and end apart: 14, of which 9 were waited for; matrix products, arithmetic and copies ran while one was open for 0% of the time, Pallas kernels for 5%

profile of v4, /device:TPU:0, one launch (start us, length us, event | category | flops | bytes accessed | tf_op | source)
XLA Modules:
  0.0 120.7 jit_solution(12158783052120836092)
XLA Ops:
  0.6 4.0 %send_rows.1 = bf16[256,4480]{1,0:T(8,128)(2,1)} custom-call(s32[8,256]{1,0:T(8,128)} %bitcast.27, s32[8,256]{1,0:T(8,128)} %bitcast.30, f32[8,256]{1,0:T(8,128)} %bitcast.33, bf16[256,1792]{1,0:T(8,128)(2,1)} %refs_3_.1, bf16[256,1792]{1,0:T(8,128)(2,1)} %refs_4_.1), custom_call_target="tpu_custom_call" | custom-call | flops 939524096 | bytes 5505024 | tf_op jit(solution)/shard_map/send_rows/pallas_call | solution.py:152
  4.7 0.0 copy-start.2
  4.7 0.0 copy-start.1
  4.7 43.8 %all_to_all.22 = bf16[32,8,4480]{2,1,0:T(8,128)(2,1)S(1)} all-to-all(bf16[32,8,4480]{2,1,0:T(8,128)(2,1)} %bitcast.36), channel_id=1, replica_groups=mesh['node'=32,'local'=4] {'node'}, dimensions={0} | all-to-all | bytes 4587520 | tf_op jit(solution)/shard_map/all_to_all | solution.py:496
  48.5 0.0 copy-done.2
  48.5 0.0 copy-start
  48.5 1.5 %grad.1 = (bf16[160,1024]{1,0:T(8,128)(2,1)S(1)}, f32[160,1024]{1,0:T(8,128)S(1)}) custom-call(s32[1]{0:T(128)} %bitcast.3.core_ref.refs_0_, bf16[256,4480]{1,0:T(8,128)(2,1)S(1)} %bitcast.23, bf16[1024,1792]{1,0:T(8,128)(2,1)S(1)} %bitcast.20), custom_call_target="tpu_custom_call" | custom-call | flops 1000000 | bytes 10000 | tf_op jit(solution)/shard_map/grad/pallas_call | solution.py:230
  50.1 0.1 collective-permute-start
  50.2 1.6 %collective-permute-done.refs_0_ = bf16[160,1024]{1,0:T(8,128)(2,1)S(1)} collective-permute-done((bf16[160,1024]{1,0:T(8,128)(2,1)S(1)}, bf16[160,1024]{1,0:T(8,128)(2,1)S(1)}, u32[]{:S(2)}, u32[]{:S(2)}) %collective-permute-start) | collective-permute-done | bytes 327712 | tf_op jit(solution)/shard_map/ppermute | solution.py:500
  51.8 0.1 add_g.1
  51.9 0.7 collective-permute-start.3
  52.6 0.0 copy-done.1
  52.6 0.0 copy-done
  52.6 1.5 %pre_a.1 = (f32[160,1024]{1,0:T(8,128)S(1)}, bf16[160,256]{1,0:T(8,128)(2,1)S(1)}, bf16[160,256]{1,0:T(8,128)(2,1)S(1)}, bf16[160,256]{1,0:T(8,128)(2,1)S(1)}, b...) custom-call(s32[1]{0:T(128)} %bitcast.3.core_ref.refs_0_, bf16[256,4480]{1,0:T(8,128)(2,1)S(1)} %bitcast.24, ...), custom_call_target="tpu_custom_call" | custom-call | flops 1000000 | bytes 10000 | tf_op jit(solution)/shard_map/pre_a/pallas_call | solution.py:209
  54.1 0.1 collective-permute-start.5
  54.2 0.5 collective-permute-start.6
  54.7 0.1 collective-permute-start.7
  54.8 0.4 collective-permute-start.8
  55.2 1.4 %pre_b.1 = (f32[160,1024]{1,0:T(8,128)S(1)}, bf16[160,512]{1,0:T(8,128)(2,1)S(1)}, bf16[160,512]{1,0:T(8,128)(2,1)S(1)}) custom-call(s32[1]{0:T(128)} %bitcast.3.core_ref.refs_0_, bf16[320,1792]{1,0:T(8,128)(2,1)S(1)} %get-tuple-element.54.refs_1_, bf16[1792,1024]{1,0:T(8,128)(2,1)S(1)} %bitcast.13, bf16[1792,1024]{1,0:T(8,128)(2,1)S(1)} %bitcast.17), custom_call_target="tpu_custom_call" | custom-call | flops 1000000 | bytes 10000 | tf_op jit(solution)/shard_map/pre_b/pallas_call | solution.py:209
  56.6 0.0 copy-start.3
  56.6 0.0 copy-start.4
  56.6 0.0 copy-start.5
  56.6 0.0 collective-permute-done.5.refs_0_
  56.7 0.2 collective-permute-start.1
  56.8 0.0 collective-permute-done.6.refs_1_
  56.8 0.0 collective-permute-done.7.refs_2_
  56.8 0.0 collective-permute-done.8.refs_3_
  56.8 0.1 add_a.1
  56.9 1.5 %collective-permute-start.9 = (bf16[160,1024]{1,0:T(8,128)(2,1)S(1)}, bf16[160,1024]{1,0:T(8,128)(2,1)S(1)}, u32[]{:S(2)}, u32[]{:S(2)}) collective-permute-start(bf16[160,1024]{1,0:T(8,128)(2,1)S(1)} %get-tuple-element.68), channel_id=1, source_target_pairs={{0,2},{1,3},{2,0},{3,1},{4,6},{5,7},{6,4},{7,5},{8,10},{9,11},{10,... | collective-permute-start | bytes 983048 | tf_op jit(solution)/shard_map/ppermute | solution.py:500
  58.4 0.2 collective-permute-start.2
  58.6 0.0 collective-permute-done.1.refs_0_
  58.6 1.2 %collective-permute-done.2.refs_1_ = bf16[160,512]{1,0:T(8,128)(2,1)S(1)} collective-permute-done((bf16[160,512]{1,0:T(8,128)(2,1)S(1)}, bf16[160,512]{1,0:T(8,128)(2,1)S(1)}, u32[]{:S(2)}, u32[]{:S(2)}) %collective-permute-start.2) | collective-permute-done | bytes 163872 | tf_op jit(solution)/shard_map/ppermute | solution.py:500
  59.8 0.1 add_b.1
  59.9 2.6 %collective-permute-done.3.refs_3_ = bf16[160,1024]{1,0:T(8,128)(2,1)S(1)} collective-permute-done((bf16[160,1024]{1,0:T(8,128)(2,1)S(1)}, bf16[160,1024]{1,0:T(8,128)(2,1)S(1)}, u32[]{:S(2)}, u32[]{:S(2)}) %collective-permute-start.3) | collective-permute-done | bytes 327712 | tf_op jit(solution)/shard_map/ppermute | solution.py:500
  62.5 0.6 collective-permute-start.4
  63.2 6.4 %collective-permute-done.9.refs_1_ = bf16[160,1024]{1,0:T(8,128)(2,1)S(1)} collective-permute-done((bf16[160,1024]{1,0:T(8,128)(2,1)S(1)}, bf16[160,1024]{1,0:T(8,128)(2,1)S(1)}, u32[]{:S(2)}, u32[]{:S(2)}) %collective-permute-start.9) | collective-permute-done | bytes 327712 | tf_op jit(solution)/shard_map/ppermute | solution.py:500
  69.6 0.3 block_a.1
  69.9 0.0 collective-permute-start.10
  69.9 0.5 collective-permute-start.11
  70.4 0.1 collective-permute-start.12
  70.5 0.0 copy-done.3
  70.5 0.0 copy-done.4
  70.5 0.0 copy-done.5
  70.5 0.6 plan.1
  71.1 0.2 collective-permute-done.10.refs_3_
  71.3 0.2 collective-permute-done.11.refs_4_
  71.5 0.3 collective-permute-done.12.refs_5_
  71.8 2.2 %spread_a.1 = (f32[320,1792]{1,0:T(8,128)S(1)}, f32[320,1792]{1,0:T(8,128)S(1)}) custom-call(bf16[160,512]{1,0:T(8,128)(2,1)S(1)} %get-tuple-element.71.refs_0_, bf16[160,512]{1,0:T(8,128)(2,1)S(1)} %get-tuple-element.72.refs_1_, bf16[160,512]{1,0:T(8,128)(2,1)S(1)} %get-tuple-element.73.refs_2_, bf16[160,512]{1,0:T(8,128)(2,1)S(1)} %collective-permute-done.10.refs_3_, ...), custom_call_target="tpu_custom_call" | custom-call | flops 1000000 | bytes 10000 | tf_op jit(solution)/shard_map/spread_a/pallas_call | solution.py:267
  74.0 1.8 %collective-permute-done.4.refs_1_ = bf16[160,1024]{1,0:T(8,128)(2,1)S(1)} collective-permute-done((bf16[160,1024]{1,0:T(8,128)(2,1)S(1)}, bf16[160,1024]{1,0:T(8,128)(2,1)S(1)}, u32[]{:S(2)}, u32[]{:S(2)}) %collective-permute-start.4) | collective-permute-done | bytes 327712 | tf_op jit(solution)/shard_map/ppermute | solution.py:500
  75.8 0.4 block_b.1.own_ref
  76.2 0.2 collective-permute-start.13
  76.4 1.9 %collective-permute-done.13.peer_ref = bf16[160,1664]{1,0:T(8,128)(2,1)S(1)} collective-permute-done((bf16[160,1664]{1,0:T(8,128)(2,1)S(1)}, bf16[160,1664]{1,0:T(8,128)(2,1)S(1)}, u32[]{:S(2)}, u32[]{:S(2)}) %collective-permute-start.13) | collective-permute-done | bytes 532512 | tf_op jit(solution)/shard_map/ppermute | solution.py:500
  78.3 2.5 %spread_b.1 = bf16[256,4608]{1,0:T(8,128)(2,1)S(1)} custom-call(s32[1]{0:T(128)} %bitcast.3.core_ref.refs_0_, bf16[160,1664]{1,0:T(8,128)(2,1)S(1)} %block_b.1.own_ref, bf16[160,1664]{1,0:T(8,128)(2,1)S(1)} %collective-permute-done.13.peer_ref, bf16[1792,1024]{1,0:T(8,128)(2,1)S(1)} %bitcast.15, bf16[1792,1024]{1,0:T(8,128)(2,1)S(1)} %bitcast.19, ...), custom_call_target="tpu_custom_call" | custom-call | flops 1000000 | bytes 10000 | tf_op jit(solution)/shard_map/spread_b/pallas_call | solution.py:328
  80.8 37.2 %all_to_all.23 = bf16[32,8,4608]{2,1,0:T(8,128)(2,1)S(1)} all-to-all(bf16[32,8,4608]{2,1,0:T(8,128)(2,1)S(1)} %bitcast.25), channel_id=1, replica_groups=mesh['node'=32,'local'=4] {'node'}, dimensions={0} | all-to-all | bytes 4718592 | tf_op jit(solution)/shard_map/all_to_all | solution.py:496
  118.0 2.5 %combine.1 = (bf16[256,1792]{1,0:T(8,128)(2,1)}, bf16[256,1792]{1,0:T(8,128)(2,1)}, f32[8,256]{1,0:T(8,128)}) custom-call(s32[8,256]{1,0:T(8,128)S(1)} %bitcast.29, s32[8,256]{1,0:T(8,128)S(1)} %bitcast.32, f32[8,256]{1,0:T(8,128)S(1)} %bitcast.35, bf16[4,256,256]{2,1,0:T(8,128)(2,1)S(1)} %get-tuple-element.82.places_ref, ...), custom_call_target="tpu_custom_call" | custom-call | flops 939524096 | bytes 3670016 | tf_op jit(solution)/shard_map/combine/pallas_call | solution.py:476
Async XLA Ops:
  4.7 43.9 %copy-start.2 = (bf16[1,1024,1792]{2,1,0:T(8,128)(2,1)S(1)}, bf16[1,1024,1792]{2,1,0:T(8,128)(2,1)}, u32[]{:S(2)}) copy-start(bf16[1,1024,1792]{2,1,0:T(8,128)(2,1)} %param.14) | copy-start | bytes 11010052
  4.7 47.9 %copy-start.1 = (bf16[1,1792,1024]{2,1,0:T(8,128)(2,1)S(1)}, bf16[1,1792,1024]{2,1,0:T(8,128)(2,1)}, u32[]{:S(2)}) copy-start(bf16[1,1792,1024]{2,1,0:T(8,128)(2,1)} %param.13) | copy-start | bytes 11010052
  48.5 4.1 %copy-start = (bf16[1,1792,1024]{2,1,0:T(8,128)(2,1)S(1)}, bf16[1,1792,1024]{2,1,0:T(8,128)(2,1)}, u32[]{:S(2)}) copy-start(bf16[1,1792,1024]{2,1,0:T(8,128)(2,1)} %param.12) | copy-start | bytes 11010052
  50.1 1.7 %collective-permute-start = (bf16[160,1024]{1,0:T(8,128)(2,1)S(1)}, bf16[160,1024]{1,0:T(8,128)(2,1)S(1)}, u32[]{:S(2)}, u32[]{:S(2)}) collective-permute-start(bf16[160,1024]{1,0:T(8,128)(2,1)S(1)} %get-tuple-element.51), channel_id=1, source_target_pairs={{0,1},{1,0},{2,3},{3,2},{4,5},{5,4},{6,7},{7,6},{8,9},{9,8},{10,11... | collective-permute-start | bytes 983048 | tf_op jit(solution)/shard_map/ppermute | solution.py:500
  51.9 10.6 %collective-permute-start.3 = (bf16[160,1024]{1,0:T(8,128)(2,1)S(1)}, bf16[160,1024]{1,0:T(8,128)(2,1)S(1)}, u32[]{:S(2)}, u32[]{:S(2)}) collective-permute-start(bf16[160,1024]{1,0:T(8,128)(2,1)S(1)} %get-tuple-element.59), channel_id=1, source_target_pairs={{0,2},{1,3},{2,0},{3,1},{4,6},{5,7},{6,4},{7,5},{8,10},{9,11},{10,... | collective-permute-start | bytes 983048 | tf_op jit(solution)/shard_map/ppermute | solution.py:500
  54.1 2.5 %collective-permute-start.5 = (bf16[160,256]{1,0:T(8,128)(2,1)S(1)}, bf16[160,256]{1,0:T(8,128)(2,1)S(1)}, u32[]{:S(2)}, u32[]{:S(2)}) collective-permute-start(bf16[160,256]{1,0:T(8,128)(2,1)S(1)} %get-tuple-element.63), channel_id=1, source_target_pairs={{0,1},{1,0},{2,3},{3,2},{4,5},{5,4},{6,7},{7,6},{8,9},{9,8},{10,11... | collective-permute-start | bytes 245768 | tf_op jit(solution)/shard_map/ppermute | solution.py:500
  54.2 2.6 %collective-permute-start.6 = (bf16[160,256]{1,0:T(8,128)(2,1)S(1)}, bf16[160,256]{1,0:T(8,128)(2,1)S(1)}, u32[]{:S(2)}, u32[]{:S(2)}) collective-permute-start(bf16[160,256]{1,0:T(8,128)(2,1)S(1)} %get-tuple-element.64), channel_id=1, source_target_pairs={{0,1},{1,0},{2,3},{3,2},{4,5},{5,4},{6,7},{7,6},{8,9},{9,8},{10,11... | collective-permute-start | bytes 245768 | tf_op jit(solution)/shard_map/ppermute | solution.py:500
  54.7 2.1 %collective-permute-start.7 = (bf16[160,256]{1,0:T(8,128)(2,1)S(1)}, bf16[160,256]{1,0:T(8,128)(2,1)S(1)}, u32[]{:S(2)}, u32[]{:S(2)}) collective-permute-start(bf16[160,256]{1,0:T(8,128)(2,1)S(1)} %get-tuple-element.65), channel_id=1, source_target_pairs={{0,1},{1,0},{2,3},{3,2},{4,5},{5,4},{6,7},{7,6},{8,9},{9,8},{10,11... | collective-permute-start | bytes 245768 | tf_op jit(solution)/shard_map/ppermute | solution.py:500
  54.8 2.0 %collective-permute-start.8 = (bf16[160,256]{1,0:T(8,128)(2,1)S(1)}, bf16[160,256]{1,0:T(8,128)(2,1)S(1)}, u32[]{:S(2)}, u32[]{:S(2)}) collective-permute-start(bf16[160,256]{1,0:T(8,128)(2,1)S(1)} %get-tuple-element.66), channel_id=1, source_target_pairs={{0,1},{1,0},{2,3},{3,2},{4,5},{5,4},{6,7},{7,6},{8,9},{9,8},{10,11... | collective-permute-start | bytes 245768 | tf_op jit(solution)/shard_map/ppermute | solution.py:500
  56.6 13.9 %copy-start.3 = (s32[256,8]{0,1:T(8,128)S(1)}, s32[256,8]{0,1:T(8,128)}, u32[]{:S(2)}) copy-start(s32[256,8]{0,1:T(8,128)} %param.9) | copy-start | bytes 24580
  56.6 13.9 %copy-start.4 = (s32[256,8]{0,1:T(8,128)S(1)}, s32[256,8]{0,1:T(8,128)}, u32[]{:S(2)}) copy-start(s32[256,8]{0,1:T(8,128)} %param.10) | copy-start | bytes 24580
  56.6 13.9 %copy-start.5 = (f32[256,8]{0,1:T(8,128)S(1)}, f32[256,8]{0,1:T(8,128)}, u32[]{:S(2)}) copy-start(f32[256,8]{0,1:T(8,128)} %param.11) | copy-start | bytes 24580
  56.7 1.9 %collective-permute-start.1 = (bf16[160,512]{1,0:T(8,128)(2,1)S(1)}, bf16[160,512]{1,0:T(8,128)(2,1)S(1)}, u32[]{:S(2)}, u32[]{:S(2)}) collective-permute-start(bf16[160,512]{1,0:T(8,128)(2,1)S(1)} %get-tuple-element.56), channel_id=1, source_target_pairs={{0,1},{1,0},{2,3},{3,2},{4,5},{5,4},{6,7},{7,6},{8,9},{9,8},{10,11... | collective-permute-start | bytes 491528 | tf_op jit(solution)/shard_map/ppermute | solution.py:500
  56.9 12.6 %collective-permute-start.9 = (bf16[160,1024]{1,0:T(8,128)(2,1)S(1)}, bf16[160,1024]{1,0:T(8,128)(2,1)S(1)}, u32[]{:S(2)}, u32[]{:S(2)}) collective-permute-start(bf16[160,1024]{1,0:T(8,128)(2,1)S(1)} %get-tuple-element.68), channel_id=1, source_target_pairs={{0,2},{1,3},{2,0},{3,1},{4,6},{5,7},{6,4},{7,5},{8,10},{9,11},{10,... | collective-permute-start | bytes 983048 | tf_op jit(solution)/shard_map/ppermute | solution.py:500
  58.4 1.4 %collective-permute-start.2 = (bf16[160,512]{1,0:T(8,128)(2,1)S(1)}, bf16[160,512]{1,0:T(8,128)(2,1)S(1)}, u32[]{:S(2)}, u32[]{:S(2)}) collective-permute-start(bf16[160,512]{1,0:T(8,128)(2,1)S(1)} %get-tuple-element.57), channel_id=1, source_target_pairs={{0,1},{1,0},{2,3},{3,2},{4,5},{5,4},{6,7},{7,6},{8,9},{9,8},{10,11... | collective-permute-start | bytes 491528 | tf_op jit(solution)/shard_map/ppermute | solution.py:500
  62.5 13.2 %collective-permute-start.4 = (bf16[160,1024]{1,0:T(8,128)(2,1)S(1)}, bf16[160,1024]{1,0:T(8,128)(2,1)S(1)}, u32[]{:S(2)}, u32[]{:S(2)}) collective-permute-start(bf16[160,1024]{1,0:T(8,128)(2,1)S(1)} %get-tuple-element.61), channel_id=1, source_target_pairs={{0,2},{1,3},{2,0},{3,1},{4,6},{5,7},{6,4},{7,5},{8,10},{9,11},{10,... | collective-permute-start | bytes 983048 | tf_op jit(solution)/shard_map/ppermute | solution.py:500
  69.9 1.4 %collective-permute-start.10 = (bf16[160,512]{1,0:T(8,128)(2,1)S(1)}, bf16[160,512]{1,0:T(8,128)(2,1)S(1)}, u32[]{:S(2)}, u32[]{:S(2)}) collective-permute-start(bf16[160,512]{1,0:T(8,128)(2,1)S(1)} %get-tuple-element.71.refs_0_), channel_id=1, source_target_pairs={{0,1},{1,0},{2,3},{3,2},{4,5},{5,4},{6,7},{7,6},{8,9},{9,8},{10,11... | collective-permute-start | bytes 491528 | tf_op jit(solution)/shard_map/ppermute | solution.py:500
  69.9 1.6 %collective-permute-start.11 = (bf16[160,512]{1,0:T(8,128)(2,1)S(1)}, bf16[160,512]{1,0:T(8,128)(2,1)S(1)}, u32[]{:S(2)}, u32[]{:S(2)}) collective-permute-start(bf16[160,512]{1,0:T(8,128)(2,1)S(1)} %get-tuple-element.72.refs_1_), channel_id=1, source_target_pairs={{0,1},{1,0},{2,3},{3,2},{4,5},{5,4},{6,7},{7,6},{8,9},{9,8},{10,11... | collective-permute-start | bytes 491528 | tf_op jit(solution)/shard_map/ppermute | solution.py:500
  70.4 1.4 %collective-permute-start.12 = (bf16[160,512]{1,0:T(8,128)(2,1)S(1)}, bf16[160,512]{1,0:T(8,128)(2,1)S(1)}, u32[]{:S(2)}, u32[]{:S(2)}) collective-permute-start(bf16[160,512]{1,0:T(8,128)(2,1)S(1)} %get-tuple-element.73.refs_2_), channel_id=1, source_target_pairs={{0,1},{1,0},{2,3},{3,2},{4,5},{5,4},{6,7},{7,6},{8,9},{9,8},{10,11... | collective-permute-start | bytes 491528 | tf_op jit(solution)/shard_map/ppermute | solution.py:500
  76.2 2.2 %collective-permute-start.13 = (bf16[160,1664]{1,0:T(8,128)(2,1)S(1)}, bf16[160,1664]{1,0:T(8,128)(2,1)S(1)}, u32[]{:S(2)}, u32[]{:S(2)}) collective-permute-start(bf16[160,1664]{1,0:T(8,128)(2,1)S(1)} %block_b.1.own_ref), channel_id=1, source_target_pairs={{0,1},{1,0},{2,3},{3,2},{4,5},{5,4},{6,7},{7,6},{8,9},{9,8},{10,11... | collective-permute-start | bytes 1597448 | tf_op jit(solution)/shard_map/ppermute | solution.py:500

commit v5 on v4

--- a/solution.py
+++ b/solution.py
@@ -109,28 +109,33 @@
         copy.wait()
     weight_ref[...] = weights_of(affinity_ref)
     marks, weights = expert_marks(ids_ref, keep_ref, weight_ref)
-    main, tail = picks(slots_of(marks))
-    place = jnp.concatenate([as_bf16(main), as_bf16(tail)], axis=0)
+    slot = slots_of(marks)
+    main, unused = picks(slot)
+    dense_row = iota((2 * FLIGHT, TOK), 0)
+    pair = as_bf16(iota((2 * FLIGHT, FLIGHT), 0) // 2 == iota((2 * FLIGHT, FLIGHT), 1))
+    dense = dot(pair, slot.astype(BF16)) == (dense_row % 2 + MAIN).astype(F32)
+    place = jnp.concatenate([as_bf16(main), as_bf16(dense)], axis=0)
     high, low = halves_of(weights)
-    wide = dot(spread_matrix(), high) + dot(spread_matrix(), low)
     main_scale, tail_scale = [
-        jnp.sum(jnp.where(mask, wide, 0.0), axis=1, keepdims=True) for mask in (main, tail)
+        jnp.sum(jnp.where(mask, dot(copies, high) + dot(copies, low), 0.0), axis=1, keepdims=True)
+        for mask, copies in ((main, spread_matrix()), (dense, pair))
     ]
-    sub = iota((ROWS, HALF_WIDTH), 0) % MAIN
-    tails = jnp.zeros((ROWS, HALF_WIDTH), BF16)
     for i in range(4):
         load(i).wait()
+    pieces = []
     for i in range(4):
-        block = in_ref[i]
-        both = dot(place, block)
+        both = dot(place, in_ref[i])
         first, second = both[:ROWS], both[ROWS:]
         if i >= 2:
             first, second = first * main_scale, second * tail_scale
         packed_ref[:, i * HALF_WIDTH : (i + 1) * HALF_WIDTH] = first.astype(BF16)
         store(i).start()
-        here = sub // 2 == 2 * (i % 2) + i // 2
-        tails = jnp.where(here, second.astype(BF16), tails)
-    packed_ref[:, 2 * WIDTH :] = tails
+        pieces.append(second.astype(BF16))
+    row, col = iota((ROWS, ROWS), 0), iota((ROWS, ROWS), 1)
+    source, expert, which = col // (2 * FLIGHT), col % (2 * FLIGHT) // 2, col % 2
+    goal = 4 * (source % 2) + 2 * (source // 2) + which
+    spot = as_bf16((row // MAIN == expert) & (row % MAIN == goal))
+    packed_ref[:, 2 * WIDTH :] = dot(spot, jnp.concatenate(pieces, axis=0)).astype(BF16)
     store(4).start()
     for i in range(5):
         store(i).wait()
@@ -217,28 +222,34 @@
     )(core, packed, gate, up)
 
 
-def grad_kernel(core_ref, packed_ref, weight_ref, send_ref, keep_ref, rows_ref):
-    core = core_ref[0]
-    unpack_half(packed_ref, 1, 1 - core, rows_ref, 0)
-    unpack_half(packed_ref, 1, core, rows_ref, HALF)
-    product = dot(rows_ref[...], weight_ref[...], NT)
+def grad_kernel(first, core_ref, packed_ref, weight_ref, send_ref, keep_ref, *rest):
+    if rest:
+        rows_ref = rest[0]
+        core = core_ref[0]
+        unpack_half(packed_ref, 1, 1 - core, rows_ref, 0)
+        unpack_half(packed_ref, 1, core, rows_ref, HALF)
+    else:
+        rows_ref = packed_ref
+    product = dot(rows_ref[...], weight_ref[first : first + SPAN, :], NT)
     send_ref[...] = product[:HALF].astype(BF16)
     keep_ref[...] = product[HALF:]
 
 
-def grad_sums(core, packed, weight):
-    return pl.pallas_call(
-        grad_kernel,
-        out_shape=(
-            jax.ShapeDtypeStruct((HALF, FF), BF16),
-            jax.ShapeDtypeStruct((HALF, FF), F32),
-        ),
+def grad_sums(name, core, packed, weight, first):
+    shapes = (
+        jax.ShapeDtypeStruct((HALF, SPAN), BF16),
+        jax.ShapeDtypeStruct((HALF, SPAN), F32),
+    )
+    if first == 0:
+        shapes += (jax.ShapeDtypeStruct((2 * HALF, WIDTH), BF16),)
+    return pl.pallas_call(
+        lambda *refs: grad_kernel(first, *refs),
+        out_shape=shapes,
         in_specs=[pl.BlockSpec(memory_space=pltpu.SMEM)] + vmem(2),
-        out_specs=tuple(vmem(2)),
-        scratch_shapes=[pltpu.VMEM((2 * HALF, WIDTH), BF16)],
-        compiler_params=LIMITED,
-        cost_estimate=cost(1e6, 1e4),
-        name="grad",
+        out_specs=tuple(vmem(len(shapes))),
+        compiler_params=LIMITED,
+        cost_estimate=cost(1e6, 1e4),
+        name=name,
     )(core, packed, weight)
 
 
@@ -279,10 +290,7 @@
     )(*own, *peer, gate, up, down)
 
 
-def spread_last_kernel(core_ref, own_ref, peer_ref, gate_ref, up_ref, down_ref, out_sum, back_sum, packed_ref, rows_ref):
-    core = core_ref[0]
-    rows_ref[:HALF] = own_ref[:, :BLOCK]
-    rows_ref[HALF:] = peer_ref[:, :BLOCK]
+def pack(core, product_of, sum_ref, packed_ref, at):
     halves = [
         (base, pl.ds(pl.multiple_of(half * HALF_MAIN, HALF_MAIN), HALF_MAIN))
         for base, half in ((0, core), (HALF, 1 - core))
@@ -291,26 +299,60 @@
     for g in range(4):
         width = min(TAIL, WIDTH - g * TAIL)
         cols = slice(g * TAIL, g * TAIL + width)
-        products = block_products(rows_ref, SPAN, gate_ref, up_ref, down_ref, cols)
-        for product, sum_ref, at in zip(products, (out_sum, back_sum), (0, PACKED)):
-            product = (product + sum_ref[:, cols]).astype(BF16)
-            for base, rows in halves:
-                packed_ref[rows, at + g * TAIL : at + g * TAIL + width] = product[
-                    base : base + HALF_MAIN
-                ]
-                tail = product[base + HALF_MAIN : base + HALF]
-                if width < TAIL:
-                    tail = jnp.concatenate([tail, jnp.zeros((HALF - HALF_MAIN, TAIL - width), BF16)], axis=1)
-                tails[at, base, g] = tail
+        product = (product_of(cols) + sum_ref[:, cols]).astype(BF16)
+        for base, rows in halves:
+            packed_ref[rows, at + cols.start : at + cols.stop] = product[base : base + HALF_MAIN]
+            tail = product[base + HALF_MAIN : base + HALF]
+            if width < TAIL:
+                rest = jnp.zeros((HALF - HALF_MAIN, TAIL - width), BF16)
+                tail = jnp.concatenate([tail, rest], axis=1)
+            tails[base, g] = tail
     row, col = iota((HALF_MAIN, HALF_MAIN), 0), iota((HALF_MAIN, HALF_MAIN), 1)
     piece, pair = col // (HALF - HALF_MAIN), col % (HALF - HALF_MAIN)
     place = as_bf16((row // MAIN == pair // 2) & (row % MAIN == 2 * piece + pair % 2))
-    for at in (0, PACKED):
-        for base, rows in halves:
-            stacked = jnp.concatenate([tails[at, base, g] for g in range(4)], axis=0)
-            packed_ref[rows, at + WIDTH : at + PACKED] = dot(place, stacked).astype(BF16)
+    for base, rows in halves:
+        stacked = jnp.concatenate([tails[base, g] for g in range(4)], axis=0)
+        packed_ref[rows, at + WIDTH : at + PACKED] = dot(place, stacked).astype(BF16)
+
+
+def spread_out_kernel(core_ref, *refs):
+    own_refs, peer_refs, (down_ref, sum_ref, packed_ref, rows_ref) = refs[:2], refs[2:4], refs[4:]
+    for i in range(2):
+        rows_ref[:HALF, i * TILE : (i + 1) * TILE] = own_refs[i][...]
+        rows_ref[HALF:, i * TILE : (i + 1) * TILE] = peer_refs[i][...]
+
+    def product_of(cols):
+        return dot(rows_ref[...], down_ref[SPAN:, cols])
+
+    pack(core_ref[0], product_of, sum_ref, packed_ref, 0)
+
+
+def spread_out(core, own, peer, down, out_sum):
+    return pl.pallas_call(
+        spread_out_kernel,
+        out_shape=jax.ShapeDtypeStruct((ROWS, PACKED), BF16),
+        in_specs=[pl.BlockSpec(memory_space=pltpu.SMEM)] + vmem(6),
+        out_specs=pl.BlockSpec(memory_space=pltpu.VMEM),
+        scratch_shapes=[pltpu.VMEM((2 * HALF, SPAN), BF16)],
+        compiler_params=LIMITED,
+        cost_estimate=cost(1e6, 1e4),
+        name="spread_out",
+    )(core, *own, *peer, down, out_sum)
+
+
+def spread_last_kernel(core_ref, own_ref, peer_ref, gate_ref, up_ref, sum_ref, out_rows_ref, packed_ref, rows_ref):
+    core = core_ref[0]
+    rows_ref[:HALF] = own_ref[:, : 2 * SPAN]
+    rows_ref[HALF:] = peer_ref[:, : 2 * SPAN]
+    packed_ref[:, :PACKED] = out_rows_ref[...]
+
+    def product_of(cols):
+        product = dot(rows_ref[:, :SPAN], gate_ref[cols, SPAN:], NT)
+        return product + dot(rows_ref[:, SPAN:], up_ref[cols, SPAN:], NT)
+
+    pack(core, product_of, sum_ref, packed_ref, PACKED)
     for half_ref, half in ((own_ref, core), (peer_ref, 1 - core)):
-        carried = half_ref[:, BLOCK:]
+        carried = half_ref[:, 2 * SPAN :]
         total = jnp.zeros((HALF_MAIN, 128), F32)
         for first, count, each, base in ((0, HALF_MAIN, MAIN, 0), (HALF_MAIN, HALF - HALF_MAIN, 2, MAIN)):
             row, col = iota((HALF_MAIN, count), 0), iota((HALF_MAIN, count), 1)
@@ -324,17 +366,17 @@
         packed_ref[rows, spare] = (packed_ref[rows, spare].astype(F32) + total).astype(BF16)
 
 
-def spread_last(core, own, peer, gate, up, down, out_sum, back_sum):
+def spread_last(core, own, peer, gate, up, back_sum, out_rows):
     return pl.pallas_call(
         spread_last_kernel,
         out_shape=jax.ShapeDtypeStruct((ROWS, PAYLOAD), BF16),
-        in_specs=[pl.BlockSpec(memory_space=pltpu.SMEM)] + vmem(7),
+        in_specs=[pl.BlockSpec(memory_space=pltpu.SMEM)] + vmem(6),
         out_specs=pl.BlockSpec(memory_space=pltpu.VMEM),
-        scratch_shapes=[pltpu.VMEM((2 * HALF, BLOCK), BF16)],
+        scratch_shapes=[pltpu.VMEM((2 * HALF, 2 * SPAN), BF16)],
         compiler_params=LIMITED,
         cost_estimate=cost(1e6, 1e4),
         name="spread_b",
-    )(core, own, peer, gate, up, down, out_sum, back_sum)
+    )(core, own, peer, gate, up, back_sum, out_rows)
 
 
 def add_kernel(keep_ref, *refs):
@@ -363,44 +405,53 @@
     )(keep, *recv)
 
 
-def block_kernel(first, total_ref, recv_ref, grad_total_ref, grad_recv_ref, *rest):
+def block_kernel(total_ref, recv_ref, grad_total_ref, grad_recv_ref, hidden_ref, gate_ref, up_ref, inner_ref):
     pre = total_ref[...] + recv_ref[...].astype(F32)
     gate, up = pre[:, :SPAN], pre[:, SPAN:]
-    cols = slice(first, first + SPAN)
-    grad = grad_total_ref[:, cols] + grad_recv_ref[:, cols].astype(F32)
+    grad = grad_total_ref[...] + grad_recv_ref[...].astype(F32)
     sigma = jax.nn.sigmoid(gate)
     hidden = gate * sigma * up
-    inner = jnp.sum(hidden * grad, axis=1, keepdims=True)
-    if first == 0:
-        *parts, inner_ref = rest
-        inner_ref[...] = jnp.broadcast_to(inner, (HALF, 128))
-    else:
-        inner_ref, out_ref = rest
-        parts = [out_ref.at[:, i * SPAN : (i + 1) * SPAN] for i in range(3)]
-        high, low = halves_of(inner + inner_ref[:, :1])
-        lane = iota((HALF, 128), 1)
-        both = jnp.where(lane == 0, high.astype(F32), jnp.where(lane == 1, low.astype(F32), 0.0))
-        out_ref[:, BLOCK:] = both.astype(BF16)
-    parts[0][...] = hidden.astype(BF16)
-    parts[1][...] = (grad * up * sigma * (1.0 + gate * (1.0 - sigma))).astype(BF16)
-    parts[2][...] = (grad * gate * sigma).astype(BF16)
-
-
-def block_of(name, first, total, recv, grad_total, grad_recv, *inner):
-    if inner:
-        shapes = jax.ShapeDtypeStruct((HALF, BLOCK + 128), BF16)
-    else:
-        shapes = (jax.ShapeDtypeStruct((HALF, SPAN), BF16),) * 3
-        shapes += (jax.ShapeDtypeStruct((HALF, 128), F32),)
-    return pl.pallas_call(
-        lambda *refs: block_kernel(first, *refs),
-        out_shape=shapes,
-        in_specs=vmem(4 + len(inner)),
-        out_specs=vmem(1)[0] if inner else tuple(vmem(4)),
+    inner_ref[...] = jnp.broadcast_to(jnp.sum(hidden * grad, axis=1, keepdims=True), (HALF, 128))
+    hidden_ref[...] = hidden.astype(BF16)
+    gate_ref[...] = (grad * up * sigma * (1.0 + gate * (1.0 - sigma))).astype(BF16)
+    up_ref[...] = (grad * gate * sigma).astype(BF16)
+
+
+def hidden_kernel(total_ref, recv_ref, *hidden_refs):
+    pre = total_ref[...] + recv_ref[...].astype(F32)
+    gate, up = pre[:, :SPAN], pre[:, SPAN:]
+    hidden = (gate * jax.nn.sigmoid(gate) * up).astype(BF16)
+    for i, hidden_ref in enumerate(hidden_refs):
+        hidden_ref[...] = hidden[:, i * TILE : (i + 1) * TILE]
+
+
+def pair_kernel(total_ref, recv_ref, grad_total_ref, grad_recv_ref, inner_ref, out_ref):
+    pre = total_ref[...] + recv_ref[...].astype(F32)
+    gate, up = pre[:, :SPAN], pre[:, SPAN:]
+    grad = grad_total_ref[...] + grad_recv_ref[...].astype(F32)
+    sigma = jax.nn.sigmoid(gate)
+    inner = jnp.sum(gate * sigma * up * grad, axis=1, keepdims=True)
+    high, low = halves_of(inner + inner_ref[:, :1])
+    lane = iota((HALF, 128), 1)
+    both = jnp.where(lane == 0, high.astype(F32), jnp.where(lane == 1, low.astype(F32), 0.0))
+    out_ref[:, 2 * SPAN :] = both.astype(BF16)
+    out_ref[:, :SPAN] = (grad * up * sigma * (1.0 + gate * (1.0 - sigma))).astype(BF16)
+    out_ref[:, SPAN : 2 * SPAN] = (grad * gate * sigma).astype(BF16)
+
+
+def part_of(name, kernel, widths, *operands):
+    shapes = [
+        jax.ShapeDtypeStruct((HALF, width), F32 if width == 128 else BF16) for width in widths
+    ]
+    return pl.pallas_call(
+        kernel,
+        out_shape=tuple(shapes) if len(shapes) > 1 else shapes[0],
+        in_specs=vmem(len(operands)),
+        out_specs=tuple(vmem(len(shapes))) if len(shapes) > 1 else vmem(1)[0],
         compiler_params=LIMITED,
         cost_estimate=cost(1e6, 1e4),
         name=name,
-    )(total, recv, grad_total, grad_recv, *inner)
+    )(*operands)
 
 
 def plan_kernel(ids_ref, keep_ref, affinity_ref, places_ref, slot_ref, weight_ref):
@@ -509,26 +560,37 @@
     payload, core = lax.optimization_barrier((payload, core))
     rows = exchange(payload)
 
-    send_g, own_g = grad_sums(core, rows, w_down)
-    total_g, send_g = add_halves("add_g", own_g, swap(send_g, 1))
+    send_g, own_g, grad_rows = grad_sums("grad_a", core, rows, w_down, 0)
+    total_g, send_g = add_halves("add_ga", own_g, swap(send_g, 1))
     rows, send_g = lax.optimization_barrier((rows, send_g))
     recv_g = swap(send_g, 2)
     own_a, *sends, unpacked = partial_sums("pre_a", core, rows, 0, w_gate, w_up, 0, 4)
     total_a, send_a = add_halves("add_a", own_a, *[swap(part, 1) for part in sends])
+    recv_a = swap(send_a, 2)
+    unpacked, recv_g = lax.optimization_barrier((unpacked, recv_g))
     own_b, *sends = partial_sums("pre_b", core, unpacked, None, w_gate, w_up, SPAN, 2)
     total_b, send_b = add_halves("add_b", own_b, *[swap(part, 1) for part in sends])
-    send_b, recv_g = lax.optimization_barrier((send_b, recv_g))
-    recv_a = swap(send_a, 2)
-    route, send_b = lax.optimization_barrier(((ids, keep, affinity_t), send_b))
     recv_b = swap(send_b, 2)
+    send_h, own_h = grad_sums("grad_b", core, grad_rows, w_down, SPAN)
+    total_h, send_h = add_halves("add_gb", own_h, swap(send_h, 1))
+    total_a, send_h = lax.optimization_barrier((total_a, send_h))
+    recv_h = swap(send_h, 2)
+    route, total_b = lax.optimization_barrier(((ids, keep, affinity_t), total_b))
     planned = plan(*route)
 
-    *block_a, inner = block_of("block_a", 0, total_a, recv_a, total_g, recv_g)
+    *block_a, inner = part_of(
+        "block_a", block_kernel, (SPAN, SPAN, SPAN, 128), total_a, recv_a, total_g, recv_g
+    )
     peer_a = [swap(part, 1) for part in block_a]
     out_sum, back_sum = spread_first(block_a, peer_a, w_gate, w_up, w_down)
     recv_b, out_sum, back_sum, planned = lax.optimization_barrier((recv_b, out_sum, back_sum, planned))
-    block_b = block_of("block_b", SPAN, total_b, recv_b, total_g, recv_g, inner)
-    payload = spread_last(core, block_b, swap(block_b, 1), w_gate, w_up, w_down, out_sum, back_sum)
+    hidden_b = part_of("hidden_b", hidden_kernel, (TILE, TILE), total_b, recv_b)
+    out_rows = spread_out(core, hidden_b, [swap(part, 1) for part in hidden_b], w_down, out_sum)
+    recv_h, out_rows = lax.optimization_barrier((recv_h, out_rows))
+    pair_b = part_of(
+        "pair_b", pair_kernel, (2 * SPAN + 128,), total_b, recv_b, total_h, recv_h, inner
+    )
+    payload = spread_last(core, pair_b, swap(pair_b, 1), w_gate, w_up, back_sum, out_rows)
     rows = exchange(payload)
     mixed, token_grad, affinity_grad = combine(ids, keep, affinity_t, planned, rows)
     return mixed, token_grad, affinity_grad.T

time: 121 us -> 120 us (level)
  waiting for transfers between devices: 16.3 us -> 12.3 us
  starting transfers between devices: 5.14 us -> 7.55 us
    ppermute x14 -> x18, waiting for transfers between devices: 16.3 us -> 12.3 us  [swap(): return lax.ppermute(values, 'local', [(i, i ^ distance) for i in range(4)])]
    ppermute x14 -> x18, starting transfers between devices: 5.14 us -> 7.55 us  [swap(): return lax.ppermute(values, 'local', [(i, i ^ distance) for i in range(4)])]
    pallas_call x3 -> x6, Pallas kernels: 2.24 us -> 3.56 us  [the longest x2 1.72 us: grad_sums(): pl.pallas_call(lambda *refs: grad_kernel(first, *refs), out_shape=shapes,...]
  transfers between devices with their start and end apart: 14 -> 18, of which waited for: 9 -> 14; matrix products, arithmetic and copies ran while one was open for 0% -> 0% of each run, Pallas kernels for 5% -> 7%
where the time goes in v5:
time: 120 us
  blocking collectives  81.5 us (68%)
  Pallas kernels  17.8 us (15%)
  waiting for transfers between devices  12.3 us (10%)
  starting transfers between devices  7.55 us (6%)
    all_to_all x2, blocking collectives, exchange(): lax.all_to_all(packed, 'node', split_axis=0, concat_axis=0, tiled=True)  81.5 us
    ppermute x18, waiting for transfers between devices, swap(): return lax.ppermute(values, 'local', [(i, i ^ distance) for i in range(4)])  12.3 us
    ppermute x18, starting transfers between devices, swap(): return lax.ppermute(values, 'local', [(i, i ^ distance) for i in range(4)])  7.55 us
    pallas_call x1, Pallas kernels, send_rows(): pl.pallas_call(send_kernel, out_shape=jax.ShapeDtypeStruct((ROWS, SENT),...  3.83 us
    pallas_call x2, Pallas kernels, partial_sums(): pl.pallas_call(lambda *refs: partial_kernel(first, at, *refs), out_shape=...  2.88 us
    pallas_call x1, Pallas kernels, combine(): pl.pallas_call(combine_kernel, out_shape=(jax.ShapeDtypeStruct((TOK, WIDT...  2.5 us
  transfers between devices with their start and end apart: 18, of which 14 were waited for; matrix products, arithmetic and copies ran while one was open for 0% of the time, Pallas kernels for 7%

profile of v5, /device:TPU:0, one launch (start us, length us, event | category | flops | bytes accessed | tf_op | source)
XLA Modules:
  0.0 120.2 jit_solution(11196711754537769757)
XLA Ops:
  0.6 3.8 %send_rows.1 = bf16[256,4480]{1,0:T(8,128)(2,1)} custom-call(s32[8,256]{1,0:T(8,128)} %bitcast.28, s32[8,256]{1,0:T(8,128)} %bitcast.31, f32[8,256]{1,0:T(8,128)} %bitcast.34, bf16[256,1792]{1,0:T(8,128)(2,1)} %refs_3_.1, bf16[256,1792]{1,0:T(8,128)(2,1)} %refs_4_.1), custom_call_target="tpu_custom_call" | custom-call | flops 939524096 | bytes 5505024 | tf_op jit(solution)/shard_map/send_rows/pallas_call | solution.py:157
  4.5 0.0 copy-start
  4.5 0.0 copy-start.2
  4.5 43.8 %all_to_all.22 = bf16[32,8,4480]{2,1,0:T(8,128)(2,1)S(1)} all-to-all(bf16[32,8,4480]{2,1,0:T(8,128)(2,1)} %bitcast.37), channel_id=1, replica_groups=mesh['node'=32,'local'=4] {'node'}, dimensions={0} | all-to-all | bytes 4587520 | tf_op jit(solution)/shard_map/all_to_all | solution.py:547
  48.3 0.0 copy-done
  48.3 0.9 grad_a.1
  49.3 0.1 collective-permute-start
  49.4 1.4 %collective-permute-done.refs_0_ = bf16[160,512]{1,0:T(8,128)(2,1)S(1)} collective-permute-done((bf16[160,512]{1,0:T(8,128)(2,1)S(1)}, bf16[160,512]{1,0:T(8,128)(2,1)S(1)}, u32[]{:S(2)}, u32[]{:S(2)}) %collective-permute-start) | collective-permute-done | bytes 163872 | tf_op jit(solution)/shard_map/ppermute | solution.py:551
  50.8 0.1 add_ga.1
  50.8 0.7 collective-permute-start.1
  51.5 0.0 copy-done.2
  51.5 0.0 copy-done.1
  51.5 1.5 %pre_a.1 = (f32[160,1024]{1,0:T(8,128)S(1)}, bf16[160,256]{1,0:T(8,128)(2,1)S(1)}, bf16[160,256]{1,0:T(8,128)(2,1)S(1)}, bf16[160,256]{1,0:T(8,128)(2,1)S(1)}, b...) custom-call(s32[1]{0:T(128)} %bitcast.3.refs_0_.core_ref, bf16[256,4480]{1,0:T(8,128)(2,1)S(1)} %bitcast.25, ...), custom_call_target="tpu_custom_call" | custom-call | flops 1000000 | bytes 10000 | tf_op jit(solution)/shard_map/pre_a/pallas_call | solution.py:214
  53.0 0.1 collective-permute-start.5
  53.1 0.5 collective-permute-start.6
  53.6 0.1 collective-permute-start.7
  53.7 0.4 collective-permute-start.8
  54.1 0.3 collective-permute-done.5.refs_0_
  54.4 0.2 collective-permute-done.6.refs_1_
  54.6 0.4 collective-permute-done.7.refs_2_
  54.9 0.2 collective-permute-done.8.refs_3_
  55.1 0.1 add_a.1
  55.2 1.5 %collective-permute-start.10 = (bf16[160,1024]{1,0:T(8,128)(2,1)S(1)}, bf16[160,1024]{1,0:T(8,128)(2,1)S(1)}, u32[]{:S(2)}, u32[]{:S(2)}) collective-permute-start(bf16[160,1024]{1,0:T(8,128)(2,1)S(1)} %get-tuple-element.83), channel_id=1, source_target_pairs={{0,2},{1,3},{2,0},{3,1},{4,6},{5,7},{6,4},{7,5},{8,10},{9,11},{10,... | collective-permute-start | bytes 983048 | tf_op jit(solution)/shard_map/ppermute | solution.py:551
  56.6 0.5 collective-permute-done.1.grad_recv_ref
  57.1 1.4 %pre_b.1 = (f32[160,1024]{1,0:T(8,128)S(1)}, bf16[160,512]{1,0:T(8,128)(2,1)S(1)}, bf16[160,512]{1,0:T(8,128)(2,1)S(1)}) custom-call(s32[1]{0:T(128)} %bitcast.3.refs_0_.core_ref, bf16[320,1792]{1,0:T(8,128)(2,1)S(1)} %get-tuple-element.67.refs_1_, bf16[1792,1024]{1,0:T(8,128)(2,1)S(1)} %bitcast.17, bf16[1792,1024]{1,0:T(8,128)(2,1)S(1)} %bitcast.21), custom_call_target="tpu_custom_call" | custom-call | flops 1000000 | bytes 10000 | tf_op jit(solution)/shard_map/pre_b/pallas_call | solution.py:214
  58.5 0.1 collective-permute-start.2
  58.6 0.5 collective-permute-start.3
  59.1 0.8 grad_b.1
  59.9 0.0 copy-start.3
  59.9 0.0 copy-start.4
  59.9 0.0 copy-start.5
  59.9 0.2 collective-permute-start.9
  60.1 0.0 collective-permute-done.2.refs_0_
  60.1 0.1 collective-permute-done.3.refs_1_
  60.2 0.1 add_b.1
  60.3 0.7 collective-permute-start.4
  61.0 0.4 collective-permute-done.9.refs_0_
  61.5 4.3 %collective-permute-done.10.recv_ref = bf16[160,1024]{1,0:T(8,128)(2,1)S(1)} collective-permute-done((bf16[160,1024]{1,0:T(8,128)(2,1)S(1)}, bf16[160,1024]{1,0:T(8,128)(2,1)S(1)}, u32[]{:S(2)}, u32[]{:S(2)}) %collective-permute-start.10) | collective-permute-done | bytes 327712 | tf_op jit(solution)/shard_map/ppermute | solution.py:551
  65.8 0.3 block_a.1
  66.1 0.0 collective-permute-start.11
  66.1 0.5 collective-permute-start.12
  66.6 0.1 collective-permute-start.13
  66.7 1.4 %collective-permute-start.14 = (bf16[160,512]{1,0:T(8,128)(2,1)S(1)}, bf16[160,512]{1,0:T(8,128)(2,1)S(1)}, u32[]{:S(2)}, u32[]{:S(2)}) collective-permute-start(bf16[160,512]{1,0:T(8,128)(2,1)S(1)} %get-tuple-element.104), channel_id=1, source_target_pairs={{0,2},{1,3},{2,0},{3,1},{4,6},{5,7},{6,4},{7,5},{8,10},{9,11},{10,... | collective-permute-start | bytes 491528 | tf_op jit(solution)/shard_map/ppermute | solution.py:551
  68.1 0.0 copy-done.3
  68.1 0.0 copy-done.4
  68.1 0.6 plan.1
  68.7 0.0 collective-permute-done.11.refs_3_
  68.7 0.0 collective-permute-done.12.refs_4_
  68.7 0.0 collective-permute-done.13.refs_5_
  68.7 2.2 %spread_a.1 = (f32[320,1792]{1,0:T(8,128)S(1)}, f32[320,1792]{1,0:T(8,128)S(1)}) custom-call(bf16[160,512]{1,0:T(8,128)(2,1)S(1)} %get-tuple-element.86.refs_0_, bf16[160,512]{1,0:T(8,128)(2,1)S(1)} %get-tuple-element.87.refs_1_, bf16[160,512]{1,0:T(8,128)(2,1)S(1)} %get-tuple-element.88.refs_2_, bf16[160,512]{1,0:T(8,128)(2,1)S(1)} %collective-permute-done.11.refs_3_, ...), custom_call_target="tpu_custom_call" | custom-call | flops 1000000 | bytes 10000 | tf_op jit(solution)/shard_map/spread_a/pallas_call | solution.py:278
  70.9 1.9 %collective-permute-done.4.recv_ref = bf16[160,1024]{1,0:T(8,128)(2,1)S(1)} collective-permute-done((bf16[160,1024]{1,0:T(8,128)(2,1)S(1)}, bf16[160,1024]{1,0:T(8,128)(2,1)S(1)}, u32[]{:S(2)}, u32[]{:S(2)}) %collective-permute-start.4) | collective-permute-done | bytes 327712 | tf_op jit(solution)/shard_map/ppermute | solution.py:551
  72.8 0.1 hidden_b.1
  72.9 0.1 collective-permute-start.15
  73.0 0.5 collective-permute-start.16
  73.5 0.8 collective-permute-done.15.refs_2_
  74.3 0.3 collective-permute-done.16.refs_3_
  74.5 1.0 spread_out.1.out_rows_ref
  75.6 0.2 collective-permute-done.14.grad_recv_ref
  75.8 0.4 pair_b.1.own_ref
  76.1 0.1 collective-permute-start.17
  76.3 1.6 %collective-permute-done.17.peer_ref = bf16[160,1152]{1,0:T(8,128)(2,1)S(1)} collective-permute-done((bf16[160,1152]{1,0:T(8,128)(2,1)S(1)}, bf16[160,1152]{1,0:T(8,128)(2,1)S(1)}, u32[]{:S(2)}, u32[]{:S(2)}) %collective-permute-start.17) | collective-permute-done | bytes 368672 | tf_op jit(solution)/shard_map/ppermute | solution.py:551
  77.9 2.0 %spread_b.1 = bf16[256,4608]{1,0:T(8,128)(2,1)S(1)} custom-call(s32[1]{0:T(128)} %bitcast.3.refs_0_.core_ref, bf16[160,1152]{1,0:T(8,128)(2,1)S(1)} %pair_b.1.own_ref, bf16[160,1152]{1,0:T(8,128)(2,1)S(1)} %collective-permute-done.17.peer_ref, bf16[1792,1024]{1,0:T(8,128)(2,1)S(1)} %bitcast.19, bf16[1792,1024]{1,0:T(8,128)(2,1)S(1)} %bitcast.23, ...), custom_call_target="tpu_custom_call" | custom-call | flops 1000000 | bytes 10000 | tf_op jit(solution)/shard_map/spread_b/pallas_call | solution.py:370
  79.8 37.7 %all_to_all.23 = bf16[32,8,4608]{2,1,0:T(8,128)(2,1)S(1)} all-to-all(bf16[32,8,4608]{2,1,0:T(8,128)(2,1)S(1)} %bitcast.26), channel_id=1, replica_groups=mesh['node'=32,'local'=4] {'node'}, dimensions={0} | all-to-all | bytes 4718592 | tf_op jit(solution)/shard_map/all_to_all | solution.py:547
  117.6 2.5 %combine.1 = (bf16[256,1792]{1,0:T(8,128)(2,1)}, bf16[256,1792]{1,0:T(8,128)(2,1)}, f32[8,256]{1,0:T(8,128)}) custom-call(s32[8,256]{1,0:T(8,128)S(1)} %bitcast.30, s32[8,256]{1,0:T(8,128)S(1)} %bitcast.33, f32[8,256]{1,0:T(8,128)S(1)} %bitcast.36, bf16[4,256,256]{2,1,0:T(8,128)(2,1)S(1)} %get-tuple-element.98.places_ref, ...), custom_call_target="tpu_custom_call" | custom-call | flops 939524096 | bytes 3670016 | tf_op jit(solution)/shard_map/combine/pallas_call | solution.py:527
  (3 shorter events, 0.0 us)
Async XLA Ops:
  4.5 43.9 %copy-start = (bf16[1,1024,1792]{2,1,0:T(8,128)(2,1)S(1)}, bf16[1,1024,1792]{2,1,0:T(8,128)(2,1)}, u32[]{:S(2)}) copy-start(bf16[1,1024,1792]{2,1,0:T(8,128)(2,1)} %param.14) | copy-start | bytes 11010052
  4.5 47.0 %copy-start.2 = (bf16[1,1792,1024]{2,1,0:T(8,128)(2,1)S(1)}, bf16[1,1792,1024]{2,1,0:T(8,128)(2,1)}, u32[]{:S(2)}) copy-start(bf16[1,1792,1024]{2,1,0:T(8,128)(2,1)} %param.13) | copy-start | bytes 11010052
  48.3 3.2 %copy-start.1 = (bf16[1,1792,1024]{2,1,0:T(8,128)(2,1)S(1)}, bf16[1,1792,1024]{2,1,0:T(8,128)(2,1)}, u32[]{:S(2)}) copy-start(bf16[1,1792,1024]{2,1,0:T(8,128)(2,1)} %param.12) | copy-start | bytes 11010052
  49.3 1.5 %collective-permute-start = (bf16[160,512]{1,0:T(8,128)(2,1)S(1)}, bf16[160,512]{1,0:T(8,128)(2,1)S(1)}, u32[]{:S(2)}, u32[]{:S(2)}) collective-permute-start(bf16[160,512]{1,0:T(8,128)(2,1)S(1)} %get-tuple-element.62), channel_id=1, source_target_pairs={{0,1},{1,0},{2,3},{3,2},{4,5},{5,4},{6,7},{7,6},{8,9},{9,8},{10,11... | collective-permute-start | bytes 491528 | tf_op jit(solution)/shard_map/ppermute | solution.py:551
  50.8 6.3 %collective-permute-start.1 = (bf16[160,512]{1,0:T(8,128)(2,1)S(1)}, bf16[160,512]{1,0:T(8,128)(2,1)S(1)}, u32[]{:S(2)}, u32[]{:S(2)}) collective-permute-start(bf16[160,512]{1,0:T(8,128)(2,1)S(1)} %get-tuple-element.66), channel_id=1, source_target_pairs={{0,2},{1,3},{2,0},{3,1},{4,6},{5,7},{6,4},{7,5},{8,10},{9,11},{10,... | collective-permute-start | bytes 491528 | tf_op jit(solution)/shard_map/ppermute | solution.py:551
  53.0 1.4 %collective-permute-start.5 = (bf16[160,256]{1,0:T(8,128)(2,1)S(1)}, bf16[160,256]{1,0:T(8,128)(2,1)S(1)}, u32[]{:S(2)}, u32[]{:S(2)}) collective-permute-start(bf16[160,256]{1,0:T(8,128)(2,1)S(1)} %get-tuple-element.73), channel_id=1, source_target_pairs={{0,1},{1,0},{2,3},{3,2},{4,5},{5,4},{6,7},{7,6},{8,9},{9,8},{10,11... | collective-permute-start | bytes 245768 | tf_op jit(solution)/shard_map/ppermute | solution.py:551
  53.1 1.4 %collective-permute-start.6 = (bf16[160,256]{1,0:T(8,128)(2,1)S(1)}, bf16[160,256]{1,0:T(8,128)(2,1)S(1)}, u32[]{:S(2)}, u32[]{:S(2)}) collective-permute-start(bf16[160,256]{1,0:T(8,128)(2,1)S(1)} %get-tuple-element.74), channel_id=1, source_target_pairs={{0,1},{1,0},{2,3},{3,2},{4,5},{5,4},{6,7},{7,6},{8,9},{9,8},{10,11... | collective-permute-start | bytes 245768 | tf_op jit(solution)/shard_map/ppermute | solution.py:551
  53.6 1.3 %collective-permute-start.7 = (bf16[160,256]{1,0:T(8,128)(2,1)S(1)}, bf16[160,256]{1,0:T(8,128)(2,1)S(1)}, u32[]{:S(2)}, u32[]{:S(2)}) collective-permute-start(bf16[160,256]{1,0:T(8,128)(2,1)S(1)} %get-tuple-element.75), channel_id=1, source_target_pairs={{0,1},{1,0},{2,3},{3,2},{4,5},{5,4},{6,7},{7,6},{8,9},{9,8},{10,11... | collective-permute-start | bytes 245768 | tf_op jit(solution)/shard_map/ppermute | solution.py:551
  53.7 1.3 %collective-permute-start.8 = (bf16[160,256]{1,0:T(8,128)(2,1)S(1)}, bf16[160,256]{1,0:T(8,128)(2,1)S(1)}, u32[]{:S(2)}, u32[]{:S(2)}) collective-permute-start(bf16[160,256]{1,0:T(8,128)(2,1)S(1)} %get-tuple-element.76), channel_id=1, source_target_pairs={{0,1},{1,0},{2,3},{3,2},{4,5},{5,4},{6,7},{7,6},{8,9},{9,8},{10,11... | collective-permute-start | bytes 245768 | tf_op jit(solution)/shard_map/ppermute | solution.py:551
  55.2 10.6 %collective-permute-start.10 = (bf16[160,1024]{1,0:T(8,128)(2,1)S(1)}, bf16[160,1024]{1,0:T(8,128)(2,1)S(1)}, u32[]{:S(2)}, u32[]{:S(2)}) collective-permute-start(bf16[160,1024]{1,0:T(8,128)(2,1)S(1)} %get-tuple-element.83), channel_id=1, source_target_pairs={{0,2},{1,3},{2,0},{3,1},{4,6},{5,7},{6,4},{7,5},{8,10},{9,11},{10,... | collective-permute-start | bytes 983048 | tf_op jit(solution)/shard_map/ppermute | solution.py:551
  58.5 1.6 %collective-permute-start.2 = (bf16[160,512]{1,0:T(8,128)(2,1)S(1)}, bf16[160,512]{1,0:T(8,128)(2,1)S(1)}, u32[]{:S(2)}, u32[]{:S(2)}) collective-permute-start(bf16[160,512]{1,0:T(8,128)(2,1)S(1)} %get-tuple-element.69), channel_id=1, source_target_pairs={{0,1},{1,0},{2,3},{3,2},{4,5},{5,4},{6,7},{7,6},{8,9},{9,8},{10,11... | collective-permute-start | bytes 491528 | tf_op jit(solution)/shard_map/ppermute | solution.py:551
  58.6 1.6 %collective-permute-start.3 = (bf16[160,512]{1,0:T(8,128)(2,1)S(1)}, bf16[160,512]{1,0:T(8,128)(2,1)S(1)}, u32[]{:S(2)}, u32[]{:S(2)}) collective-permute-start(bf16[160,512]{1,0:T(8,128)(2,1)S(1)} %get-tuple-element.70), channel_id=1, source_target_pairs={{0,1},{1,0},{2,3},{3,2},{4,5},{5,4},{6,7},{7,6},{8,9},{9,8},{10,11... | collective-permute-start | bytes 491528 | tf_op jit(solution)/shard_map/ppermute | solution.py:551
  59.9 8.2 %copy-start.3 = (s32[256,8]{0,1:T(8,128)S(1)}, s32[256,8]{0,1:T(8,128)}, u32[]{:S(2)}) copy-start(s32[256,8]{0,1:T(8,128)} %param.9) | copy-start | bytes 24580
  59.9 8.2 %copy-start.4 = (s32[256,8]{0,1:T(8,128)S(1)}, s32[256,8]{0,1:T(8,128)}, u32[]{:S(2)}) copy-start(s32[256,8]{0,1:T(8,128)} %param.10) | copy-start | bytes 24580
  59.9 8.2 %copy-start.5 = (f32[256,8]{0,1:T(8,128)S(1)}, f32[256,8]{0,1:T(8,128)}, u32[]{:S(2)}) copy-start(f32[256,8]{0,1:T(8,128)} %param.11) | copy-start | bytes 24580
  59.9 1.5 %collective-permute-start.9 = (bf16[160,512]{1,0:T(8,128)(2,1)S(1)}, bf16[160,512]{1,0:T(8,128)(2,1)S(1)}, u32[]{:S(2)}, u32[]{:S(2)}) collective-permute-start(bf16[160,512]{1,0:T(8,128)(2,1)S(1)} %get-tuple-element.80), channel_id=1, source_target_pairs={{0,1},{1,0},{2,3},{3,2},{4,5},{5,4},{6,7},{7,6},{8,9},{9,8},{10,11... | collective-permute-start | bytes 491528 | tf_op jit(solution)/shard_map/ppermute | solution.py:551
  60.3 12.5 %collective-permute-start.4 = (bf16[160,1024]{1,0:T(8,128)(2,1)S(1)}, bf16[160,1024]{1,0:T(8,128)(2,1)S(1)}, u32[]{:S(2)}, u32[]{:S(2)}) collective-permute-start(bf16[160,1024]{1,0:T(8,128)(2,1)S(1)} %get-tuple-element.71), channel_id=1, source_target_pairs={{0,2},{1,3},{2,0},{3,1},{4,6},{5,7},{6,4},{7,5},{8,10},{9,11},{10,... | collective-permute-start | bytes 983048 | tf_op jit(solution)/shard_map/ppermute | solution.py:551
  66.1 2.6 %collective-permute-start.11 = (bf16[160,512]{1,0:T(8,128)(2,1)S(1)}, bf16[160,512]{1,0:T(8,128)(2,1)S(1)}, u32[]{:S(2)}, u32[]{:S(2)}) collective-permute-start(bf16[160,512]{1,0:T(8,128)(2,1)S(1)} %get-tuple-element.86.refs_0_), channel_id=1, source_target_pairs={{0,1},{1,0},{2,3},{3,2},{4,5},{5,4},{6,7},{7,6},{8,9},{9,8},{10,11... | collective-permute-start | bytes 491528 | tf_op jit(solution)/shard_map/ppermute | solution.py:551
  66.1 2.6 %collective-permute-start.12 = (bf16[160,512]{1,0:T(8,128)(2,1)S(1)}, bf16[160,512]{1,0:T(8,128)(2,1)S(1)}, u32[]{:S(2)}, u32[]{:S(2)}) collective-permute-start(bf16[160,512]{1,0:T(8,128)(2,1)S(1)} %get-tuple-element.87.refs_1_), channel_id=1, source_target_pairs={{0,1},{1,0},{2,3},{3,2},{4,5},{5,4},{6,7},{7,6},{8,9},{9,8},{10,11... | collective-permute-start | bytes 491528 | tf_op jit(solution)/shard_map/ppermute | solution.py:551
  66.6 2.1 %collective-permute-start.13 = (bf16[160,512]{1,0:T(8,128)(2,1)S(1)}, bf16[160,512]{1,0:T(8,128)(2,1)S(1)}, u32[]{:S(2)}, u32[]{:S(2)}) collective-permute-start(bf16[160,512]{1,0:T(8,128)(2,1)S(1)} %get-tuple-element.88.refs_2_), channel_id=1, source_target_pairs={{0,1},{1,0},{2,3},{3,2},{4,5},{5,4},{6,7},{7,6},{8,9},{9,8},{10,11... | collective-permute-start | bytes 491528 | tf_op jit(solution)/shard_map/ppermute | solution.py:551
  66.7 9.0 %collective-permute-start.14 = (bf16[160,512]{1,0:T(8,128)(2,1)S(1)}, bf16[160,512]{1,0:T(8,128)(2,1)S(1)}, u32[]{:S(2)}, u32[]{:S(2)}) collective-permute-start(bf16[160,512]{1,0:T(8,128)(2,1)S(1)} %get-tuple-element.104), channel_id=1, source_target_pairs={{0,2},{1,3},{2,0},{3,1},{4,6},{5,7},{6,4},{7,5},{8,10},{9,11},{10,... | collective-permute-start | bytes 491528 | tf_op jit(solution)/shard_map/ppermute | solution.py:551
  72.9 1.4 %collective-permute-start.15 = (bf16[160,256]{1,0:T(8,128)(2,1)S(1)}, bf16[160,256]{1,0:T(8,128)(2,1)S(1)}, u32[]{:S(2)}, u32[]{:S(2)}) collective-permute-start(bf16[160,256]{1,0:T(8,128)(2,1)S(1)} %get-tuple-element.105.refs_0_), channel_id=1, source_target_pairs={{0,1},{1,0},{2,3},{3,2},{4,5},{5,4},{6,7},{7,6},{8,9},{9,8},{10,11... | collective-permute-start | bytes 245768 | tf_op jit(solution)/shard_map/ppermute | solution.py:551
  73.0 1.5 %collective-permute-start.16 = (bf16[160,256]{1,0:T(8,128)(2,1)S(1)}, bf16[160,256]{1,0:T(8,128)(2,1)S(1)}, u32[]{:S(2)}, u32[]{:S(2)}) collective-permute-start(bf16[160,256]{1,0:T(8,128)(2,1)S(1)} %get-tuple-element.106.refs_1_), channel_id=1, source_target_pairs={{0,1},{1,0},{2,3},{3,2},{4,5},{5,4},{6,7},{7,6},{8,9},{9,8},{10,11... | collective-permute-start | bytes 245768 | tf_op jit(solution)/shard_map/ppermute | solution.py:551
  76.1 1.7 %collective-permute-start.17 = (bf16[160,1152]{1,0:T(8,128)(2,1)S(1)}, bf16[160,1152]{1,0:T(8,128)(2,1)S(1)}, u32[]{:S(2)}, u32[]{:S(2)}) collective-permute-start(bf16[160,1152]{1,0:T(8,128)(2,1)S(1)} %pair_b.1.own_ref), channel_id=1, source_target_pairs={{0,1},{1,0},{2,3},{3,2},{4,5},{5,4},{6,7},{7,6},{8,9},{9,8},{10,11... | collective-permute-start | bytes 1105928 | tf_op jit(solution)/shard_map/ppermute | solution.py:551

commit v6 on v5

--- a/solution.py
+++ b/solution.py
@@ -142,7 +142,7 @@
 
 
 ROOMY = pltpu.CompilerParams(vmem_limit_bytes=60 * 2**20)
-LIMITED = pltpu.CompilerParams(vmem_limit_bytes=24 * 2**20)
+LIMITED = pltpu.CompilerParams(vmem_limit_bytes=32 * 2**20)
 
 
 def vmem(n):
@@ -197,18 +197,21 @@
     else:
         send_refs, rows_ref = rest, packed_ref
     span = slice(first, first + SPAN)
-    width = 2 * SPAN // len(send_refs)
+    sent = []
     for i, weight_ref in enumerate((gate_ref, up_ref)):
         product = dot(rows_ref[...], weight_ref[:, span])
-        sent = product[:HALF].astype(BF16)
-        for j in range(SPAN // width):
-            send_refs[i * SPAN // width + j][...] = sent[:, j * width : (j + 1) * width]
+        sent.append(product[:HALF].astype(BF16))
         keep_ref[:, i * SPAN : (i + 1) * SPAN] = product[HALF:]
+    sent = jnp.concatenate(sent, axis=1)
+    begin = 0
+    for send_ref in send_refs:
+        send_ref[...] = sent[:, begin : begin + send_ref.shape[1]]
+        begin += send_ref.shape[1]
 
 
 def partial_sums(name, core, packed, at, gate, up, first, pieces):
     shapes = (jax.ShapeDtypeStruct((HALF, 2 * SPAN), F32),)
-    shapes += (jax.ShapeDtypeStruct((HALF, 2 * SPAN // pieces), BF16),) * pieces
+    shapes += tuple(jax.ShapeDtypeStruct((HALF, width), BF16) for width in pieces)
     if at is not None:
         shapes += (jax.ShapeDtypeStruct((2 * HALF, WIDTH), BF16),)
     return pl.pallas_call(
@@ -564,11 +567,11 @@
     total_g, send_g = add_halves("add_ga", own_g, swap(send_g, 1))
     rows, send_g = lax.optimization_barrier((rows, send_g))
     recv_g = swap(send_g, 2)
-    own_a, *sends, unpacked = partial_sums("pre_a", core, rows, 0, w_gate, w_up, 0, 4)
+    own_a, *sends, unpacked = partial_sums("pre_a", core, rows, 0, w_gate, w_up, 0, (384, 384, 256))
     total_a, send_a = add_halves("add_a", own_a, *[swap(part, 1) for part in sends])
     recv_a = swap(send_a, 2)
     unpacked, recv_g = lax.optimization_barrier((unpacked, recv_g))
-    own_b, *sends = partial_sums("pre_b", core, unpacked, None, w_gate, w_up, SPAN, 2)
+    own_b, *sends = partial_sums("pre_b", core, unpacked, None, w_gate, w_up, SPAN, (SPAN, SPAN))
     total_b, send_b = add_halves("add_b", own_b, *[swap(part, 1) for part in sends])
     recv_b = swap(send_b, 2)
     send_h, own_h = grad_sums("grad_b", core, grad_rows, w_down, SPAN)

time: 120 us -> 120 us (level)
    ppermute x18 -> x17, starting transfers between devices: 7.55 us -> 7.28 us  [swap(): return lax.ppermute(values, 'local', [(i, i ^ distance) for i in range(4)])]
    ppermute x18 -> x17, waiting for transfers between devices: 12.3 us -> 12.3 us  [swap(): return lax.ppermute(values, 'local', [(i, i ^ distance) for i in range(4)])]
  transfers between devices with their start and end apart: 18 -> 17, of which waited for: 14 -> 10; matrix products, arithmetic and copies ran while one was open for 0% -> 0% of each run, Pallas kernels for 7% -> 7%
where the time goes in v6:
time: 120 us
  blocking collectives  81.6 us (68%)
  Pallas kernels  17.7 us (15%)
  waiting for transfers between devices  12.3 us (10%)
  starting transfers between devices  7.28 us (6%)
    all_to_all x2, blocking collectives, exchange(): lax.all_to_all(packed, 'node', split_axis=0, concat_axis=0, tiled=True)  81.6 us
    ppermute x17, waiting for transfers between devices, swap(): return lax.ppermute(values, 'local', [(i, i ^ distance) for i in range(4)])  12.3 us
    ppermute x17, starting transfers between devices, swap(): return lax.ppermute(values, 'local', [(i, i ^ distance) for i in range(4)])  7.28 us
    pallas_call x1, Pallas kernels, send_rows(): pl.pallas_call(send_kernel, out_shape=jax.ShapeDtypeStruct((ROWS, SENT),...  3.76 us
    pallas_call x2, Pallas kernels, partial_sums(): pl.pallas_call(lambda *refs: partial_kernel(first, at, *refs), out_shape=...  2.88 us
    pallas_call x1, Pallas kernels, combine(): pl.pallas_call(combine_kernel, out_shape=(jax.ShapeDtypeStruct((TOK, WIDT...  2.5 us
  transfers between devices with their start and end apart: 17, of which 10 were waited for; matrix products, arithmetic and copies ran while one was open for 0% of the time, Pallas kernels for 7%

profile of v6, /device:TPU:0, one launch (start us, length us, event | category | flops | bytes accessed | tf_op | source)
XLA Modules:
  0.0 120.0 jit_solution(6879395130014399062)
XLA Ops:
  0.6 3.8 %send_rows.1 = bf16[256,4480]{1,0:T(8,128)(2,1)} custom-call(s32[8,256]{1,0:T(8,128)} %bitcast.28, s32[8,256]{1,0:T(8,128)} %bitcast.31, f32[8,256]{1,0:T(8,128)} %bitcast.34, bf16[256,1792]{1,0:T(8,128)(2,1)} %refs_3_.1, bf16[256,1792]{1,0:T(8,128)(2,1)} %refs_4_.1), custom_call_target="tpu_custom_call" | custom-call | flops 939524096 | bytes 5505024 | tf_op jit(solution)/shard_map/send_rows/pallas_call | solution.py:157
  4.4 0.0 copy-start
  4.4 0.0 copy-start.2
  4.4 43.8 %all_to_all.22 = bf16[32,8,4480]{2,1,0:T(8,128)(2,1)S(1)} all-to-all(bf16[32,8,4480]{2,1,0:T(8,128)(2,1)} %bitcast.37), channel_id=1, replica_groups=mesh['node'=32,'local'=4] {'node'}, dimensions={0} | all-to-all | bytes 4587520 | tf_op jit(solution)/shard_map/all_to_all | solution.py:550
  48.3 0.0 copy-done
  48.3 0.0 copy-start.1
  48.3 0.9 grad_a.1
  49.2 0.1 collective-permute-start
  49.3 1.4 %collective-permute-done.refs_0_ = bf16[160,512]{1,0:T(8,128)(2,1)S(1)} collective-permute-done((bf16[160,512]{1,0:T(8,128)(2,1)S(1)}, bf16[160,512]{1,0:T(8,128)(2,1)S(1)}, u32[]{:S(2)}, u32[]{:S(2)}) %collective-permute-start) | collective-permute-done | bytes 163872 | tf_op jit(solution)/shard_map/ppermute | solution.py:554
  50.7 0.1 add_ga.1
  50.8 0.7 collective-permute-start.1
  51.5 0.0 copy-done.2
  51.5 0.0 copy-done.1
  51.5 1.5 %pre_a.1 = (f32[160,1024]{1,0:T(8,128)S(1)}, bf16[160,384]{1,0:T(8,128)(2,1)S(1)}, bf16[160,384]{1,0:T(8,128)(2,1)S(1)}, bf16[160,256]{1,0:T(8,128)(2,1)S(1)}, bf16[320,1792]{1,0:T(8,128)(2,1)S(1)}) custom-call(s32[1]{0:T(128)} %bitcast.3.refs_0_.core_ref, bf16[256,4480]{1,0:T(8,128)(2,1)S(1)} %bitcast.25, bf16[1792,1024]{1,0:T(8,128)(2,1)S(1)} %bitcast.16, ...), custom_call_target="tpu_custom_call" | custom-call | flops 1000000 | bytes 10000 | tf_op jit(solution)/shard_map/pre_a/pallas_call | solution.py:217
  53.0 0.1 collective-permute-start.5
  53.1 0.5 collective-permute-start.6
  53.6 0.1 collective-permute-start.7
  53.7 1.2 collective-permute-done.7.refs_2_
  54.9 0.0 collective-permute-done.5.refs_0_
  54.9 0.0 collective-permute-done.6.refs_1_
  54.9 0.1 add_a.1
  55.0 1.5 %collective-permute-start.9 = (bf16[160,1024]{1,0:T(8,128)(2,1)S(1)}, bf16[160,1024]{1,0:T(8,128)(2,1)S(1)}, u32[]{:S(2)}, u32[]{:S(2)}) collective-permute-start(bf16[160,1024]{1,0:T(8,128)(2,1)S(1)} %get-tuple-element.81), channel_id=1, source_target_pairs={{0,2},{1,3},{2,0},{3,1},{4,6},{5,7},{6,4},{7,5},{8,10},{9,11},{10,... | collective-permute-start | bytes 983048 | tf_op jit(solution)/shard_map/ppermute | solution.py:554
  56.4 0.7 collective-permute-done.1.grad_recv_ref
  57.1 1.4 %pre_b.1 = (f32[160,1024]{1,0:T(8,128)S(1)}, bf16[160,512]{1,0:T(8,128)(2,1)S(1)}, bf16[160,512]{1,0:T(8,128)(2,1)S(1)}) custom-call(s32[1]{0:T(128)} %bitcast.3.refs_0_.core_ref, bf16[320,1792]{1,0:T(8,128)(2,1)S(1)} %get-tuple-element.66.refs_1_, bf16[1792,1024]{1,0:T(8,128)(2,1)S(1)} %bitcast.17, bf16[1792,1024]{1,0:T(8,128)(2,1)S(1)} %bitcast.21), custom_call_target="tpu_custom_call" | custom-call | flops 1000000 | bytes 10000 | tf_op jit(solution)/shard_map/pre_b/pallas_call | solution.py:217
  58.5 0.1 collective-permute-start.2
  58.5 0.5 collective-permute-start.3
  59.0 0.8 grad_b.1
  59.8 0.0 copy-start.3
  59.8 0.0 copy-start.4
  59.9 0.0 copy-start.5
  59.9 0.2 collective-permute-start.8
  60.0 0.0 collective-permute-done.2.refs_0_
  60.0 0.1 collective-permute-done.3.refs_1_
  60.2 0.1 add_b.1
  60.3 0.7 collective-permute-start.4
  61.0 0.4 collective-permute-done.8.refs_0_
  61.4 4.2 %collective-permute-done.9.recv_ref = bf16[160,1024]{1,0:T(8,128)(2,1)S(1)} collective-permute-done((bf16[160,1024]{1,0:T(8,128)(2,1)S(1)}, bf16[160,1024]{1,0:T(8,128)(2,1)S(1)}, u32[]{:S(2)}, u32[]{:S(2)}) %collective-permute-start.9) | collective-permute-done | bytes 327712 | tf_op jit(solution)/shard_map/ppermute | solution.py:554
  65.6 0.3 block_a.1
  65.9 0.0 collective-permute-start.10
  65.9 0.5 collective-permute-start.11
  66.4 0.1 collective-permute-start.12
  66.5 1.4 %collective-permute-start.13 = (bf16[160,512]{1,0:T(8,128)(2,1)S(1)}, bf16[160,512]{1,0:T(8,128)(2,1)S(1)}, u32[]{:S(2)}, u32[]{:S(2)}) collective-permute-start(bf16[160,512]{1,0:T(8,128)(2,1)S(1)} %get-tuple-element.102), channel_id=1, source_target_pairs={{0,2},{1,3},{2,0},{3,1},{4,6},{5,7},{6,4},{7,5},{8,10},{9,11},{10,... | collective-permute-start | bytes 491528 | tf_op jit(solution)/shard_map/ppermute | solution.py:554
  67.9 0.0 copy-done.3
  67.9 0.0 copy-done.4
  67.9 0.0 copy-done.5
  67.9 0.6 plan.1
  68.5 0.0 collective-permute-done.10.refs_3_
  68.5 0.0 collective-permute-done.11.refs_4_
  68.5 0.0 collective-permute-done.12.refs_5_
  68.5 2.2 %spread_a.1 = (f32[320,1792]{1,0:T(8,128)S(1)}, f32[320,1792]{1,0:T(8,128)S(1)}) custom-call(bf16[160,512]{1,0:T(8,128)(2,1)S(1)} %get-tuple-element.84.refs_0_, bf16[160,512]{1,0:T(8,128)(2,1)S(1)} %get-tuple-element.85.refs_1_, bf16[160,512]{1,0:T(8,128)(2,1)S(1)} %get-tuple-element.86.refs_2_, bf16[160,512]{1,0:T(8,128)(2,1)S(1)} %collective-permute-done.10.refs_3_, ...), custom_call_target="tpu_custom_call" | custom-call | flops 1000000 | bytes 10000 | tf_op jit(solution)/shard_map/spread_a/pallas_call | solution.py:281
  70.7 1.9 %collective-permute-done.4.recv_ref = bf16[160,1024]{1,0:T(8,128)(2,1)S(1)} collective-permute-done((bf16[160,1024]{1,0:T(8,128)(2,1)S(1)}, bf16[160,1024]{1,0:T(8,128)(2,1)S(1)}, u32[]{:S(2)}, u32[]{:S(2)}) %collective-permute-start.4) | collective-permute-done | bytes 327712 | tf_op jit(solution)/shard_map/ppermute | solution.py:554
  72.6 0.1 hidden_b.1
  72.7 0.1 collective-permute-start.14
  72.8 0.5 collective-permute-start.15
  73.3 0.8 collective-permute-done.14.refs_2_
  74.1 0.3 collective-permute-done.15.refs_3_
  74.3 1.0 spread_out.1.out_rows_ref
  75.4 0.0 collective-permute-done.13.grad_recv_ref
  75.4 0.4 pair_b.1.own_ref
  75.8 0.3 collective-permute-start.16
  76.1 1.4 %collective-permute-done.16.peer_ref = bf16[160,1152]{1,0:T(8,128)(2,1)S(1)} collective-permute-done((bf16[160,1152]{1,0:T(8,128)(2,1)S(1)}, bf16[160,1152]{1,0:T(8,128)(2,1)S(1)}, u32[]{:S(2)}, u32[]{:S(2)}) %collective-permute-start.16) | collective-permute-done | bytes 368672 | tf_op jit(solution)/shard_map/ppermute | solution.py:554
  77.5 2.0 %spread_b.1 = bf16[256,4608]{1,0:T(8,128)(2,1)S(1)} custom-call(s32[1]{0:T(128)} %bitcast.3.refs_0_.core_ref, bf16[160,1152]{1,0:T(8,128)(2,1)S(1)} %pair_b.1.own_ref, bf16[160,1152]{1,0:T(8,128)(2,1)S(1)} %collective-permute-done.16.peer_ref, bf16[1792,1024]{1,0:T(8,128)(2,1)S(1)} %bitcast.19, bf16[1792,1024]{1,0:T(8,128)(2,1)S(1)} %bitcast.23, ...), custom_call_target="tpu_custom_call" | custom-call | flops 1000000 | bytes 10000 | tf_op jit(solution)/shard_map/spread_b/pallas_call | solution.py:373
  79.5 37.8 %all_to_all.23 = bf16[32,8,4608]{2,1,0:T(8,128)(2,1)S(1)} all-to-all(bf16[32,8,4608]{2,1,0:T(8,128)(2,1)S(1)} %bitcast.26), channel_id=1, replica_groups=mesh['node'=32,'local'=4] {'node'}, dimensions={0} | all-to-all | bytes 4718592 | tf_op jit(solution)/shard_map/all_to_all | solution.py:550
  117.3 2.5 %combine.1 = (bf16[256,1792]{1,0:T(8,128)(2,1)}, bf16[256,1792]{1,0:T(8,128)(2,1)}, f32[8,256]{1,0:T(8,128)}) custom-call(s32[8,256]{1,0:T(8,128)S(1)} %bitcast.30, s32[8,256]{1,0:T(8,128)S(1)} %bitcast.33, f32[8,256]{1,0:T(8,128)S(1)} %bitcast.36, bf16[4,256,256]{2,1,0:T(8,128)(2,1)S(1)} %get-tuple-element.96.places_ref, ...), custom_call_target="tpu_custom_call" | custom-call | flops 939524096 | bytes 3670016 | tf_op jit(solution)/shard_map/combine/pallas_call | solution.py:530
  (1 shorter events, 0.0 us)
Async XLA Ops:
  4.4 43.9 %copy-start = (bf16[1,1024,1792]{2,1,0:T(8,128)(2,1)S(1)}, bf16[1,1024,1792]{2,1,0:T(8,128)(2,1)}, u32[]{:S(2)}) copy-start(bf16[1,1024,1792]{2,1,0:T(8,128)(2,1)} %param.14) | copy-start | bytes 11010052
  4.4 47.0 %copy-start.2 = (bf16[1,1792,1024]{2,1,0:T(8,128)(2,1)S(1)}, bf16[1,1792,1024]{2,1,0:T(8,128)(2,1)}, u32[]{:S(2)}) copy-start(bf16[1,1792,1024]{2,1,0:T(8,128)(2,1)} %param.13) | copy-start | bytes 11010052
  48.3 3.2 %copy-start.1 = (bf16[1,1792,1024]{2,1,0:T(8,128)(2,1)S(1)}, bf16[1,1792,1024]{2,1,0:T(8,128)(2,1)}, u32[]{:S(2)}) copy-start(bf16[1,1792,1024]{2,1,0:T(8,128)(2,1)} %param.12) | copy-start | bytes 11010052
  49.2 1.5 %collective-permute-start = (bf16[160,512]{1,0:T(8,128)(2,1)S(1)}, bf16[160,512]{1,0:T(8,128)(2,1)S(1)}, u32[]{:S(2)}, u32[]{:S(2)}) collective-permute-start(bf16[160,512]{1,0:T(8,128)(2,1)S(1)} %get-tuple-element.61), channel_id=1, source_target_pairs={{0,1},{1,0},{2,3},{3,2},{4,5},{5,4},{6,7},{7,6},{8,9},{9,8},{10,11... | collective-permute-start | bytes 491528 | tf_op jit(solution)/shard_map/ppermute | solution.py:554
  50.8 6.3 %collective-permute-start.1 = (bf16[160,512]{1,0:T(8,128)(2,1)S(1)}, bf16[160,512]{1,0:T(8,128)(2,1)S(1)}, u32[]{:S(2)}, u32[]{:S(2)}) collective-permute-start(bf16[160,512]{1,0:T(8,128)(2,1)S(1)} %get-tuple-element.65), channel_id=1, source_target_pairs={{0,2},{1,3},{2,0},{3,1},{4,6},{5,7},{6,4},{7,5},{8,10},{9,11},{10,... | collective-permute-start | bytes 491528 | tf_op jit(solution)/shard_map/ppermute | solution.py:554
  53.0 1.9 %collective-permute-start.5 = (bf16[160,384]{1,0:T(8,128)(2,1)S(1)}, bf16[160,384]{1,0:T(8,128)(2,1)S(1)}, u32[]{:S(2)}, u32[]{:S(2)}) collective-permute-start(bf16[160,384]{1,0:T(8,128)(2,1)S(1)} %get-tuple-element.72), channel_id=1, source_target_pairs={{0,1},{1,0},{2,3},{3,2},{4,5},{5,4},{6,7},{7,6},{8,9},{9,8},{10,11... | collective-permute-start | bytes 368648 | tf_op jit(solution)/shard_map/ppermute | solution.py:554
  53.1 1.8 %collective-permute-start.6 = (bf16[160,384]{1,0:T(8,128)(2,1)S(1)}, bf16[160,384]{1,0:T(8,128)(2,1)S(1)}, u32[]{:S(2)}, u32[]{:S(2)}) collective-permute-start(bf16[160,384]{1,0:T(8,128)(2,1)S(1)} %get-tuple-element.73), channel_id=1, source_target_pairs={{0,1},{1,0},{2,3},{3,2},{4,5},{5,4},{6,7},{7,6},{8,9},{9,8},{10,11... | collective-permute-start | bytes 368648 | tf_op jit(solution)/shard_map/ppermute | solution.py:554
  53.6 1.3 %collective-permute-start.7 = (bf16[160,256]{1,0:T(8,128)(2,1)S(1)}, bf16[160,256]{1,0:T(8,128)(2,1)S(1)}, u32[]{:S(2)}, u32[]{:S(2)}) collective-permute-start(bf16[160,256]{1,0:T(8,128)(2,1)S(1)} %get-tuple-element.74), channel_id=1, source_target_pairs={{0,1},{1,0},{2,3},{3,2},{4,5},{5,4},{6,7},{7,6},{8,9},{9,8},{10,11... | collective-permute-start | bytes 245768 | tf_op jit(solution)/shard_map/ppermute | solution.py:554
  55.0 10.6 %collective-permute-start.9 = (bf16[160,1024]{1,0:T(8,128)(2,1)S(1)}, bf16[160,1024]{1,0:T(8,128)(2,1)S(1)}, u32[]{:S(2)}, u32[]{:S(2)}) collective-permute-start(bf16[160,1024]{1,0:T(8,128)(2,1)S(1)} %get-tuple-element.81), channel_id=1, source_target_pairs={{0,2},{1,3},{2,0},{3,1},{4,6},{5,7},{6,4},{7,5},{8,10},{9,11},{10,... | collective-permute-start | bytes 983048 | tf_op jit(solution)/shard_map/ppermute | solution.py:554
  58.5 1.6 %collective-permute-start.2 = (bf16[160,512]{1,0:T(8,128)(2,1)S(1)}, bf16[160,512]{1,0:T(8,128)(2,1)S(1)}, u32[]{:S(2)}, u32[]{:S(2)}) collective-permute-start(bf16[160,512]{1,0:T(8,128)(2,1)S(1)} %get-tuple-element.68), channel_id=1, source_target_pairs={{0,1},{1,0},{2,3},{3,2},{4,5},{5,4},{6,7},{7,6},{8,9},{9,8},{10,11... | collective-permute-start | bytes 491528 | tf_op jit(solution)/shard_map/ppermute | solution.py:554
  58.5 1.6 %collective-permute-start.3 = (bf16[160,512]{1,0:T(8,128)(2,1)S(1)}, bf16[160,512]{1,0:T(8,128)(2,1)S(1)}, u32[]{:S(2)}, u32[]{:S(2)}) collective-permute-start(bf16[160,512]{1,0:T(8,128)(2,1)S(1)} %get-tuple-element.69), channel_id=1, source_target_pairs={{0,1},{1,0},{2,3},{3,2},{4,5},{5,4},{6,7},{7,6},{8,9},{9,8},{10,11... | collective-permute-start | bytes 491528 | tf_op jit(solution)/shard_map/ppermute | solution.py:554
  59.8 8.1 %copy-start.3 = (s32[256,8]{0,1:T(8,128)S(1)}, s32[256,8]{0,1:T(8,128)}, u32[]{:S(2)}) copy-start(s32[256,8]{0,1:T(8,128)} %param.9) | copy-start | bytes 24580
  59.8 8.1 %copy-start.4 = (s32[256,8]{0,1:T(8,128)S(1)}, s32[256,8]{0,1:T(8,128)}, u32[]{:S(2)}) copy-start(s32[256,8]{0,1:T(8,128)} %param.10) | copy-start | bytes 24580
  59.9 8.1 %copy-start.5 = (f32[256,8]{0,1:T(8,128)S(1)}, f32[256,8]{0,1:T(8,128)}, u32[]{:S(2)}) copy-start(f32[256,8]{0,1:T(8,128)} %param.11) | copy-start | bytes 24580
  59.9 1.5 %collective-permute-start.8 = (bf16[160,512]{1,0:T(8,128)(2,1)S(1)}, bf16[160,512]{1,0:T(8,128)(2,1)S(1)}, u32[]{:S(2)}, u32[]{:S(2)}) collective-permute-start(bf16[160,512]{1,0:T(8,128)(2,1)S(1)} %get-tuple-element.78), channel_id=1, source_target_pairs={{0,1},{1,0},{2,3},{3,2},{4,5},{5,4},{6,7},{7,6},{8,9},{9,8},{10,11... | collective-permute-start | bytes 491528 | tf_op jit(solution)/shard_map/ppermute | solution.py:554
  60.3 12.4 %collective-permute-start.4 = (bf16[160,1024]{1,0:T(8,128)(2,1)S(1)}, bf16[160,1024]{1,0:T(8,128)(2,1)S(1)}, u32[]{:S(2)}, u32[]{:S(2)}) collective-permute-start(bf16[160,1024]{1,0:T(8,128)(2,1)S(1)} %get-tuple-element.70), channel_id=1, source_target_pairs={{0,2},{1,3},{2,0},{3,1},{4,6},{5,7},{6,4},{7,5},{8,10},{9,11},{10,... | collective-permute-start | bytes 983048 | tf_op jit(solution)/shard_map/ppermute | solution.py:554
  65.9 2.6 %collective-permute-start.10 = (bf16[160,512]{1,0:T(8,128)(2,1)S(1)}, bf16[160,512]{1,0:T(8,128)(2,1)S(1)}, u32[]{:S(2)}, u32[]{:S(2)}) collective-permute-start(bf16[160,512]{1,0:T(8,128)(2,1)S(1)} %get-tuple-element.84.refs_0_), channel_id=1, source_target_pairs={{0,1},{1,0},{2,3},{3,2},{4,5},{5,4},{6,7},{7,6},{8,9},{9,8},{10,11... | collective-permute-start | bytes 491528 | tf_op jit(solution)/shard_map/ppermute | solution.py:554
  65.9 2.6 %collective-permute-start.11 = (bf16[160,512]{1,0:T(8,128)(2,1)S(1)}, bf16[160,512]{1,0:T(8,128)(2,1)S(1)}, u32[]{:S(2)}, u32[]{:S(2)}) collective-permute-start(bf16[160,512]{1,0:T(8,128)(2,1)S(1)} %get-tuple-element.85.refs_1_), channel_id=1, source_target_pairs={{0,1},{1,0},{2,3},{3,2},{4,5},{5,4},{6,7},{7,6},{8,9},{9,8},{10,11... | collective-permute-start | bytes 491528 | tf_op jit(solution)/shard_map/ppermute | solution.py:554
  66.4 2.1 %collective-permute-start.12 = (bf16[160,512]{1,0:T(8,128)(2,1)S(1)}, bf16[160,512]{1,0:T(8,128)(2,1)S(1)}, u32[]{:S(2)}, u32[]{:S(2)}) collective-permute-start(bf16[160,512]{1,0:T(8,128)(2,1)S(1)} %get-tuple-element.86.refs_2_), channel_id=1, source_target_pairs={{0,1},{1,0},{2,3},{3,2},{4,5},{5,4},{6,7},{7,6},{8,9},{9,8},{10,11... | collective-permute-start | bytes 491528 | tf_op jit(solution)/shard_map/ppermute | solution.py:554
  66.5 8.9 %collective-permute-start.13 = (bf16[160,512]{1,0:T(8,128)(2,1)S(1)}, bf16[160,512]{1,0:T(8,128)(2,1)S(1)}, u32[]{:S(2)}, u32[]{:S(2)}) collective-permute-start(bf16[160,512]{1,0:T(8,128)(2,1)S(1)} %get-tuple-element.102), channel_id=1, source_target_pairs={{0,2},{1,3},{2,0},{3,1},{4,6},{5,7},{6,4},{7,5},{8,10},{9,11},{10,... | collective-permute-start | bytes 491528 | tf_op jit(solution)/shard_map/ppermute | solution.py:554
  72.7 1.4 %collective-permute-start.14 = (bf16[160,256]{1,0:T(8,128)(2,1)S(1)}, bf16[160,256]{1,0:T(8,128)(2,1)S(1)}, u32[]{:S(2)}, u32[]{:S(2)}) collective-permute-start(bf16[160,256]{1,0:T(8,128)(2,1)S(1)} %get-tuple-element.103.refs_0_), channel_id=1, source_target_pairs={{0,1},{1,0},{2,3},{3,2},{4,5},{5,4},{6,7},{7,6},{8,9},{9,8},{10,11... | collective-permute-start | bytes 245768 | tf_op jit(solution)/shard_map/ppermute | solution.py:554
  72.8 1.5 %collective-permute-start.15 = (bf16[160,256]{1,0:T(8,128)(2,1)S(1)}, bf16[160,256]{1,0:T(8,128)(2,1)S(1)}, u32[]{:S(2)}, u32[]{:S(2)}) collective-permute-start(bf16[160,256]{1,0:T(8,128)(2,1)S(1)} %get-tuple-element.104.refs_1_), channel_id=1, source_target_pairs={{0,1},{1,0},{2,3},{3,2},{4,5},{5,4},{6,7},{7,6},{8,9},{9,8},{10,11... | collective-permute-start | bytes 245768 | tf_op jit(solution)/shard_map/ppermute | solution.py:554
  75.8 1.7 %collective-permute-start.16 = (bf16[160,1152]{1,0:T(8,128)(2,1)S(1)}, bf16[160,1152]{1,0:T(8,128)(2,1)S(1)}, u32[]{:S(2)}, u32[]{:S(2)}) collective-permute-start(bf16[160,1152]{1,0:T(8,128)(2,1)S(1)} %pair_b.1.own_ref), channel_id=1, source_target_pairs={{0,1},{1,0},{2,3},{3,2},{4,5},{5,4},{6,7},{7,6},{8,9},{9,8},{10,11... | collective-permute-start | bytes 1105928 | tf_op jit(solution)/shard_map/ppermute | solution.py:554

commit v7 on v6

--- a/solution.py
+++ b/solution.py
@@ -347,11 +347,13 @@
     core = core_ref[0]
     rows_ref[:HALF] = own_ref[:, : 2 * SPAN]
     rows_ref[HALF:] = peer_ref[:, : 2 * SPAN]
-    packed_ref[:, :PACKED] = out_rows_ref[...]
 
     def product_of(cols):
         product = dot(rows_ref[:, :SPAN], gate_ref[cols, SPAN:], NT)
+        packed_ref[:, cols] = out_rows_ref[:, cols]
         return product + dot(rows_ref[:, SPAN:], up_ref[cols, SPAN:], NT)
+
+    packed_ref[:, WIDTH:PACKED] = out_rows_ref[:, WIDTH:]
 
     pack(core, product_of, sum_ref, packed_ref, PACKED)
     for half_ref, half in ((own_ref, core), (peer_ref, 1 - core)):

time: 120 us -> 120 us (level)
  no operation moved by 1% of the time
where the time goes in v7:
time: 120 us
  blocking collectives  81.6 us (68%)
  Pallas kernels  17.7 us (15%)
  waiting for transfers between devices  12.3 us (10%)
  starting transfers between devices  7.28 us (6%)
    all_to_all x2, blocking collectives, exchange(): lax.all_to_all(packed, 'node', split_axis=0, concat_axis=0, tiled=True)  81.6 us
    ppermute x17, waiting for transfers between devices, swap(): return lax.ppermute(values, 'local', [(i, i ^ distance) for i in range(4)])  12.3 us
    ppermute x17, starting transfers between devices, swap(): return lax.ppermute(values, 'local', [(i, i ^ distance) for i in range(4)])  7.28 us
    pallas_call x1, Pallas kernels, send_rows(): pl.pallas_call(send_kernel, out_shape=jax.ShapeDtypeStruct((ROWS, SENT),...  3.76 us
    pallas_call x2, Pallas kernels, partial_sums(): pl.pallas_call(lambda *refs: partial_kernel(first, at, *refs), out_shape=...  2.88 us
    pallas_call x1, Pallas kernels, combine(): pl.pallas_call(combine_kernel, out_shape=(jax.ShapeDtypeStruct((TOK, WIDT...  2.5 us
  transfers between devices with their start and end apart: 17, of which 10 were waited for; matrix products, arithmetic and copies ran while one was open for 0% of the time, Pallas kernels for 7%

profile of v7, /device:TPU:0, one launch (start us, length us, event | category | flops | bytes accessed | tf_op | source)
XLA Modules:
  0.0 120.0 jit_solution(5080366044651283341)
XLA Ops:
  0.6 3.8 %send_rows.1 = bf16[256,4480]{1,0:T(8,128)(2,1)} custom-call(s32[8,256]{1,0:T(8,128)} %bitcast.28, s32[8,256]{1,0:T(8,128)} %bitcast.31, f32[8,256]{1,0:T(8,128)} %bitcast.34, bf16[256,1792]{1,0:T(8,128)(2,1)} %refs_3_.1, bf16[256,1792]{1,0:T(8,128)(2,1)} %refs_4_.1), custom_call_target="tpu_custom_call" | custom-call | flops 939524096 | bytes 5505024 | tf_op jit(solution)/shard_map/send_rows/pallas_call | solution.py:157
  4.4 0.0 copy-start
  4.4 0.0 copy-start.2
  4.4 43.8 %all_to_all.22 = bf16[32,8,4480]{2,1,0:T(8,128)(2,1)S(1)} all-to-all(bf16[32,8,4480]{2,1,0:T(8,128)(2,1)} %bitcast.37), channel_id=1, replica_groups=mesh['node'=32,'local'=4] {'node'}, dimensions={0} | all-to-all | bytes 4587520 | tf_op jit(solution)/shard_map/all_to_all | solution.py:552
  48.3 0.0 copy-done
  48.3 0.0 copy-start.1
  48.3 0.9 grad_a.1
  49.2 0.1 collective-permute-start
  49.3 1.4 %collective-permute-done.refs_0_ = bf16[160,512]{1,0:T(8,128)(2,1)S(1)} collective-permute-done((bf16[160,512]{1,0:T(8,128)(2,1)S(1)}, bf16[160,512]{1,0:T(8,128)(2,1)S(1)}, u32[]{:S(2)}, u32[]{:S(2)}) %collective-permute-start) | collective-permute-done | bytes 163872 | tf_op jit(solution)/shard_map/ppermute | solution.py:556
  50.7 0.1 add_ga.1
  50.8 0.7 collective-permute-start.1
  51.5 0.0 copy-done.2
  51.5 0.0 copy-done.1
  51.5 1.5 %pre_a.1 = (f32[160,1024]{1,0:T(8,128)S(1)}, bf16[160,384]{1,0:T(8,128)(2,1)S(1)}, bf16[160,384]{1,0:T(8,128)(2,1)S(1)}, bf16[160,256]{1,0:T(8,128)(2,1)S(1)}, bf16[320,1792]{1,0:T(8,128)(2,1)S(1)}) custom-call(s32[1]{0:T(128)} %bitcast.3.refs_0_.core_ref, bf16[256,4480]{1,0:T(8,128)(2,1)S(1)} %bitcast.25, bf16[1792,1024]{1,0:T(8,128)(2,1)S(1)} %bitcast.16, ...), custom_call_target="tpu_custom_call" | custom-call | flops 1000000 | bytes 10000 | tf_op jit(solution)/shard_map/pre_a/pallas_call | solution.py:217
  53.0 0.1 collective-permute-start.5
  53.1 0.5 collective-permute-start.6
  53.6 0.1 collective-permute-start.7
  53.7 1.2 collective-permute-done.7.refs_2_
  54.9 0.0 collective-permute-done.5.refs_0_
  54.9 0.0 collective-permute-done.6.refs_1_
  54.9 0.1 add_a.1
  55.0 1.5 %collective-permute-start.9 = (bf16[160,1024]{1,0:T(8,128)(2,1)S(1)}, bf16[160,1024]{1,0:T(8,128)(2,1)S(1)}, u32[]{:S(2)}, u32[]{:S(2)}) collective-permute-start(bf16[160,1024]{1,0:T(8,128)(2,1)S(1)} %get-tuple-element.81), channel_id=1, source_target_pairs={{0,2},{1,3},{2,0},{3,1},{4,6},{5,7},{6,4},{7,5},{8,10},{9,11},{10,... | collective-permute-start | bytes 983048 | tf_op jit(solution)/shard_map/ppermute | solution.py:556
  56.4 0.7 collective-permute-done.1.grad_recv_ref
  57.1 1.4 %pre_b.1 = (f32[160,1024]{1,0:T(8,128)S(1)}, bf16[160,512]{1,0:T(8,128)(2,1)S(1)}, bf16[160,512]{1,0:T(8,128)(2,1)S(1)}) custom-call(s32[1]{0:T(128)} %bitcast.3.refs_0_.core_ref, bf16[320,1792]{1,0:T(8,128)(2,1)S(1)} %get-tuple-element.66.refs_1_, bf16[1792,1024]{1,0:T(8,128)(2,1)S(1)} %bitcast.17, bf16[1792,1024]{1,0:T(8,128)(2,1)S(1)} %bitcast.21), custom_call_target="tpu_custom_call" | custom-call | flops 1000000 | bytes 10000 | tf_op jit(solution)/shard_map/pre_b/pallas_call | solution.py:217
  58.5 0.1 collective-permute-start.2
  58.5 0.5 collective-permute-start.3
  59.0 0.8 grad_b.1
  59.8 0.0 copy-start.3
  59.8 0.0 copy-start.4
  59.9 0.0 copy-start.5
  59.9 0.2 collective-permute-start.8
  60.0 0.0 collective-permute-done.2.refs_0_
  60.0 0.1 collective-permute-done.3.refs_1_
  60.2 0.1 add_b.1
  60.3 0.7 collective-permute-start.4
  61.0 0.4 collective-permute-done.8.refs_0_
  61.4 4.2 %collective-permute-done.9.recv_ref = bf16[160,1024]{1,0:T(8,128)(2,1)S(1)} collective-permute-done((bf16[160,1024]{1,0:T(8,128)(2,1)S(1)}, bf16[160,1024]{1,0:T(8,128)(2,1)S(1)}, u32[]{:S(2)}, u32[]{:S(2)}) %collective-permute-start.9) | collective-permute-done | bytes 327712 | tf_op jit(solution)/shard_map/ppermute | solution.py:556
  65.6 0.3 block_a.1
  65.9 0.0 collective-permute-start.10
  65.9 0.5 collective-permute-start.11
  66.4 0.1 collective-permute-start.12
  66.5 1.4 %collective-permute-start.13 = (bf16[160,512]{1,0:T(8,128)(2,1)S(1)}, bf16[160,512]{1,0:T(8,128)(2,1)S(1)}, u32[]{:S(2)}, u32[]{:S(2)}) collective-permute-start(bf16[160,512]{1,0:T(8,128)(2,1)S(1)} %get-tuple-element.102), channel_id=1, source_target_pairs={{0,2},{1,3},{2,0},{3,1},{4,6},{5,7},{6,4},{7,5},{8,10},{9,11},{10,... | collective-permute-start | bytes 491528 | tf_op jit(solution)/shard_map/ppermute | solution.py:556
  67.9 0.0 copy-done.3
  67.9 0.0 copy-done.4
  67.9 0.0 copy-done.5
  67.9 0.6 plan.1
  68.5 0.0 collective-permute-done.10.refs_3_
  68.5 0.0 collective-permute-done.11.refs_4_
  68.5 0.0 collective-permute-done.12.refs_5_
  68.5 2.2 %spread_a.1 = (f32[320,1792]{1,0:T(8,128)S(1)}, f32[320,1792]{1,0:T(8,128)S(1)}) custom-call(bf16[160,512]{1,0:T(8,128)(2,1)S(1)} %get-tuple-element.84.refs_0_, bf16[160,512]{1,0:T(8,128)(2,1)S(1)} %get-tuple-element.85.refs_1_, bf16[160,512]{1,0:T(8,128)(2,1)S(1)} %get-tuple-element.86.refs_2_, bf16[160,512]{1,0:T(8,128)(2,1)S(1)} %collective-permute-done.10.refs_3_, ...), custom_call_target="tpu_custom_call" | custom-call | flops 1000000 | bytes 10000 | tf_op jit(solution)/shard_map/spread_a/pallas_call | solution.py:281
  70.7 1.9 %collective-permute-done.4.recv_ref = bf16[160,1024]{1,0:T(8,128)(2,1)S(1)} collective-permute-done((bf16[160,1024]{1,0:T(8,128)(2,1)S(1)}, bf16[160,1024]{1,0:T(8,128)(2,1)S(1)}, u32[]{:S(2)}, u32[]{:S(2)}) %collective-permute-start.4) | collective-permute-done | bytes 327712 | tf_op jit(solution)/shard_map/ppermute | solution.py:556
  72.6 0.1 hidden_b.1
  72.7 0.1 collective-permute-start.14
  72.8 0.5 collective-permute-start.15
  73.3 0.8 collective-permute-done.14.refs_2_
  74.1 0.3 collective-permute-done.15.refs_3_
  74.3 1.0 spread_out.1.out_rows_ref
  75.4 0.0 collective-permute-done.13.grad_recv_ref
  75.4 0.4 pair_b.1.own_ref
  75.8 0.3 collective-permute-start.16
  76.1 1.4 %collective-permute-done.16.peer_ref = bf16[160,1152]{1,0:T(8,128)(2,1)S(1)} collective-permute-done((bf16[160,1152]{1,0:T(8,128)(2,1)S(1)}, bf16[160,1152]{1,0:T(8,128)(2,1)S(1)}, u32[]{:S(2)}, u32[]{:S(2)}) %collective-permute-start.16) | collective-permute-done | bytes 368672 | tf_op jit(solution)/shard_map/ppermute | solution.py:556
  77.5 2.0 %spread_b.1 = bf16[256,4608]{1,0:T(8,128)(2,1)S(1)} custom-call(s32[1]{0:T(128)} %bitcast.3.refs_0_.core_ref, bf16[160,1152]{1,0:T(8,128)(2,1)S(1)} %pair_b.1.own_ref, bf16[160,1152]{1,0:T(8,128)(2,1)S(1)} %collective-permute-done.16.peer_ref, bf16[1792,1024]{1,0:T(8,128)(2,1)S(1)} %bitcast.19, bf16[1792,1024]{1,0:T(8,128)(2,1)S(1)} %bitcast.23, ...), custom_call_target="tpu_custom_call" | custom-call | flops 1000000 | bytes 10000 | tf_op jit(solution)/shard_map/spread_b/pallas_call | solution.py:375
  79.5 37.8 %all_to_all.23 = bf16[32,8,4608]{2,1,0:T(8,128)(2,1)S(1)} all-to-all(bf16[32,8,4608]{2,1,0:T(8,128)(2,1)S(1)} %bitcast.26), channel_id=1, replica_groups=mesh['node'=32,'local'=4] {'node'}, dimensions={0} | all-to-all | bytes 4718592 | tf_op jit(solution)/shard_map/all_to_all | solution.py:552
  117.3 2.5 %combine.1 = (bf16[256,1792]{1,0:T(8,128)(2,1)}, bf16[256,1792]{1,0:T(8,128)(2,1)}, f32[8,256]{1,0:T(8,128)}) custom-call(s32[8,256]{1,0:T(8,128)S(1)} %bitcast.30, s32[8,256]{1,0:T(8,128)S(1)} %bitcast.33, f32[8,256]{1,0:T(8,128)S(1)} %bitcast.36, bf16[4,256,256]{2,1,0:T(8,128)(2,1)S(1)} %get-tuple-element.96.places_ref, ...), custom_call_target="tpu_custom_call" | custom-call | flops 939524096 | bytes 3670016 | tf_op jit(solution)/shard_map/combine/pallas_call | solution.py:532
  (1 shorter events, 0.0 us)
Async XLA Ops:
  4.4 43.9 %copy-start = (bf16[1,1024,1792]{2,1,0:T(8,128)(2,1)S(1)}, bf16[1,1024,1792]{2,1,0:T(8,128)(2,1)}, u32[]{:S(2)}) copy-start(bf16[1,1024,1792]{2,1,0:T(8,128)(2,1)} %param.14) | copy-start | bytes 11010052
  4.4 47.0 %copy-start.2 = (bf16[1,1792,1024]{2,1,0:T(8,128)(2,1)S(1)}, bf16[1,1792,1024]{2,1,0:T(8,128)(2,1)}, u32[]{:S(2)}) copy-start(bf16[1,1792,1024]{2,1,0:T(8,128)(2,1)} %param.13) | copy-start | bytes 11010052
  48.3 3.2 %copy-start.1 = (bf16[1,1792,1024]{2,1,0:T(8,128)(2,1)S(1)}, bf16[1,1792,1024]{2,1,0:T(8,128)(2,1)}, u32[]{:S(2)}) copy-start(bf16[1,1792,1024]{2,1,0:T(8,128)(2,1)} %param.12) | copy-start | bytes 11010052
  49.2 1.5 %collective-permute-start = (bf16[160,512]{1,0:T(8,128)(2,1)S(1)}, bf16[160,512]{1,0:T(8,128)(2,1)S(1)}, u32[]{:S(2)}, u32[]{:S(2)}) collective-permute-start(bf16[160,512]{1,0:T(8,128)(2,1)S(1)} %get-tuple-element.61), channel_id=1, source_target_pairs={{0,1},{1,0},{2,3},{3,2},{4,5},{5,4},{6,7},{7,6},{8,9},{9,8},{10,11... | collective-permute-start | bytes 491528 | tf_op jit(solution)/shard_map/ppermute | solution.py:556
  50.8 6.3 %collective-permute-start.1 = (bf16[160,512]{1,0:T(8,128)(2,1)S(1)}, bf16[160,512]{1,0:T(8,128)(2,1)S(1)}, u32[]{:S(2)}, u32[]{:S(2)}) collective-permute-start(bf16[160,512]{1,0:T(8,128)(2,1)S(1)} %get-tuple-element.65), channel_id=1, source_target_pairs={{0,2},{1,3},{2,0},{3,1},{4,6},{5,7},{6,4},{7,5},{8,10},{9,11},{10,... | collective-permute-start | bytes 491528 | tf_op jit(solution)/shard_map/ppermute | solution.py:556
  53.0 1.9 %collective-permute-start.5 = (bf16[160,384]{1,0:T(8,128)(2,1)S(1)}, bf16[160,384]{1,0:T(8,128)(2,1)S(1)}, u32[]{:S(2)}, u32[]{:S(2)}) collective-permute-start(bf16[160,384]{1,0:T(8,128)(2,1)S(1)} %get-tuple-element.72), channel_id=1, source_target_pairs={{0,1},{1,0},{2,3},{3,2},{4,5},{5,4},{6,7},{7,6},{8,9},{9,8},{10,11... | collective-permute-start | bytes 368648 | tf_op jit(solution)/shard_map/ppermute | solution.py:556
  53.1 1.8 %collective-permute-start.6 = (bf16[160,384]{1,0:T(8,128)(2,1)S(1)}, bf16[160,384]{1,0:T(8,128)(2,1)S(1)}, u32[]{:S(2)}, u32[]{:S(2)}) collective-permute-start(bf16[160,384]{1,0:T(8,128)(2,1)S(1)} %get-tuple-element.73), channel_id=1, source_target_pairs={{0,1},{1,0},{2,3},{3,2},{4,5},{5,4},{6,7},{7,6},{8,9},{9,8},{10,11... | collective-permute-start | bytes 368648 | tf_op jit(solution)/shard_map/ppermute | solution.py:556
  53.6 1.3 %collective-permute-start.7 = (bf16[160,256]{1,0:T(8,128)(2,1)S(1)}, bf16[160,256]{1,0:T(8,128)(2,1)S(1)}, u32[]{:S(2)}, u32[]{:S(2)}) collective-permute-start(bf16[160,256]{1,0:T(8,128)(2,1)S(1)} %get-tuple-element.74), channel_id=1, source_target_pairs={{0,1},{1,0},{2,3},{3,2},{4,5},{5,4},{6,7},{7,6},{8,9},{9,8},{10,11... | collective-permute-start | bytes 245768 | tf_op jit(solution)/shard_map/ppermute | solution.py:556
  55.0 10.6 %collective-permute-start.9 = (bf16[160,1024]{1,0:T(8,128)(2,1)S(1)}, bf16[160,1024]{1,0:T(8,128)(2,1)S(1)}, u32[]{:S(2)}, u32[]{:S(2)}) collective-permute-start(bf16[160,1024]{1,0:T(8,128)(2,1)S(1)} %get-tuple-element.81), channel_id=1, source_target_pairs={{0,2},{1,3},{2,0},{3,1},{4,6},{5,7},{6,4},{7,5},{8,10},{9,11},{10,... | collective-permute-start | bytes 983048 | tf_op jit(solution)/shard_map/ppermute | solution.py:556
  58.5 1.6 %collective-permute-start.2 = (bf16[160,512]{1,0:T(8,128)(2,1)S(1)}, bf16[160,512]{1,0:T(8,128)(2,1)S(1)}, u32[]{:S(2)}, u32[]{:S(2)}) collective-permute-start(bf16[160,512]{1,0:T(8,128)(2,1)S(1)} %get-tuple-element.68), channel_id=1, source_target_pairs={{0,1},{1,0},{2,3},{3,2},{4,5},{5,4},{6,7},{7,6},{8,9},{9,8},{10,11... | collective-permute-start | bytes 491528 | tf_op jit(solution)/shard_map/ppermute | solution.py:556
  58.5 1.6 %collective-permute-start.3 = (bf16[160,512]{1,0:T(8,128)(2,1)S(1)}, bf16[160,512]{1,0:T(8,128)(2,1)S(1)}, u32[]{:S(2)}, u32[]{:S(2)}) collective-permute-start(bf16[160,512]{1,0:T(8,128)(2,1)S(1)} %get-tuple-element.69), channel_id=1, source_target_pairs={{0,1},{1,0},{2,3},{3,2},{4,5},{5,4},{6,7},{7,6},{8,9},{9,8},{10,11... | collective-permute-start | bytes 491528 | tf_op jit(solution)/shard_map/ppermute | solution.py:556
  59.8 8.1 %copy-start.3 = (s32[256,8]{0,1:T(8,128)S(1)}, s32[256,8]{0,1:T(8,128)}, u32[]{:S(2)}) copy-start(s32[256,8]{0,1:T(8,128)} %param.9) | copy-start | bytes 24580
  59.8 8.1 %copy-start.4 = (s32[256,8]{0,1:T(8,128)S(1)}, s32[256,8]{0,1:T(8,128)}, u32[]{:S(2)}) copy-start(s32[256,8]{0,1:T(8,128)} %param.10) | copy-start | bytes 24580
  59.9 8.1 %copy-start.5 = (f32[256,8]{0,1:T(8,128)S(1)}, f32[256,8]{0,1:T(8,128)}, u32[]{:S(2)}) copy-start(f32[256,8]{0,1:T(8,128)} %param.11) | copy-start | bytes 24580
  59.9 1.5 %collective-permute-start.8 = (bf16[160,512]{1,0:T(8,128)(2,1)S(1)}, bf16[160,512]{1,0:T(8,128)(2,1)S(1)}, u32[]{:S(2)}, u32[]{:S(2)}) collective-permute-start(bf16[160,512]{1,0:T(8,128)(2,1)S(1)} %get-tuple-element.78), channel_id=1, source_target_pairs={{0,1},{1,0},{2,3},{3,2},{4,5},{5,4},{6,7},{7,6},{8,9},{9,8},{10,11... | collective-permute-start | bytes 491528 | tf_op jit(solution)/shard_map/ppermute | solution.py:556
  60.3 12.4 %collective-permute-start.4 = (bf16[160,1024]{1,0:T(8,128)(2,1)S(1)}, bf16[160,1024]{1,0:T(8,128)(2,1)S(1)}, u32[]{:S(2)}, u32[]{:S(2)}) collective-permute-start(bf16[160,1024]{1,0:T(8,128)(2,1)S(1)} %get-tuple-element.70), channel_id=1, source_target_pairs={{0,2},{1,3},{2,0},{3,1},{4,6},{5,7},{6,4},{7,5},{8,10},{9,11},{10,... | collective-permute-start | bytes 983048 | tf_op jit(solution)/shard_map/ppermute | solution.py:556
  65.9 2.6 %collective-permute-start.10 = (bf16[160,512]{1,0:T(8,128)(2,1)S(1)}, bf16[160,512]{1,0:T(8,128)(2,1)S(1)}, u32[]{:S(2)}, u32[]{:S(2)}) collective-permute-start(bf16[160,512]{1,0:T(8,128)(2,1)S(1)} %get-tuple-element.84.refs_0_), channel_id=1, source_target_pairs={{0,1},{1,0},{2,3},{3,2},{4,5},{5,4},{6,7},{7,6},{8,9},{9,8},{10,11... | collective-permute-start | bytes 491528 | tf_op jit(solution)/shard_map/ppermute | solution.py:556
  65.9 2.6 %collective-permute-start.11 = (bf16[160,512]{1,0:T(8,128)(2,1)S(1)}, bf16[160,512]{1,0:T(8,128)(2,1)S(1)}, u32[]{:S(2)}, u32[]{:S(2)}) collective-permute-start(bf16[160,512]{1,0:T(8,128)(2,1)S(1)} %get-tuple-element.85.refs_1_), channel_id=1, source_target_pairs={{0,1},{1,0},{2,3},{3,2},{4,5},{5,4},{6,7},{7,6},{8,9},{9,8},{10,11... | collective-permute-start | bytes 491528 | tf_op jit(solution)/shard_map/ppermute | solution.py:556
  66.4 2.1 %collective-permute-start.12 = (bf16[160,512]{1,0:T(8,128)(2,1)S(1)}, bf16[160,512]{1,0:T(8,128)(2,1)S(1)}, u32[]{:S(2)}, u32[]{:S(2)}) collective-permute-start(bf16[160,512]{1,0:T(8,128)(2,1)S(1)} %get-tuple-element.86.refs_2_), channel_id=1, source_target_pairs={{0,1},{1,0},{2,3},{3,2},{4,5},{5,4},{6,7},{7,6},{8,9},{9,8},{10,11... | collective-permute-start | bytes 491528 | tf_op jit(solution)/shard_map/ppermute | solution.py:556
  66.5 8.9 %collective-permute-start.13 = (bf16[160,512]{1,0:T(8,128)(2,1)S(1)}, bf16[160,512]{1,0:T(8,128)(2,1)S(1)}, u32[]{:S(2)}, u32[]{:S(2)}) collective-permute-start(bf16[160,512]{1,0:T(8,128)(2,1)S(1)} %get-tuple-element.102), channel_id=1, source_target_pairs={{0,2},{1,3},{2,0},{3,1},{4,6},{5,7},{6,4},{7,5},{8,10},{9,11},{10,... | collective-permute-start | bytes 491528 | tf_op jit(solution)/shard_map/ppermute | solution.py:556
  72.7 1.4 %collective-permute-start.14 = (bf16[160,256]{1,0:T(8,128)(2,1)S(1)}, bf16[160,256]{1,0:T(8,128)(2,1)S(1)}, u32[]{:S(2)}, u32[]{:S(2)}) collective-permute-start(bf16[160,256]{1,0:T(8,128)(2,1)S(1)} %get-tuple-element.103.refs_0_), channel_id=1, source_target_pairs={{0,1},{1,0},{2,3},{3,2},{4,5},{5,4},{6,7},{7,6},{8,9},{9,8},{10,11... | collective-permute-start | bytes 245768 | tf_op jit(solution)/shard_map/ppermute | solution.py:556
  72.8 1.5 %collective-permute-start.15 = (bf16[160,256]{1,0:T(8,128)(2,1)S(1)}, bf16[160,256]{1,0:T(8,128)(2,1)S(1)}, u32[]{:S(2)}, u32[]{:S(2)}) collective-permute-start(bf16[160,256]{1,0:T(8,128)(2,1)S(1)} %get-tuple-element.104.refs_1_), channel_id=1, source_target_pairs={{0,1},{1,0},{2,3},{3,2},{4,5},{5,4},{6,7},{7,6},{8,9},{9,8},{10,11... | collective-permute-start | bytes 245768 | tf_op jit(solution)/shard_map/ppermute | solution.py:556
  75.8 1.7 %collective-permute-start.16 = (bf16[160,1152]{1,0:T(8,128)(2,1)S(1)}, bf16[160,1152]{1,0:T(8,128)(2,1)S(1)}, u32[]{:S(2)}, u32[]{:S(2)}) collective-permute-start(bf16[160,1152]{1,0:T(8,128)(2,1)S(1)} %pair_b.1.own_ref), channel_id=1, source_target_pairs={{0,1},{1,0},{2,3},{3,2},{4,5},{5,4},{6,7},{7,6},{8,9},{9,8},{10,11... | collective-permute-start | bytes 1105928 | tf_op jit(solution)/shard_map/ppermute | solution.py:556
